TPU v7x, 256 devices: a whole 4x4x8 slice. The times are simulated.
256 devices in a mesh: blocks: 128 (over z, y, x), slab: 2 (over core).
Axes of the slice: x: 4, y: 4, z: 8, core: 2. Of those that a mesh axis runs over, the one named last changes fastest.
Arguments:
- state: float32 [4096, 32, 1024], P('blocks', 'slab'), may hold values from -6 to 6
- courant_row: float32 [32], P('slab'), may hold values from -0.8 to 0.8
- courant_col: float32 [32], P('slab'), may hold values from -0.8 to 0.8
- mixing: float32 [32], P('slab'), may hold values from 0.05 to 0.25
- nbr_block: int32 [4096, 4], P('blocks'), may hold values from 0 to 4095, as said below
- nbr_side: int32 [4096, 4], P('blocks'), may hold values from 0 to 3
- nbr_flip: int32 [4096, 4], P('blocks'), may hold values from 0 to 1
- send_idx: int32 [128, 128, 2], P('blocks'), may hold values from 0 to 511
- fine_slot: int32 [128, 192], P('blocks'), may hold values from 0 to 255, as said below
- fine_count: int32 [128], P('blocks'), may hold values from 48 to 192, as said below
Outputs:
- advanced: float32 [4096, 32, 1024], P('blocks', 'slab')
- refined: bfloat16 [24576, 32, 1024], P('blocks', 'slab')
Inputs may be any that keep to these rules, and one draw needn't show every extreme that they name: `nbr_block`: every neighbour block lies on the device that holds the block or on the device just before or after it in block order, cyclically. `fine_slot`: the slots of one new owner are distinct. `fine_count`: some new owner uses all 192 slots.
All inputs are finite; a program needn't handle non-finite values.
Results may differ from a plain program's by a relative error of at most 0.001.
Values sent between devices are 32-bit elements; how exact they have to be, the bound alone decides.
No kernel may reach another device: no remote copies, remote signals or barrier semaphores. Data moves between devices by JAX's collectives and lax.ppermute only.
A program may use at most 128 MiB of HBM per device.

v0:
```python
import jax
import jax.numpy as jnp
import numpy as np
from jax import lax
from jax.sharding import PartitionSpec as P


def with_halo(shard, sides, width, wrap):
    for axis, dim in sides:
        count, length = (lax.axis_size(axis), shard.shape[dim])
        up = [(i, (i + 1) % count) for i in range(count if wrap else count - 1)]
        down = [(j, i) for i, j in up]
        last = lax.slice_in_dim(shard, length - width, length, axis=dim)
        leading = lax.slice_in_dim(shard, 0, width, axis=dim)
        before = lax.ppermute(last, axis, up)
        after = lax.ppermute(leading, axis, down)
        shard = jnp.concatenate([before, shard, after], axis=dim)
    return shard


def interp_table():
    table = np.zeros((32, 8))
    for fine in range(32):
        x = (fine + 0.5) / 4.0
        start = min(max(int(np.floor(x - 0.5)) - 1, 0), 4)
        nodes = start + np.arange(4) + 0.5
        for a in range(4):
            weight = 1.0
            for b in range(4):
                if b != a:
                    weight *= (x - nodes[b]) / (nodes[a] - nodes[b])
            table[fine, start + a] = weight
    return np.kron(table, table).T.astype(np.float32)


def edge_strips(grid):
    sides = [
        jnp.stack([grid[:, :, 0, :], grid[:, :, 1, :]], 1),
        jnp.stack([grid[:, :, 31, :], grid[:, :, 30, :]], 1),
        jnp.stack([grid[:, :, :, 0], grid[:, :, :, 1]], 1),
        jnp.stack([grid[:, :, :, 31], grid[:, :, :, 30]], 1),
    ]
    return jnp.stack(sides, 1)


def advance(state, ghost, vert, courant_row, courant_col, mixing):
    count, lev = (state.shape[0], state.shape[1])
    grid = state.reshape(count, lev, 32, 32)
    ext_row = jnp.concatenate(
        [
            ghost[:, 0, 1][:, :, None, :],
            ghost[:, 0, 0][:, :, None, :],
            grid,
            ghost[:, 1, 0][:, :, None, :],
            ghost[:, 1, 1][:, :, None, :],
        ],
        2,
    )
    ext_col = jnp.concatenate(
        [
            ghost[:, 2, 1][..., None],
            ghost[:, 2, 0][..., None],
            grid,
            ghost[:, 3, 0][..., None],
            ghost[:, 3, 1][..., None],
        ],
        3,
    )
    row_diff = (
        8.0 * (ext_row[:, :, 3:35] - ext_row[:, :, 1:33])
        - (ext_row[:, :, 4:36] - ext_row[:, :, 0:32])
    ) / 12.0
    col_diff = (
        8.0 * (ext_col[..., 3:35] - ext_col[..., 1:33]) - (ext_col[..., 4:36] - ext_col[..., 0:32])
    ) / 12.0
    tend = (
        -courant_row[None, :, None, None] * row_diff - courant_col[None, :, None, None] * col_diff
    )
    return state + tend.reshape(count, lev, 1024) + mixing[None, :, None] * vert


def windows_of(advanced):
    count, lev = (advanced.shape[0], advanced.shape[1])
    grid = advanced.reshape(count, lev, 4, 8, 4, 8)
    return grid.transpose(0, 2, 4, 1, 3, 5).reshape(count * 16, lev, 64)


def body(
    state,
    courant_row,
    courant_col,
    mixing,
    nbr_block,
    nbr_side,
    nbr_flip,
    send_idx,
    fine_slot,
    fine_count,
):
    count, lev = (state.shape[0], state.shape[1])
    peers = lax.axis_size("blocks")
    here = lax.axis_index("blocks")
    padded = with_halo(state, (("slab", 1),), 1, False)
    vert = padded[:, 2:] - 2.0 * state + padded[:, :-2]
    nearby = with_halo(state, (("blocks", 0),), count, True)
    strips = edge_strips(nearby.reshape(3 * count, lev, 32, 32))
    flat = strips.reshape(3 * count * 4, 2, lev, 32)
    owner = nbr_block // count
    relative = (owner - here + 1 + peers) % peers
    candidate = relative * count + nbr_block % count
    ghost = flat[(candidate * 4 + nbr_side).reshape(-1)].reshape(count, 4, 2, lev, 32)
    ghost = jnp.where(nbr_flip[:, :, None, None, None] == 1, ghost[..., ::-1], ghost)
    advanced = advance(state, ghost, vert, courant_row, courant_col, mixing)
    windows = windows_of(advanced)
    payload = windows[send_idx[0].reshape(-1)].reshape(peers, send_idx.shape[2], lev, 64)
    table = jnp.asarray(interp_table())
    slots = fine_slot[0]
    received = lax.all_to_all(payload, "blocks", split_axis=0, concat_axis=0, tiled=True)
    parent = received.reshape(-1, lev, 64)[slots]
    fine = jnp.einsum("flc,cp->flp", parent, table, precision=lax.Precision.HIGHEST)
    live = jnp.arange(slots.shape[0], dtype=jnp.int32) < fine_count[0]
    fine = jnp.where(live[:, None, None], fine, 0.0).astype(jnp.bfloat16)
    return (advanced, fine)


def solution(mesh):
    in_specs = (
        P("blocks", "slab", None),
        P("slab"),
        P("slab"),
        P("slab"),
        P("blocks", None),
        P("blocks", None),
        P("blocks", None),
        P("blocks", None, None),
        P("blocks", None),
        P("blocks"),
    )
    out_specs = (P("blocks", "slab", None), P("blocks", "slab", None))
    return jax.shard_map(body, mesh=mesh, in_specs=in_specs, out_specs=out_specs, check_vma=False)
```

profile of v0, /device:TPU:32, one launch (start us, length us, event | category | flops | bytes accessed | tf_op | source)
XLA Modules:
  0.0 230.7 jit_solution(1046811363810077757)
XLA Ops:
  0.7 1.6 collective-permute-start
  2.3 4.8 %collective-permute-start.1 = (f32[32,16,1024]{2,1,0:T(8,128)}, f32[32,16,1024]{2,1,0:T(8,128)S(1)}, u32[]{:S(2)}, u32[]{:S(2)}) collective-permute-start(f32[32,16,1024]{2,1,0:T(8,128)} %param.11), channel_id=1, source_target_pairs={{2,0},{4,2},{6,4},{8,6},{10,8},{12,10},{14,12},{16,14},{18,16},{20... | collective-permute-start | bytes 6291464 | tf_op jit(solution)/shard_map/ppermute | solution.py:16
  7.0 6.3 %copy.191 = f32[32,16,1024]{0,2,1:T(8,128)} copy(f32[32,16,1024]{2,1,0:T(8,128)} %param.11) | data formatting | bytes 4194304 | tf_op args[0]
  13.3 2.3 %fusion.25 = (f32[32,1,1024]{0,2,1:T(8,128)}, f32[32,1,1024]{0,2,1:T(8,128)}) fusion(f32[32,16,1024]{0,2,1:T(8,128)} %copy.191), kind=kLoop, calls=%fused_computation.82 | loop fusion | bytes 524288 | tf_op jit(solution)/shard_map/slice | solution.py:14
  15.7 1.3 collective-permute-start.2
  16.9 3.3 %collective-permute-start.3 = (f32[32,1,1024]{0,2,1:T(8,128)}, f32[32,1,1024]{0,2,1:T(8,128)S(1)}, u32[]{:S(2)}, u32[]{:S(2)}) collective-permute-start(f32[32,1,1024]{0,2,1:T(8,128)} %get-tuple-element.19), channel_id=1, source_target_pairs={{0,1},{2,3},{4,5},{6,7},{8,9},{10,11},{12,13},{14,15},{16,17},{18,... | collective-permute-start | bytes 393224 | tf_op jit(solution)/shard_map/ppermute | solution.py:15
  20.3 0.1 copy.170
  20.4 0.1 reshape.131
  20.5 0.1 copy.159
  20.6 0.1 copy.198
  20.7 0.1 reshape_squeeze.3
  20.9 31.7 %collective-permute-done = f32[32,16,1024]{2,1,0:T(8,128)} collective-permute-done((f32[32,16,1024]{2,1,0:T(8,128)}, f32[32,16,1024]{2,1,0:T(8,128)}, u32[]{:S(2)}, u32[]{:S(2)}) %collective-permute-start) | collective-permute-done | bytes 2097184 | tf_op jit(solution)/shard_map/ppermute | solution.py:15
  52.7 6.3 %copy.160 = f32[32,16,1024]{0,2,1:T(8,128)} copy(f32[32,16,1024]{2,1,0:T(8,128)} %collective-permute-done) | data formatting | bytes 4194304 | tf_op jit(solution)/shard_map/ppermute | solution.py:15
  58.9 4.8 %copy.162 = f32[32,16,1024]{0,2,1:T(8,128)} copy(f32[32,16,1024]{2,1,0:T(8,128)S(1)} %collective-permute-done.1) | data formatting | bytes 4194304 | tf_op jit(solution)/shard_map/ppermute | solution.py:16
  63.7 10.5 %pad_maximum_fusion.14 = f32[96,16,1024]{0,2,1:T(8,128)S(1)} fusion(f32[32,16,1024]{0,2,1:T(8,128)} %copy.162, f32[32,16,1024]{0,2,1:T(8,128)} %copy.191, f32[32,16,1024]{0,2,1:T(8,128)} %copy.160), kind=kLoop, calls=%fused_computation.33 | loop fusion | flops 3145728 | bytes 12582912 | tf_op jit(solution)/shard_map/concatenate | solution.py:17
  74.2 0.1 slice_bitcast_fusion.11
  74.3 1.0 fusion.24
  75.3 0.1 maximum_bitcast_fusion
  75.4 0.1 maximum_bitcast_fusion.2
  75.5 0.2 pad_maximum_fusion.15
  75.8 5.9 %copy.169 = f32[96,4,2,16,32]{4,3,2,1,0:T(8,128)} copy(f32[96,4,2,16,32]{0,4,3,2,1:T(8,128)S(1)} %pad_maximum_fusion.15) | data formatting | bytes 3145728 | tf_op jit(solution)/shard_map/stack | solution.py:43
  81.7 3.5 %gather_fusion = f32[128,2,16,32]{3,2,1,0:T(8,128)S(1)} fusion(f32[384,2,16,32]{3,2,1,0:T(8,128)} %bitcast.81, s32[1024]{0:T(1024)S(1)} %pad_clamp_fusion.2), kind=kCustom, calls=%fused_computation | custom fusion | bytes 1049088 | tf_op jit(solution)/shard_map/gather | solution.py:111
  85.2 2.3 %rev.3 = f32[32,4,2,16,32]{4,3,2,1,0:T(8,128)} reverse(f32[32,4,2,16,32]{4,3,2,1,0:T(8,128)S(1)} %bitcast.76), dimensions={4} | reverse | bytes 1048576 | tf_op jit(solution)/shard_map/rev | solution.py:112
  87.5 1.9 broadcast_select_fusion
  89.4 0.2 slice_bitcast_fusion.7
  89.5 0.2 copy.172
  89.7 0.2 copy.173
  89.9 0.2 copy.177
  90.0 0.2 copy.178
  90.2 0.2 copy.182
  90.3 0.2 copy.183
  90.5 0.2 copy.187
  90.7 0.2 copy.188
  90.8 31.1 %fusion.7 = f32[32,16,32,32]{0,3,2,1:T(8,128)S(1)} fusion(f32[32,16,32,32]{0,3,2,1:T(8,128)} %bitcast.73, f32[32,16,32,1]{0,3,2,1:T(1,128)S(1)} %copy.183, f32[32,16,32,1]{0,3,2,1:T(1,128)S(1)} %copy.188, f32[32,16,32,1]{0,3,2,1:T(1,128)S(1)} %copy.187, f32[32,16,32,1]{0,3,2,1:T(1,128)S(1)} %copy.182, f32[32,16,1,32]{0,3,2,1:T(8,128)S(1)} %copy.173, ...), kind=kLoop, calls=%fused_computation.14 | loop fusion | flops 12058624 | bytes 4718720 | tf_op jit(solution)/shard_map/sub | solution.py:77
  122.0 13.5 %fusion.2 = f32[32,16,1024]{0,2,1:T(8,128)} fusion(f32[32,16,1024]{0,2,1:T(8,128)} %copy.191, f32[32,1,1024]{0,2,1:T(8,128)S(1)} %collective-permute-done.3, f32[32,1,1024]{0,2,1:T(8,128)S(1)} %collective-permute-done.2, f32[32,16,32,32]{0,3,2,1:T(8,128)S(1)} %fusion.7, f32[16]{0:T(128)S(1)} %copy-done.6), kind=kLoop, calls=%fused_computation.7 | loop fusion | flops 4194304 | bytes 6553664 | tf_op jit(solution)/shard_map/add | solution.py:79
  135.5 16.3 %copy.197 = f32[32,4,4,16,8,8]{3,5,4,2,1,0:T(8,128)} copy(f32[32,4,4,16,8,8]{0,5,2,4,1,3:T(8,128)} %bitcast.74) | data formatting | bytes 4194304 | tf_op jit(solution)/shard_map/transpose | solution.py:85
  151.8 10.1 %gather_fusion.1 = f32[256,16,64]{1,2,0:T(8,128)} fusion(f32[512,16,64]{1,2,0:T(8,128)} %bitcast.75, s32[1024]{0:T(1024)S(1)} %pad_clamp_fusion.1), kind=kCustom, calls=%fused_computation.1 | custom fusion | bytes 2098176 | tf_op jit(solution)/shard_map/gather | solution.py:115
  161.9 5.2 %copy.199 = f32[128,2,16,64]{3,2,1,0:T(8,128)S(1)} copy(f32[128,2,16,64]{2,3,1,0:T(8,128)} %bitcast.78) | data formatting | bytes 2097152 | tf_op jit(solution)/shard_map/reshape | solution.py:115
  167.0 2.3 reshape.163
  169.3 11.1 %all-to-all-start = ((f32[128,1,2048]{2,1,0:T(1,128)}), f32[128,1,2048]{2,1,0:T(1,128)S(1)}, u32[]{:S(2)}, u32[]{:S(2)}) async-start(f32[128,1,2048]{2,1,0:T(1,128)} %reshape.163), calls=%async_computation | async-start | bytes 2097152 | tf_op jit(solution)/shard_map/all_to_all | solution.py:118
  181.2 0.0 copy-start
  181.2 6.5 %copy.200 = f32[32,16,1024]{2,1,0:T(8,128)} copy(f32[32,16,1024]{0,2,1:T(8,128)} %fusion.2) | data formatting | bytes 4194304
  187.6 23.3 %all-to-all-done = f32[128,1,2048]{2,1,0:T(1,128)S(1)} async-done(((f32[128,1,2048]{2,1,0:T(1,128)}), f32[128,1,2048]{2,1,0:T(1,128)S(1)}, u32[]{:S(2)}, u32[]{:S(2)}) %all-to-all-start) | async-done | bytes 1048608 | tf_op jit(solution)/shard_map/all_to_all | solution.py:118
  210.9 0.5 broadcast.94
  211.5 3.1 %reduce = f32[128,2048]{1,0:T(8,128)S(1)} reduce(f32[128,1,2048]{2,1,0:T(1,128)S(1)} %all-to-all-done, f32[]{:T(128)} %broadcast.94), dimensions={1}, to_apply=%all_to_all.3.reduce_sub_computation | reduce | bytes 2097156 | tf_op jit(solution)/shard_map/all_to_all | solution.py:118
  214.6 0.8 reshape.164
  215.4 2.1 gather_fusion.2
  217.5 13.2 %select_convert_fusion = bf16[192,16,1024]{2,1,0:T(8,128)(2,1)} fusion(pred[192]{0:T(512)(128)(4,1)S(1)} %iota_compare_fusion, f32[192,16,64]{2,1,0:T(8,128)} %gather_fusion.2, f32[64,1024,1]{1,0,2:T(8,128)S(1)} %copy-done), kind=kOutput, calls=%fused_computation.3 | convolution fusion | flops 2422210560 | bytes 7340224 | tf_op jit(solution)/shard_map/flc,cp->flp/dot_general | solution.py:120
  (30 shorter events, 0.1 us)
Async XLA Ops:
  0.6 19.6 %copy-start.3 = (s32[32,4]{0,1:T(4,128)S(1)}, s32[32,4]{0,1:T(4,128)}, u32[]{:S(2)}) copy-start(s32[32,4]{0,1:T(4,128)} %param.15) | copy-start | bytes 1540
  0.6 19.6 %copy-start.2 = (s32[32,4]{0,1:T(4,128)S(1)}, s32[32,4]{0,1:T(4,128)}, u32[]{:S(2)}) copy-start(s32[32,4]{0,1:T(4,128)} %param.16) | copy-start | bytes 1540
  0.7 19.8 %copy-start.1 = (s32[32,4]{0,1:T(4,128)S(1)}, s32[32,4]{0,1:T(4,128)}, u32[]{:S(2)}) copy-start(s32[32,4]{0,1:T(4,128)} %param.17) | copy-start | bytes 1540
  0.7 19.9 %copy-start.4 = (s32[1,128,2]{1,2,0:T(2,128)S(1)}, s32[1,128,2]{1,2,0:T(2,128)}, u32[]{:S(2)}) copy-start(s32[1,128,2]{1,2,0:T(2,128)} %param.18) | copy-start | bytes 3076
  0.7 20.2 %copy-start.7 = (f32[16]{0:T(128)S(1)}, f32[16]{0:T(128)}, u32[]{:S(2)}) copy-start(f32[16]{0:T(128)} %param.12) | copy-start | bytes 196
  0.7 20.2 %copy-start.8 = (f32[16]{0:T(128)S(1)}, f32[16]{0:T(128)}, u32[]{:S(2)}) copy-start(f32[16]{0:T(128)} %param.13) | copy-start | bytes 196
  0.7 52.0 %collective-permute-start = (f32[32,16,1024]{2,1,0:T(8,128)}, f32[32,16,1024]{2,1,0:T(8,128)}, u32[]{:S(2)}, u32[]{:S(2)}) collective-permute-start(f32[32,16,1024]{2,1,0:T(8,128)} %param.11), channel_id=1, source_target_pairs={{0,2},{2,4},{4,6},{6,8},{8,10},{10,12},{12,14},{14,16},{16,18},{18... | collective-permute-start | bytes 6291464 | tf_op jit(solution)/shard_map/ppermute | solution.py:15
  2.3 56.7 %collective-permute-start.1 = (f32[32,16,1024]{2,1,0:T(8,128)}, f32[32,16,1024]{2,1,0:T(8,128)S(1)}, u32[]{:S(2)}, u32[]{:S(2)}) collective-permute-start(f32[32,16,1024]{2,1,0:T(8,128)} %param.11), channel_id=1, source_target_pairs={{2,0},{4,2},{6,4},{8,6},{10,8},{12,10},{14,12},{16,14},{18,16},{20... | collective-permute-start | bytes 6291464 | tf_op jit(solution)/shard_map/ppermute | solution.py:16
  15.7 106.3 %collective-permute-start.2 = (f32[32,1,1024]{0,2,1:T(8,128)}, f32[32,1,1024]{0,2,1:T(8,128)S(1)}, u32[]{:S(2)}, u32[]{:S(2)}) collective-permute-start(f32[32,1,1024]{0,2,1:T(8,128)} %get-tuple-element.18), channel_id=1, source_target_pairs={{1,0},{3,2},{5,4},{7,6},{9,8},{11,10},{13,12},{15,14},{17,16},{19,... | collective-permute-start | bytes 393224 | tf_op jit(solution)/shard_map/ppermute | solution.py:16
  16.9 105.0 %collective-permute-start.3 = (f32[32,1,1024]{0,2,1:T(8,128)}, f32[32,1,1024]{0,2,1:T(8,128)S(1)}, u32[]{:S(2)}, u32[]{:S(2)}) collective-permute-start(f32[32,1,1024]{0,2,1:T(8,128)} %get-tuple-element.19), channel_id=1, source_target_pairs={{0,1},{2,3},{4,5},{6,7},{8,9},{10,11},{12,13},{14,15},{16,17},{18,... | collective-permute-start | bytes 393224 | tf_op jit(solution)/shard_map/ppermute | solution.py:15
  90.8 31.2 %copy-start.6 = (f32[16]{0:T(128)S(1)}, f32[16]{0:T(128)}, u32[]{:S(2)}) copy-start(f32[16]{0:T(128)} %param.14) | copy-start | bytes 196
  161.9 19.2 %copy-start.5 = (s32[1,192]{1,0:T(1,128)S(1)}, s32[1,192]{1,0:T(1,128)}, u32[]{:S(2)}) copy-start(s32[1,192]{1,0:T(1,128)} %param.19) | copy-start | bytes 2308
  169.3 41.6 %all-to-all-start = ((f32[128,1,2048]{2,1,0:T(1,128)}), f32[128,1,2048]{2,1,0:T(1,128)S(1)}, u32[]{:S(2)}, u32[]{:S(2)}) async-start(f32[128,1,2048]{2,1,0:T(1,128)} %reshape.163), calls=%async_computation | async-start | bytes 2097152 | tf_op jit(solution)/shard_map/all_to_all | solution.py:118
  181.2 36.3 %copy-start = (f32[64,1024,1]{1,0,2:T(8,128)S(1)}, f32[64,1024,1]{1,0,2:T(8,128)}, u32[]{:S(2)}) copy-start(f32[64,1024,1]{1,0,2:T(8,128)} %constant.82) | copy-start | bytes 786436
where the time goes:
time: 232 us; the launch traced here: 231 us
  local copies, waits for them, and re-layouts  78.2 us (34%)
  other arithmetic  60.6 us (26%)
  waiting for transfers between devices  55 us (24%)
  starting transfers between devices  22 us (9%)
  matrix products  13.2 us (6%)
    ppermute x2, waiting for transfers between devices, with_halo(): before = lax.ppermute(last, axis, up)  31.7 us
    sub x1, other arithmetic, advance(): -courant_row[None, :, None, None] * row_diff  31.1 us
    all_to_all x1, waiting for transfers between devices, body(): lax.all_to_all(payload, 'blocks', split_axis=0, concat_axis=0, tiled=True)  23.3 us
    transpose x1, local copies, waits for them, and re-layouts, windows_of(): return grid.transpose(0, 2, 4, 1, 3, 5).reshape(count * 16, lev, 64)  16.3 us
    unnamed x23, local copies, waits for them, and re-layouts  16 us
    add x1, other arithmetic, advance(): return state + tend.reshape(count, lev, 1024) + mixing[None, :, None] * vert  13.5 us
    dot_general x1, matrix products, body(): jnp.einsum('flc,cp->flp', parent, table, precision=lax.Precision.HIGHEST)  13.2 us
    all_to_all x1, starting transfers between devices, body(): lax.all_to_all(payload, 'blocks', split_axis=0, concat_axis=0, tiled=True)  11.1 us
  transfers between devices with their start and end apart: 5, of which 2 were waited for; matrix products, arithmetic and copies ran while one was open for 37% of the time, Pallas kernels for 0%

commit v1 on v0

v1 whole, which is shorter than its diff:
```python
import jax
import jax.numpy as jnp
import ml_dtypes
import numpy as np
from jax import lax
from jax.experimental import pallas as pl
from jax.experimental.pallas import tpu as pltpu
from jax.sharding import PartitionSpec as P

CHUNK = 8
VMEM_LIMIT = 48 * 1024 * 1024


def interp_1d():
    table = np.zeros((32, 8))
    for fine in range(32):
        x = (fine + 0.5) / 4.0
        start = min(max(int(np.floor(x - 0.5)) - 1, 0), 4)
        nodes = start + np.arange(4) + 0.5
        for a in range(4):
            weight = 1.0
            for b in range(4):
                if b != a:
                    weight *= (x - nodes[b]) / (nodes[a] - nodes[b])
            table[fine, start + a] = weight
    return table


def as_bf16(array):
    return np.asarray(array, np.float32).astype(ml_dtypes.bfloat16)


def refine_table():
    table = interp_1d()
    full = np.kron(table, table).T.astype(np.float32)
    high = as_bf16(full)
    low = as_bf16(full - high.astype(np.float32))
    return np.concatenate([high, low, high, low], 0)


def strip_cell(side, depth, t):
    line = depth if side in (0, 2) else 31 - depth
    return line * 32 + t if side < 2 else t * 32 + line


def strip_map():
    pick = np.zeros((1024, 256))
    for side in range(4):
        for depth in range(2):
            for t in range(32):
                pick[strip_cell(side, depth, t), side * 64 + depth * 32 + t] = 1.0
    return as_bf16(pick)


def ghost_map(side):
    first = side in (0, 2)
    out = np.zeros((128, 1024))
    for flip in range(2):
        for t in range(32):
            to = 31 - t if flip else t
            near = flip * 64 + t
            far = flip * 64 + 32 + t
            sign = 1.0 if first else -1.0
            out[near, strip_cell(side, 0, to)] += 8.0 * sign
            out[far, strip_cell(side, 0, to)] -= sign
            out[near, strip_cell(side, 1, to)] -= sign
    return as_bf16(np.concatenate([out, out], 0))


def stencil_map():
    own = np.zeros((128, 256))
    other = np.zeros((128, 256))
    weights = {-2: -1.0, -1: 8.0, 1: -8.0, 2: 1.0}
    for row in range(4):
        for col in range(32):
            lane = row * 32 + col
            for step, weight in weights.items():
                r = row + step
                if 0 <= r < 4:
                    own[r * 32 + col, lane] += weight
                else:
                    other[(r % 4) * 32 + col, lane] += weight
                c = col + step
                if 0 <= c < 32:
                    own[row * 32 + c, 128 + lane] += weight
    return as_bf16(np.concatenate([own, own, other, other], 0))


def window_map():
    pick = np.zeros((256, 256))
    for row in range(8):
        for col in range(32):
            pick[row * 32 + col, (col // 8) * 64 + row * 8 + col % 8] = 1.0
    return as_bf16(np.concatenate([pick, pick], 0))


def split(x):
    high = x.astype(jnp.bfloat16)
    low = (x - high.astype(jnp.float32)).astype(jnp.bfloat16)
    return high, low


def dot(a, b):
    return jnp.dot(a, b, preferred_element_type=jnp.float32)


def strips_kernel(state_ref, pick_ref, strips_ref, edge_ref):
    slab = lax.axis_index("slab")
    count, lev = state_ref.shape[0], state_ref.shape[1]

    def step(i, carry):
        b = i * CHUNK
        x = state_ref[pl.ds(b, CHUNK)]
        high, low = split(x.reshape(CHUNK * lev, 1024))
        s = dot(high, pick_ref[...]) + dot(low, pick_ref[...])
        s = s.reshape(CHUNK, lev, 256)
        strips_ref[pl.ds(b, CHUNK), 0] = s[:, :, :128]
        strips_ref[pl.ds(b, CHUNK), 1] = s[:, :, 128:]
        edge_ref[pl.ds(b, CHUNK), :] = jnp.where(slab == 0, x[:, lev - 1, :], x[:, 0, :])
        return carry

    lax.fori_loop(0, count // CHUNK, step, 0)


def levels_of(ref, lev):
    at = lax.broadcasted_iota(jnp.int32, (lev, 128), 0)
    out = jnp.zeros((lev, 128), jnp.float32)
    for l in range(lev):
        out = jnp.where(at == l, ref[l], out)
    return out


def advance_kernel(
    block_ref,
    side_ref,
    flip_ref,
    send_ref,
    crow_ref,
    ccol_ref,
    mix_ref,
    state_ref,
    edge_ref,
    prev_ref,
    own_ref,
    next_ref,
    col_ref,
    row0_ref,
    row1_ref,
    sten_ref,
    win_ref,
    adv_ref,
    pay_ref,
    near,
    ghosts,
    wins,
):
    slab = lax.axis_index("slab")
    here = lax.axis_index("blocks")
    peers = lax.axis_size("blocks")
    count, lev = state_ref.shape[0], state_ref.shape[1]
    near[0] = prev_ref[...]
    near[1] = own_ref[...]
    near[2] = next_ref[...]
    a_row = levels_of(crow_ref, lev) * (1.0 / 12.0)
    a_col = levels_of(ccol_ref, lev) * (1.0 / 12.0)
    mix = levels_of(mix_ref, lev)
    half = lax.broadcasted_iota(jnp.int32, (lev, 128), 1) // 64

    def gather(b, carry):
        for s in range(4):
            block = block_ref[b, s]
            side = side_ref[b, s]
            flip = flip_ref[b, s]
            rel = block // count - here + 1
            rel = jnp.where(rel < 0, rel + peers, rel)
            rel = jnp.where(rel >= peers, rel - peers, rel)
            x = near[rel, block % count, side // 2]
            x = jnp.where(side % 2 == flip, x, pltpu.roll(x, 64, 1))
            x = jnp.where(half == flip, x, 0.0) * (a_row if s < 2 else a_col)
            high, low = split(x)
            rows = pl.ds(pl.multiple_of(b * lev, lev), lev)
            ghosts[rows, s * 256 : s * 256 + 128] = high
            ghosts[rows, s * 256 + 128 : s * 256 + 256] = low
        return carry

    lax.fori_loop(0, count, gather, 0)

    rows = CHUNK * lev
    lane = lax.broadcasted_iota(jnp.int32, (rows, 128), 1)
    level = lax.broadcasted_iota(jnp.int32, (CHUNK, lev, 128), 1)

    def step(i, carry):
        b = i * CHUNK
        r = pl.ds(pl.multiple_of(i * rows, rows), rows)
        side_cols = dot(ghosts[r, 512:1024], col_ref[...])
        side_rows = {0: dot(ghosts[r, 0:256], row0_ref[...]), 7: dot(ghosts[r, 256:512], row1_ref[...])}
        tiles = [state_ref[pl.ds(b, CHUNK), :, 128 * j : 128 * j + 128] for j in range(8)]
        flat = [t.reshape(rows, 128) for t in tiles]
        zero = jnp.zeros((rows, 128), jnp.float32)
        done = []
        for j in range(8):
            other = jnp.where(lane < 64, flat[j + 1] if j < 7 else zero, flat[j - 1] if j else zero)
            diff = dot(jnp.concatenate(split(flat[j]) + split(other), 1), sten_ref[...])
            diff = diff.reshape(CHUNK, lev, 256)
            x = tiles[j]
            edge = edge_ref[pl.ds(b, CHUNK), 128 * j : 128 * j + 128][:, None, :]
            below = jnp.where(level == 0, jnp.where(slab == 0, 0.0, edge), pltpu.roll(x, 1, 1))
            above = jnp.where(level == lev - 1, jnp.where(slab == 0, edge, 0.0), pltpu.roll(x, lev - 1, 1))
            vert = above - 2.0 * x + below
            side_part = side_cols[:, 128 * j : 128 * j + 128]
            if j in side_rows:
                side_part = side_part + side_rows[j]
            out = x + a_row * diff[:, :, :128] + a_col * diff[:, :, 128:] + mix * vert
            out = out + side_part.reshape(CHUNK, lev, 128)
            adv_ref[pl.ds(b, CHUNK), :, 128 * j : 128 * j + 128] = out
            done.append(out.reshape(rows, 128))
            if j % 2:
                pair = jnp.concatenate(done[-2:], 1)
                w = dot(jnp.concatenate(split(pair), 1), win_ref[...])
                w = w.reshape(CHUNK, lev, 256)
                wins[pl.ds(b, CHUNK), j // 2, 0] = w[:, :, :128]
                wins[pl.ds(b, CHUNK), j // 2, 1] = w[:, :, 128:]
        return carry

    lax.fori_loop(0, count // CHUNK, step, 0)

    def pack(d, carry):
        parts = []
        for k in range(2):
            w = send_ref[d, k]
            x = wins[w // 16, (w // 4) % 4, (w // 2) % 2]
            parts.append(jnp.where(w % 2 == k, x, pltpu.roll(x, 64, 1)))
        pay_ref[d] = jnp.where(half == 0, parts[0], parts[1])
        return carry

    lax.fori_loop(0, peers, pack, 0)


def refine_kernel(slot_ref, count_ref, recv_ref, table_ref, out_ref, parents):
    start = pl.program_id(0) * out_ref.shape[0]
    lev = recv_ref.shape[1]
    half = lax.broadcasted_iota(jnp.int32, (lev, 128), 1) // 64
    live = count_ref[0]
    for f in range(out_ref.shape[0]):
        slot = slot_ref[0, start + f]
        x = recv_ref[slot // 2]
        x = jnp.where(half == slot % 2, x, pltpu.roll(x, 64, 1))
        x = jnp.where(start + f < live, x, 0.0)
        high, low = split(x)
        parents[f * lev : (f + 1) * lev, :128] = high
        parents[f * lev : (f + 1) * lev, 128:] = low
    fine = dot(parents[...], table_ref[...])
    out_ref[...] = fine.astype(jnp.bfloat16).reshape(out_ref.shape)


VMEM = pl.BlockSpec(memory_space=pltpu.VMEM)
SMEM = pl.BlockSpec(memory_space=pltpu.SMEM)


def make_strips(state):
    count, lev = state.shape[:2]
    return pl.pallas_call(
        strips_kernel,
        out_shape=(
            jax.ShapeDtypeStruct((count, 2, lev, 128), jnp.float32),
            jax.ShapeDtypeStruct((count, 1024), jnp.float32),
        ),
        in_specs=[VMEM, VMEM],
        out_specs=(VMEM, VMEM),
        compiler_params=pltpu.CompilerParams(vmem_limit_bytes=VMEM_LIMIT),
        name="strips",
    )(state, jnp.asarray(strip_map()))


def make_advanced(ints, coefs, state, edge, nearby, peers):
    count, lev = state.shape[:2]
    col = np.concatenate([ghost_map(2), ghost_map(3)], 0)
    maps = [col, ghost_map(0)[:, :128], ghost_map(1)[:, 896:], stencil_map(), window_map()]
    return pl.pallas_call(
        advance_kernel,
        out_shape=(
            jax.ShapeDtypeStruct(state.shape, jnp.float32),
            jax.ShapeDtypeStruct((peers, lev, 128), jnp.float32),
        ),
        in_specs=[SMEM] * 7 + [VMEM] * 10,
        out_specs=(VMEM, VMEM),
        scratch_shapes=[
            pltpu.VMEM((3, count, 2, lev, 128), jnp.float32),
            pltpu.VMEM((count * lev, 1024), jnp.bfloat16),
            pltpu.VMEM((count, 4, 2, lev, 128), jnp.float32),
        ],
        compiler_params=pltpu.CompilerParams(vmem_limit_bytes=VMEM_LIMIT),
        name="advance",
    )(*ints, *coefs, state, edge, *nearby, *[jnp.asarray(m) for m in maps])


def make_refined(slots, live, received):
    fine = slots.shape[1]
    peers, lev = received.shape[:2]
    size = next(n for n in (24, 16, 8, 6, 4, 2, 1) if fine % n == 0)
    return pl.pallas_call(
        refine_kernel,
        grid=(fine // size,),
        out_shape=jax.ShapeDtypeStruct((fine, lev, 1024), jnp.bfloat16),
        in_specs=[SMEM, SMEM, VMEM, VMEM],
        out_specs=pl.BlockSpec((size, lev, 1024), lambda i: (i, 0, 0)),
        scratch_shapes=[pltpu.VMEM((size * lev, 256), jnp.bfloat16)],
        compiler_params=pltpu.CompilerParams(vmem_limit_bytes=VMEM_LIMIT),
        name="refine",
    )(slots, live, received, jnp.asarray(refine_table()))


def body(
    state,
    courant_row,
    courant_col,
    mixing,
    nbr_block,
    nbr_side,
    nbr_flip,
    send_idx,
    fine_slot,
    fine_count,
):
    peers = lax.axis_size("blocks")
    strips, edge = make_strips(state)
    up = [(i, (i + 1) % peers) for i in range(peers)]
    down = [(j, i) for i, j in up]
    before = lax.ppermute(strips, "blocks", up)
    after = lax.ppermute(strips, "blocks", down)
    edge = lax.ppermute(edge, "slab", [(0, 1), (1, 0)])
    advanced, payload = make_advanced(
        (nbr_block, nbr_side, nbr_flip, send_idx[0]),
        (courant_row, courant_col, mixing),
        state,
        edge,
        (before, strips, after),
        peers,
    )
    received = lax.all_to_all(payload, "blocks", split_axis=0, concat_axis=0, tiled=True)
    return advanced, make_refined(fine_slot, fine_count, received)


def solution(mesh):
    in_specs = (
        P("blocks", "slab", None),
        P("slab"),
        P("slab"),
        P("slab"),
        P("blocks", None),
        P("blocks", None),
        P("blocks", None),
        P("blocks", None, None),
        P("blocks", None),
        P("blocks"),
    )
    out_specs = (P("blocks", "slab", None), P("blocks", "slab", None))
    return jax.shard_map(body, mesh=mesh, in_specs=in_specs, out_specs=out_specs, check_vma=False)
```

time: 232 us -> 99.9 us (0.43)
  local copies, waits for them, and re-layouts: 78.2 us -> 3.07 us
  other arithmetic: 60.6 us -> 0 us
  Pallas kernels: 0 us -> 30.9 us
  matrix products: 13.2 us -> 0 us
  waiting for transfers between devices: 55 us -> 47 us
  starting transfers between devices: 22 us -> 17.3 us
    sub x1 -> x0, other arithmetic: 31.1 us -> none  [advance(): -courant_row[None, :, None, None] * row_diff]
    pallas_call x0 -> x3, Pallas kernels: none -> 30.9 us  [the longest x1 22.7 us: make_advanced(): pl.pallas_call(advance_kernel, out_shape=(jax.ShapeDtypeStruct(state.shap...]
    transpose x1 -> x0, local copies, waits for them, and re-layouts: 16.3 us -> none  [windows_of(): return grid.transpose(0, 2, 4, 1, 3, 5).reshape(count * 16, lev, 64)]
    gather x3 -> x0, local copies, waits for them, and re-layouts: 15.6 us -> none  [the longest x1 10.1 us: body(): windows[send_idx[0].reshape(-1)].reshape(peers, send_idx.shape[2], lev, 64)]
    ppermute x4 -> x3, waiting for transfers between devices: 31.8 us -> 17.2 us  [the longest x1 9.62 us: body(): after = lax.ppermute(strips, 'blocks', down)]
    add x2 -> x0, other arithmetic: 13.5 us -> none  [the longest x1 13.5 us: advance(): return state + tend.reshape(count, lev, 1024) + mixing[None, :, None] * vert]
    dot_general x1 -> x0, matrix products: 13.2 us -> none  [body(): jnp.einsum('flc,cp->flp', parent, table, precision=lax.Precision.HIGHEST)]
    unnamed x23 -> x36, local copies, waits for them, and re-layouts: 16 us -> 3.07 us
  transfers between devices with their start and end apart: 5 -> 4, of which waited for: 2 -> 4; matrix products, arithmetic and copies ran while one was open for 37% -> 0% of each run, Pallas kernels for 0% -> 0%
where the time goes in v1:
time: 99.9 us; the launch traced here: 99.7 us
  waiting for transfers between devices  47 us (47%)
  Pallas kernels  30.9 us (31%)
  starting transfers between devices  17.3 us (17%)
  local copies, waits for them, and re-layouts  3.07 us (3%)
  between operations  1.42 us (1%)
    all_to_all x1, waiting for transfers between devices, body(): lax.all_to_all(payload, 'blocks', split_axis=0, concat_axis=0, tiled=True)  29.8 us
    pallas_call x1, Pallas kernels, make_advanced(): pl.pallas_call(advance_kernel, out_shape=(jax.ShapeDtypeStruct(state.shap...  22.7 us
    all_to_all x1, starting transfers between devices, body(): lax.all_to_all(payload, 'blocks', split_axis=0, concat_axis=0, tiled=True)  12.5 us
    ppermute x1, waiting for transfers between devices, body(): after = lax.ppermute(strips, 'blocks', down)  9.62 us
    pallas_call x1, Pallas kernels, make_refined(): pl.pallas_call(refine_kernel, grid=(fine // size,), out_shape=jax.ShapeDt...  6.43 us
    ppermute x1, waiting for transfers between devices, body(): before = lax.ppermute(strips, 'blocks', up)  6.42 us
    ppermute x1, starting transfers between devices, body(): after = lax.ppermute(strips, 'blocks', down)  4.75 us
    unnamed x36, local copies, waits for them, and re-layouts  3.07 us
  transfers between devices with their start and end apart: 4, of which 4 were waited for; matrix products, arithmetic and copies ran while one was open for 0% of the time, Pallas kernels for 0%

profile of v1, /device:TPU:32, one launch (start us, length us, event | category | flops | bytes accessed | tf_op | source)
XLA Modules:
  0.0 99.7 jit_solution(10635331621653452959)
XLA Ops:
  0.6 0.0 copy-start
  0.6 1.6 %copy-done = f32[32,16,1024]{2,1,0:T(8,128)S(1)} copy-done((f32[32,16,1024]{2,1,0:T(8,128)S(1)}, f32[32,16,1024]{2,1,0:T(8,128)}, u32[]{:S(2)}) %copy-start) | copy-done | bytes 2097176
  2.2 0.0 copy-start.3
  2.2 1.0 %copy-done.3 = bf16[1024,256]{1,0:T(8,128)(2,1)S(1)} copy-done((bf16[1024,256]{1,0:T(8,128)(2,1)S(1)}, bf16[1024,256]{1,0:T(8,128)(2,1)}, u32[]{:S(2)}) %copy-start.3) | copy-done | bytes 524312
  3.3 0.0 copy-start.12
  3.3 0.0 copy-start.13
  3.3 0.0 copy-start.14
  3.3 0.0 copy-start.15
  3.3 0.0 copy-start.1
  3.3 0.0 copy-start.4
  3.3 0.0 copy-start.5
  3.3 0.0 copy-start.6
  3.3 0.0 copy-start.7
  3.3 0.0 copy-start.9
  3.4 0.0 copy-start.10
  3.4 0.0 copy-start.11
  3.4 1.7 %strips.1 = (f32[32,2,16,128]{3,2,1,0:T(8,128)S(1)}, f32[32,1024]{1,0:T(8,128)}) custom-call(f32[32,16,1024]{2,1,0:T(8,128)S(1)} %copy-done, bf16[1024,256]{1,0:T(8,128)(2,1)S(1)} %copy-done.3), custom_call_target="tpu_custom_call" | custom-call | tf_op jit(solution)/shard_map/strips/pallas_call | solution.py:262
  5.1 4.8 %collective-permute-start.2 = (f32[32,2,16,128]{3,2,1,0:T(8,128)S(1)}, f32[32,2,16,128]{3,2,1,0:T(8,128)S(1)}, u32[]{:S(2)}, u32[]{:S(2)}) collective-permute-start(f32[32,2,16,128]{3,2,1,0:T(8,128)S(1)} %get-tuple-element.7.own_ref), channel_id=1, source_target_pairs={{2,0},{4,2},{6,4},{8,6},{10,8},{12,10},{14,12},{16,14},{18,16},{20... | collective-permute-start | bytes 1572872 | tf_op jit(solution)/shard_map/ppermute | solution.py:330
  9.9 0.0 collective-permute-start.1
  9.9 0.0 collective-permute-start
  9.9 0.0 copy-done.12
  9.9 0.1 copy.20.block_ref
  10.0 0.0 copy-done.13
  10.0 0.1 copy.21.side_ref
  10.1 0.0 copy-done.14
  10.1 0.1 copy.22.flip_ref
  10.1 0.0 copy-done.15
  10.1 0.1 copy.19
  10.3 1.2 %collective-permute-done.edge_ref = f32[32,1024]{1,0:T(8,128)S(1)} collective-permute-done((f32[32,1024]{1,0:T(8,128)}, f32[32,1024]{1,0:T(8,128)S(1)}, u32[]{:S(2)}, u32[]{:S(2)}) %collective-permute-start) | collective-permute-done | bytes 131104 | tf_op jit(solution)/shard_map/ppermute | solution.py:331
  11.4 9.6 %collective-permute-done.2.next_ref = f32[32,2,16,128]{3,2,1,0:T(8,128)S(1)} collective-permute-done((f32[32,2,16,128]{3,2,1,0:T(8,128)S(1)}, f32[32,2,16,128]{3,2,1,0:T(8,128)S(1)}, u32[]{:S(2)}, u32[]{:S(2)}) %collective-permute-start.2) | collective-permute-done | bytes 524320 | tf_op jit(solution)/shard_map/ppermute | solution.py:330
  21.0 6.4 %collective-permute-done.1.prev_ref = f32[32,2,16,128]{3,2,1,0:T(8,128)S(1)} collective-permute-done((f32[32,2,16,128]{3,2,1,0:T(8,128)S(1)}, f32[32,2,16,128]{3,2,1,0:T(8,128)S(1)}, u32[]{:S(2)}, u32[]{:S(2)}) %collective-permute-start.1) | collective-permute-done | bytes 524320 | tf_op jit(solution)/shard_map/ppermute | solution.py:329
  27.5 0.0 copy-done.1
  27.5 0.0 copy-done.4
  27.5 0.0 copy-done.5
  27.5 0.0 copy-done.6
  27.5 0.0 copy-done.7
  27.5 0.0 copy-done.9
  27.5 0.0 copy-done.10
  27.5 0.0 copy-done.11
  27.5 22.7 %advance.1 = (f32[32,16,1024]{2,1,0:T(8,128)}, f32[128,16,128]{2,1,0:T(8,128)}) custom-call(s32[32,4]{1,0:T(8,128)S(1)} %copy.20.block_ref, s32[32,4]{1,0:T(8,128)S(1)} %copy.21.side_ref, s32[32,4]{1,0:T(8,128)S(1)} %copy.22.flip_ref, s32[128,2]{1,0:T(8,128)S(1)} %bitcast.1, f32[16]{0:T(128)S(1)} %copy-done.9, f32[16]{0:T(128)S(1)} %copy-done.10, ...), custom_call_target="tpu_custom_call" | custom-call | tf_op jit(solution)/shard_map/advance/pallas_call | solution.py:279
  50.3 0.0 copy-start.2
  50.3 0.0 copy-start.8
  50.3 12.5 %all-to-all-start = ((f32[128,16,128]{2,1,0:T(8,128)}), f32[128,16,128]{2,1,0:T(8,128)S(1)}, u32[]{:S(2)}, u32[]{:S(2)}) async-start(f32[128,16,128]{2,1,0:T(8,128)} %get-tuple-element.9), calls=%async_computation | async-start | bytes 2097152 | tf_op jit(solution)/shard_map/all_to_all | solution.py:340
  63.4 29.8 %all-to-all-done.recv_ref = f32[128,16,128]{2,1,0:T(8,128)S(1)} async-done(((f32[128,16,128]{2,1,0:T(8,128)}), f32[128,16,128]{2,1,0:T(8,128)S(1)}, u32[]{:S(2)}, u32[]{:S(2)}) %all-to-all-start) | async-done | bytes 1048608 | tf_op jit(solution)/shard_map/all_to_all | solution.py:340
  93.2 0.0 copy-done.2
  93.2 0.0 copy-done.8
  93.2 6.4 %refine.1 = bf16[192,16,1024]{2,1,0:T(8,128)(2,1)} custom-call(s32[1,192]{1,0:T(1,128)S(1)} %copy-done.8, s32[1]{0:T(128)S(6)} %copy.23.count_ref, f32[128,16,128]{2,1,0:T(8,128)S(1)} %all-to-all-done.recv_ref, bf16[256,1024]{1,0:T(8,128)(2,1)S(1)} %copy-done.2), custom_call_target="tpu_custom_call" | custom-call | tf_op jit(solution)/shard_map/refine/pallas_call | solution.py:301
Async XLA Ops:
  0.6 1.6 %copy-start = (f32[32,16,1024]{2,1,0:T(8,128)S(1)}, f32[32,16,1024]{2,1,0:T(8,128)}, u32[]{:S(2)}) copy-start(f32[32,16,1024]{2,1,0:T(8,128)} %state_ref.3) | copy-start | bytes 6291460
  2.2 1.0 %copy-start.3 = (bf16[1024,256]{1,0:T(8,128)(2,1)S(1)}, bf16[1024,256]{1,0:T(8,128)(2,1)}, u32[]{:S(2)}) copy-start(bf16[1024,256]{1,0:T(8,128)(2,1)} %constant.14.clone.pick_ref) | copy-start | bytes 1572868
  3.3 6.6 %copy-start.12 = (s32[32,4]{0,1:T(4,128)S(1)}, s32[32,4]{0,1:T(4,128)}, u32[]{:S(2)}) copy-start(s32[32,4]{0,1:T(4,128)} %param.21) | copy-start | bytes 1540
  3.3 6.7 %copy-start.13 = (s32[32,4]{0,1:T(4,128)S(1)}, s32[32,4]{0,1:T(4,128)}, u32[]{:S(2)}) copy-start(s32[32,4]{0,1:T(4,128)} %param.22) | copy-start | bytes 1540
  3.3 6.8 %copy-start.14 = (s32[32,4]{0,1:T(4,128)S(1)}, s32[32,4]{0,1:T(4,128)}, u32[]{:S(2)}) copy-start(s32[32,4]{0,1:T(4,128)} %param.23) | copy-start | bytes 1540
  3.3 6.9 %copy-start.15 = (s32[1,128,2]{1,2,0:T(2,128)S(1)}, s32[1,128,2]{1,2,0:T(2,128)}, u32[]{:S(2)}) copy-start(s32[1,128,2]{1,2,0:T(2,128)} %param.24) | copy-start | bytes 3076
  3.3 24.2 %copy-start.1 = (bf16[512,1024]{1,0:T(8,128)(2,1)S(1)}, bf16[512,1024]{1,0:T(8,128)(2,1)}, u32[]{:S(2)}) copy-start(bf16[512,1024]{1,0:T(8,128)(2,1)} %constant.15.clone.col_ref) | copy-start | bytes 3145732
  3.3 24.2 %copy-start.4 = (bf16[512,256]{1,0:T(8,128)(2,1)S(1)}, bf16[512,256]{1,0:T(8,128)(2,1)}, u32[]{:S(2)}) copy-start(bf16[512,256]{1,0:T(8,128)(2,1)} %constant.19.clone.win_ref) | copy-start | bytes 786436
  3.3 24.2 %copy-start.5 = (bf16[512,256]{1,0:T(8,128)(2,1)S(1)}, bf16[512,256]{1,0:T(8,128)(2,1)}, u32[]{:S(2)}) copy-start(bf16[512,256]{1,0:T(8,128)(2,1)} %constant.18.clone.sten_ref) | copy-start | bytes 786436
  3.3 24.2 %copy-start.6 = (bf16[256,128]{1,0:T(8,128)(2,1)S(1)}, bf16[256,128]{1,0:T(8,128)(2,1)}, u32[]{:S(2)}) copy-start(bf16[256,128]{1,0:T(8,128)(2,1)} %constant.17.clone.row1_ref) | copy-start | bytes 196612
  3.3 24.2 %copy-start.7 = (bf16[256,128]{1,0:T(8,128)(2,1)S(1)}, bf16[256,128]{1,0:T(8,128)(2,1)}, u32[]{:S(2)}) copy-start(bf16[256,128]{1,0:T(8,128)(2,1)} %constant.16.clone.row0_ref) | copy-start | bytes 196612
  3.3 24.2 %copy-start.9 = (f32[16]{0:T(128)S(1)}, f32[16]{0:T(128)}, u32[]{:S(2)}) copy-start(f32[16]{0:T(128)} %crow_ref.1) | copy-start | bytes 196
  3.4 24.2 %copy-start.10 = (f32[16]{0:T(128)S(1)}, f32[16]{0:T(128)}, u32[]{:S(2)}) copy-start(f32[16]{0:T(128)} %ccol_ref.1) | copy-start | bytes 196
  3.4 24.2 %copy-start.11 = (f32[16]{0:T(128)S(1)}, f32[16]{0:T(128)}, u32[]{:S(2)}) copy-start(f32[16]{0:T(128)} %mix_ref.1) | copy-start | bytes 196
  5.1 15.9 %collective-permute-start.2 = (f32[32,2,16,128]{3,2,1,0:T(8,128)S(1)}, f32[32,2,16,128]{3,2,1,0:T(8,128)S(1)}, u32[]{:S(2)}, u32[]{:S(2)}) collective-permute-start(f32[32,2,16,128]{3,2,1,0:T(8,128)S(1)} %get-tuple-element.7.own_ref), channel_id=1, source_target_pairs={{2,0},{4,2},{6,4},{8,6},{10,8},{12,10},{14,12},{16,14},{18,16},{20... | collective-permute-start | bytes 1572872 | tf_op jit(solution)/shard_map/ppermute | solution.py:330
  9.9 17.6 %collective-permute-start.1 = (f32[32,2,16,128]{3,2,1,0:T(8,128)S(1)}, f32[32,2,16,128]{3,2,1,0:T(8,128)S(1)}, u32[]{:S(2)}, u32[]{:S(2)}) collective-permute-start(f32[32,2,16,128]{3,2,1,0:T(8,128)S(1)} %get-tuple-element.7.own_ref), channel_id=1, source_target_pairs={{0,2},{2,4},{4,6},{6,8},{8,10},{10,12},{12,14},{14,16},{16,18},{18... | collective-permute-start | bytes 1572872 | tf_op jit(solution)/shard_map/ppermute | solution.py:329
  9.9 1.6 %collective-permute-start = (f32[32,1024]{1,0:T(8,128)}, f32[32,1024]{1,0:T(8,128)S(1)}, u32[]{:S(2)}, u32[]{:S(2)}) collective-permute-start(f32[32,1024]{1,0:T(8,128)} %get-tuple-element.6), channel_id=1, source_target_pairs={{0,1},{1,0},{2,3},{3,2},{4,5},{5,4},{6,7},{7,6},{8,9},{9,8},{10,11... | collective-permute-start | bytes 393224 | tf_op jit(solution)/shard_map/ppermute | solution.py:331
  50.3 43.0 %copy-start.2 = (bf16[256,1024]{1,0:T(8,128)(2,1)S(1)}, bf16[256,1024]{1,0:T(8,128)(2,1)}, u32[]{:S(2)}) copy-start(bf16[256,1024]{1,0:T(8,128)(2,1)} %constant.20.clone.table_ref) | copy-start | bytes 1572868
  50.3 43.0 %copy-start.8 = (s32[1,192]{1,0:T(1,128)S(1)}, s32[1,192]{1,0:T(1,128)}, u32[]{:S(2)}) copy-start(s32[1,192]{1,0:T(1,128)} %slot_ref.1) | copy-start | bytes 2308
  50.3 43.0 %all-to-all-start = ((f32[128,16,128]{2,1,0:T(8,128)}), f32[128,16,128]{2,1,0:T(8,128)S(1)}, u32[]{:S(2)}, u32[]{:S(2)}) async-start(f32[128,16,128]{2,1,0:T(8,128)} %get-tuple-element.9), calls=%async_computation | async-start | bytes 2097152 | tf_op jit(solution)/shard_map/all_to_all | solution.py:340

commit v2 on v1

v2 whole, which is shorter than its diff:
```python
import jax
import jax.numpy as jnp
import ml_dtypes
import numpy as np
from jax import lax
from jax.experimental import pallas as pl
from jax.experimental.pallas import tpu as pltpu
from jax.sharding import PartitionSpec as P

CHUNK = 8
PACK = 16
VMEM_LIMIT = 24 * 1024 * 1024


def interp_1d():
    table = np.zeros((32, 8))
    for fine in range(32):
        x = (fine + 0.5) / 4.0
        start = min(max(int(np.floor(x - 0.5)) - 1, 0), 4)
        nodes = start + np.arange(4) + 0.5
        for a in range(4):
            weight = 1.0
            for b in range(4):
                if b != a:
                    weight *= (x - nodes[b]) / (nodes[a] - nodes[b])
            table[fine, start + a] = weight
    return table


def as_bf16(array):
    return np.asarray(array, np.float32).astype(ml_dtypes.bfloat16)


def refine_table():
    table = interp_1d()
    full = np.kron(table, table).T.astype(np.float32)
    high = as_bf16(full)
    low = as_bf16(full - high.astype(np.float32))
    return np.concatenate([high, low, high, low], 0)


def strip_cell(side, depth, t):
    line = depth if side in (0, 2) else 31 - depth
    return line * 32 + t if side < 2 else t * 32 + line


def ghost_map(side):
    first = side in (0, 2)
    out = np.zeros((128, 1024))
    for flip in range(2):
        for t in range(32):
            to = 31 - t if flip else t
            near = flip * 64 + t
            far = flip * 64 + 32 + t
            sign = 1.0 if first else -1.0
            out[near, strip_cell(side, 0, to)] += 8.0 * sign
            out[far, strip_cell(side, 0, to)] -= sign
            out[near, strip_cell(side, 1, to)] -= sign
    return as_bf16(np.concatenate([out, out], 0))


def window_order(table):
    out = np.zeros_like(table)
    for row in range(32):
        for col in range(32):
            to = (row // 8) * 256 + (col // 8) * 64 + (row % 8) * 8 + col % 8
            out[:, to] = table[:, row * 32 + col]
    return out


def stencil_map():
    own = np.zeros((128, 256))
    other = np.zeros((128, 256))
    weights = {-2: -1.0, -1: 8.0, 1: -8.0, 2: 1.0}
    for row in range(4):
        for col in range(32):
            lane = row * 32 + col
            for step, weight in weights.items():
                r = row + step
                if 0 <= r < 4:
                    own[r * 32 + col, lane] += weight
                else:
                    other[(r % 4) * 32 + col, lane] += weight
                c = col + step
                if 0 <= c < 32:
                    own[row * 32 + c, 128 + lane] += weight
    return as_bf16(np.concatenate([own, own, other, other], 0))


def window_map():
    pick = np.zeros((256, 256))
    for row in range(8):
        for col in range(32):
            pick[row * 32 + col, (col // 8) * 64 + row * 8 + col % 8] = 1.0
    return as_bf16(np.concatenate([pick, pick], 0))


def split(x):
    high = x.astype(jnp.bfloat16)
    low = (x - high.astype(jnp.float32)).astype(jnp.bfloat16)
    return high, low


def dot(a, b):
    return jnp.dot(a, b, preferred_element_type=jnp.float32)


def strips_kernel(state_ref, strips_ref, edge_ref, held, sems):
    slab = lax.axis_index("slab")
    count, lev = state_ref.shape[0], state_ref.shape[1]
    steps = count // CHUNK
    copies = []
    for i in range(steps):
        part = pl.ds(i * CHUNK, CHUNK)
        copies.append(pltpu.make_async_copy(state_ref.at[part], held.at[part], sems.at[i]))
        copies[i].start()
    cell = lax.broadcasted_iota(jnp.int32, (1024, 128), 0)
    to = lax.broadcasted_iota(jnp.int32, (1024, 128), 1)
    line = to // 32
    line = jnp.where(line < 2, line, 33 - line)
    pick = jnp.where((cell // 32 == to % 32) & (cell % 32 == line), 1.0, 0.0).astype(jnp.bfloat16)
    rows = CHUNK * lev
    lane = lax.broadcasted_iota(jnp.int32, (rows, 128), 1)
    for i in range(steps):
        copies[i].wait()
        part = slice(i * CHUNK, i * CHUNK + CHUNK)
        x = held[part]
        tail = x[:, :, 896:].reshape(rows, 128)
        tail = jnp.where((lane // 32) % 2 == 0, pltpu.roll(tail, 96, 1), pltpu.roll(tail, 32, 1))
        strips_ref[part, 0] = jnp.where(lane < 64, x[:, :, :128].reshape(rows, 128), tail).reshape(CHUNK, lev, 128)
        high, low = split(x.reshape(rows, 1024))
        strips_ref[part, 1] = (dot(high, pick) + dot(low, pick)).reshape(CHUNK, lev, 128)
        edge_ref[part] = jnp.where(slab == 0, x[:, lev - 1, :], x[:, 0, :])


def levels_of(ref, lev):
    at = lax.broadcasted_iota(jnp.int32, (lev, 128), 0)
    out = jnp.zeros((lev, 128), jnp.float32)
    for l in range(lev):
        out = jnp.where(at == l, ref[l], out)
    return out


def local_kernel(crow_ref, ccol_ref, mix_ref, state_ref, edge_ref, sten_ref, win_ref, base_ref, wins_ref):
    slab = lax.axis_index("slab")
    count, lev = state_ref.shape[0], state_ref.shape[1]
    a_row = levels_of(crow_ref, lev) * (1.0 / 12.0)
    a_col = levels_of(ccol_ref, lev) * (1.0 / 12.0)
    mix = levels_of(mix_ref, lev)
    rows = CHUNK * lev
    lane = lax.broadcasted_iota(jnp.int32, (rows, 128), 1)
    level = lax.broadcasted_iota(jnp.int32, (CHUNK, lev, 128), 1)
    zero = jnp.zeros((rows, 128), jnp.float32)

    def step(i, carry):
        blocks = pl.ds(pl.multiple_of(i * CHUNK, CHUNK), CHUNK)
        tiles = [state_ref[blocks, :, 128 * j : 128 * j + 128] for j in range(8)]
        flat = [t.reshape(rows, 128) for t in tiles]
        left = []
        for j in range(8):
            other = jnp.where(lane < 64, flat[j + 1] if j < 7 else zero, flat[j - 1] if j else zero)
            left.append(jnp.concatenate(split(flat[j]) + split(other), 1))
        diff = dot(jnp.concatenate(left, 0), sten_ref[...])
        done = []
        for j in range(8):
            lanes = slice(128 * j, 128 * j + 128)
            x = tiles[j]
            edge = edge_ref[blocks, lanes][:, None, :]
            below = jnp.where(level == 0, jnp.where(slab == 0, 0.0, edge), pltpu.roll(x, 1, 1))
            above = jnp.where(level == lev - 1, jnp.where(slab == 0, edge, 0.0), pltpu.roll(x, lev - 1, 1))
            vert = above - 2.0 * x + below
            d = diff[rows * j : rows * j + rows].reshape(CHUNK, lev, 256)
            out = x + a_row * d[:, :, :128] + a_col * d[:, :, 128:] + mix * vert
            base_ref[blocks, :, lanes] = out
            done.append(out.reshape(rows, 128))
        pairs = []
        for j in range(4):
            pairs.append(jnp.concatenate(split(jnp.concatenate(done[2 * j : 2 * j + 2], 1)), 1))
        w = dot(jnp.concatenate(pairs, 0), win_ref[...])
        for j in range(4):
            v = w[rows * j : rows * j + rows].reshape(CHUNK, lev, 256)
            wins_ref[blocks, 2 * j] = v[:, :, :128]
            wins_ref[blocks, 2 * j + 1] = v[:, :, 128:]
        return carry

    lax.fori_loop(0, count // CHUNK, step, 0)


def pack_kernel(
    code_ref,
    send_ref,
    crow_ref,
    ccol_ref,
    base_ref,
    prev_ref,
    own_ref,
    next_ref,
    col0_ref,
    col1_ref,
    row0_ref,
    row1_ref,
    pay_ref,
    ghosts_ref,
    near,
    wins,
):
    count, lev = own_ref.shape[0], own_ref.shape[2]
    near[0:count] = prev_ref[...]
    near[count : 2 * count] = own_ref[...]
    near[2 * count :] = next_ref[...]
    a_row = levels_of(crow_ref, lev) * (1.0 / 12.0)
    a_col = levels_of(ccol_ref, lev) * (1.0 / 12.0)
    half = lax.broadcasted_iota(jnp.int32, (lev, 128), 1) // 64
    rows = CHUNK * lev

    def gather(i, carry):
        for s in range(4):
            parts = []
            for n in range(CHUNK):
                code = code_ref[s, i * CHUNK + n]
                x = near[code >> 3, (code >> 2) & 1]
                x = jnp.where((code & 2) == 0, x, pltpu.roll(x, 64, 1))
                parts.append(jnp.where(half == (code & 1), x, 0.0))
            x = jnp.stack(parts) * (a_row if s < 2 else a_col)
            high, low = split(x.reshape(rows, 128))
            at = pl.ds(pl.multiple_of(i * rows, rows), rows)
            ghosts_ref[at, s * 256 : s * 256 + 128] = high
            ghosts_ref[at, s * 256 + 128 : s * 256 + 256] = low
        return carry

    lax.fori_loop(0, count // CHUNK, gather, 0)

    def add(i, carry):
        blocks = pl.ds(pl.multiple_of(i * CHUNK, CHUNK), CHUNK)
        at = pl.ds(pl.multiple_of(i * rows, rows), rows)
        row0 = dot(ghosts_ref[at, 0:256], row0_ref[...]).reshape(CHUNK, lev, 256)
        row1 = dot(ghosts_ref[at, 256:512], row1_ref[...]).reshape(CHUNK, lev, 256)
        for h, col_ref in enumerate((col0_ref, col1_ref)):
            c = dot(ghosts_ref[at, 512 + 256 * h : 768 + 256 * h], col_ref[...]).reshape(CHUNK, lev, 512)
            for j in range(4):
                v = base_ref[blocks, 2 * j + h] + c[:, :, 128 * j : 128 * j + 128]
                if j == 0:
                    v = v + row0[:, :, 128 * h : 128 * h + 128]
                if j == 3:
                    v = v + row1[:, :, 128 * h : 128 * h + 128]
                wins[blocks, 2 * j + h] = v
        return carry

    lax.fori_loop(0, count // CHUNK, add, 0)

    def pack(d, carry):
        parts = []
        for k in range(2):
            w = send_ref[k, d]
            x = wins[w >> 4, (w >> 1) & 7]
            parts.append(jnp.where((w & 1) == k, x, pltpu.roll(x, 64, 1)))
        pay_ref[d] = jnp.where(half == 0, parts[0], parts[1])
        return carry

    lax.fori_loop(0, pay_ref.shape[0], pack, 0, unroll=PACK)


def finish_kernel(base_ref, ghosts_ref, col_ref, row0_ref, row1_ref, out_ref):
    blocks, lev = base_ref.shape[0], base_ref.shape[1]
    c = dot(ghosts_ref[:, 512:1024], col_ref[...]).reshape(blocks, lev, 1024)
    out_ref[...] = base_ref[...] + c
    out_ref[:, :, :128] += dot(ghosts_ref[:, 0:256], row0_ref[...]).reshape(blocks, lev, 128)
    out_ref[:, :, 896:] += dot(ghosts_ref[:, 256:512], row1_ref[...]).reshape(blocks, lev, 128)


def refine_kernel(slot_ref, count_ref, recv_ref, table_ref, out_ref, parents, held, sems):
    lev = recv_ref.shape[1]
    steps = sems.shape[0]
    size = out_ref.shape[0] // steps
    half = lax.broadcasted_iota(jnp.int32, (lev, 128), 1) // 64
    live = count_ref[0]

    def copy(i):
        part = pl.ds(i * size, size)
        return pltpu.make_async_copy(held.at[part], out_ref.at[part], sems.at[i])

    def step(i, carry):
        start = i * size
        for f in range(size):
            slot = slot_ref[0, start + f]
            x = recv_ref[slot >> 1]
            x = jnp.where(half == (slot & 1), x, pltpu.roll(x, 64, 1))
            x = jnp.where(start + f < live, x, 0.0)
            high, low = split(x)
            parents[f * lev : (f + 1) * lev, :128] = high
            parents[f * lev : (f + 1) * lev, 128:] = low
        fine = dot(parents[...], table_ref[...])
        held[pl.ds(start, size)] = fine.astype(jnp.bfloat16).reshape(size, lev, 1024)
        copy(i).start()
        return carry

    lax.fori_loop(0, steps, step, 0)
    for i in range(steps):
        copy(i).wait()


VMEM = pl.BlockSpec(memory_space=pltpu.VMEM)
SMEM = pl.BlockSpec(memory_space=pltpu.SMEM)
HBM = pl.BlockSpec(memory_space=pltpu.HBM)
PARAMS = pltpu.CompilerParams(vmem_limit_bytes=VMEM_LIMIT)


def cost(flops, size):
    return pl.CostEstimate(flops=flops, bytes_accessed=size, transcendentals=0)


def make_strips(state):
    count, lev = state.shape[:2]
    return pl.pallas_call(
        strips_kernel,
        out_shape=(
            jax.ShapeDtypeStruct((count, 2, lev, 128), jnp.float32),
            jax.ShapeDtypeStruct((count, 1024), jnp.float32),
        ),
        in_specs=[HBM],
        out_specs=(VMEM, VMEM),
        scratch_shapes=[pltpu.VMEM(state.shape, jnp.float32), pltpu.SemaphoreType.DMA((count // CHUNK,))],
        compiler_params=PARAMS,
        name="strips",
    )(pltpu.with_memory_space_constraint(state, pltpu.HBM))


def make_local(coefs, state, edge):
    count, lev = state.shape[:2]
    return pl.pallas_call(
        local_kernel,
        out_shape=(
            jax.ShapeDtypeStruct(state.shape, jnp.float32),
            jax.ShapeDtypeStruct((count, 8, lev, 128), jnp.float32),
        ),
        in_specs=[SMEM] * 3 + [VMEM] * 4,
        out_specs=(VMEM, VMEM),
        compiler_params=PARAMS,
        cost_estimate=cost(4 * 10**9, 8 * 10**6),
        name="local",
    )(*coefs, state, edge, jnp.asarray(stencil_map()), jnp.asarray(window_map()))


def make_payload(code, send, coefs, base, nearby):
    count, lev = base.shape[0], base.shape[2]
    sides = [window_order(ghost_map(s)) for s in range(4)]
    cols = [m.reshape(256, 4, 256)[:, :, 128 * h : 128 * h + 128].reshape(256, 512) for h, m in enumerate(sides[2:])]
    maps = cols + [sides[0][:, :256], sides[1][:, 768:]]
    return pl.pallas_call(
        pack_kernel,
        out_shape=(
            jax.ShapeDtypeStruct((send.shape[1], lev, 128), jnp.float32),
            jax.ShapeDtypeStruct((count * lev, 1024), jnp.bfloat16),
        ),
        in_specs=[SMEM] * 4 + [VMEM] * 8,
        out_specs=(VMEM, VMEM),
        scratch_shapes=[
            pltpu.VMEM((3 * count, 2, lev, 128), jnp.float32),
            pltpu.VMEM((count, 8, lev, 128), jnp.float32),
        ],
        compiler_params=PARAMS,
        cost_estimate=cost(10**9, 8 * 10**6),
        name="pack",
    )(code, send, *coefs[:2], base, *nearby, *[jnp.asarray(m) for m in maps])


def make_advanced(base, ghosts):
    count, lev = base.shape[:2]
    maps = [np.concatenate([ghost_map(2), ghost_map(3)], 0), ghost_map(0)[:, :128], ghost_map(1)[:, 896:]]
    return pl.pallas_call(
        finish_kernel,
        grid=(count // CHUNK,),
        out_shape=jax.ShapeDtypeStruct(base.shape, jnp.float32),
        in_specs=[
            pl.BlockSpec((CHUNK, lev, 1024), lambda i: (i, 0, 0)),
            pl.BlockSpec((CHUNK * lev, 1024), lambda i: (i, 0)),
            VMEM,
            VMEM,
            VMEM,
        ],
        out_specs=pl.BlockSpec((CHUNK, lev, 1024), lambda i: (i, 0, 0)),
        compiler_params=PARAMS,
        cost_estimate=cost(2 * 10**9, 8 * 10**6),
        name="finish",
    )(base, ghosts, *[jnp.asarray(m) for m in maps])


def make_refined(slots, live, received):
    fine = slots.shape[1]
    lev = received.shape[1]
    size = next(n for n in (24, 16, 8, 6, 4, 2, 1) if fine % n == 0)
    return pl.pallas_call(
        refine_kernel,
        out_shape=jax.ShapeDtypeStruct((fine, lev, 1024), jnp.bfloat16),
        in_specs=[SMEM, SMEM, VMEM, VMEM],
        out_specs=HBM,
        scratch_shapes=[
            pltpu.VMEM((size * lev, 256), jnp.bfloat16),
            pltpu.VMEM((fine, lev, 1024), jnp.bfloat16),
            pltpu.SemaphoreType.DMA((fine // size,)),
        ],
        compiler_params=PARAMS,
        name="refine",
    )(slots, live, received, jnp.asarray(refine_table()))


def ghost_codes(nbr_block, nbr_side, nbr_flip, count, peers, here):
    rel = (nbr_block // count - here + 1 + peers) % peers
    rel = jnp.where(here % 2 == 0, 2 - rel, rel)
    swap = (nbr_side % 2) ^ nbr_flip
    near = rel * count + nbr_block % count
    return near * 8 + (nbr_side // 2) * 4 + swap * 2 + nbr_flip


def body(
    state,
    courant_row,
    courant_col,
    mixing,
    nbr_block,
    nbr_side,
    nbr_flip,
    send_idx,
    fine_slot,
    fine_count,
):
    peers = lax.axis_size("blocks")
    here = lax.axis_index("blocks")
    strips, edge = make_strips(state)
    first = [(i, i ^ 1) for i in range(peers)]
    second = [(i, (i + (1 if i % 2 else -1)) % peers) for i in range(peers)]
    before = lax.ppermute(strips, "blocks", first)
    after = lax.ppermute(strips, "blocks", second)
    edge = lax.ppermute(edge, "slab", [(0, 1), (1, 0)])
    coefs = (courant_row, courant_col, mixing)
    base, wins = make_local(coefs, state, edge)
    code = ghost_codes(nbr_block.T, nbr_side.T, nbr_flip.T, state.shape[0], peers, here)
    payload, ghosts = make_payload(code, send_idx[0].T, coefs, wins, (before, strips, after))
    received = lax.all_to_all(payload, "blocks", split_axis=0, concat_axis=0, tiled=True)
    advanced = make_advanced(base, ghosts)
    return advanced, make_refined(fine_slot, fine_count, received)


def solution(mesh):
    in_specs = (
        P("blocks", "slab", None),
        P("slab"),
        P("slab"),
        P("slab"),
        P("blocks", None),
        P("blocks", None),
        P("blocks", None),
        P("blocks", None, None),
        P("blocks", None),
        P("blocks"),
    )
    out_specs = (P("blocks", "slab", None), P("blocks", "slab", None))
    return jax.shard_map(body, mesh=mesh, in_specs=in_specs, out_specs=out_specs, check_vma=False)
```

time: 99.9 us -> 77.9 us (0.78)
  waiting for transfers between devices: 47 us -> 30.3 us
  Pallas kernels: 30.9 us -> 19.4 us
  local copies, waits for them, and re-layouts: 3.07 us -> 7.09 us
  starting transfers between devices: 17.3 us -> 19.2 us
    pallas_call x2 -> x4, Pallas kernels: 29.2 us -> 17 us  [the longest x1 5.32 us: make_payload(): pl.pallas_call(pack_kernel, out_shape=(jax.ShapeDtypeStruct((send.shape[1...]
    ppermute x2, waiting for transfers between devices: 16 us -> 4.79 us  [the longest x1 4.43 us: body(): after = lax.ppermute(strips, 'blocks', second)]
    all_to_all x1, waiting for transfers between devices: 29.8 us -> 24.3 us  [body(): lax.all_to_all(payload, 'blocks', split_axis=0, concat_axis=0, tiled=True)]
    unnamed x36 -> x46, local copies, waits for them, and re-layouts: 3.07 us -> 7.09 us
    all_to_all x1, starting transfers between devices: 12.5 us -> 14.3 us  [body(): lax.all_to_all(payload, 'blocks', split_axis=0, concat_axis=0, tiled=True)]
  transfers between devices with their start and end apart: 4 -> 4, of which waited for: 4 -> 4; matrix products, arithmetic and copies ran while one was open for 0% -> 0% of each run, Pallas kernels for 0% -> 9%
where the time goes in v2:
time: 77.9 us; the launch traced here: 77.6 us
  waiting for transfers between devices  30.3 us (39%)
  Pallas kernels  19.4 us (25%)
  starting transfers between devices  19.2 us (25%)
  local copies, waits for them, and re-layouts  7.09 us (9%)
  between operations  1.51 us (2%)
    all_to_all x1, waiting for transfers between devices, body(): lax.all_to_all(payload, 'blocks', split_axis=0, concat_axis=0, tiled=True)  24.3 us
    all_to_all x1, starting transfers between devices, body(): lax.all_to_all(payload, 'blocks', split_axis=0, concat_axis=0, tiled=True)  14.3 us
    unnamed x46, local copies, waits for them, and re-layouts  7.09 us
    pallas_call x1, Pallas kernels, make_payload(): pl.pallas_call(pack_kernel, out_shape=(jax.ShapeDtypeStruct((send.shape[1...  5.32 us
    pallas_call x1, Pallas kernels, make_refined(): pl.pallas_call(refine_kernel, out_shape=jax.ShapeDtypeStruct((fine, lev,...  4.91 us
    ppermute x1, starting transfers between devices, body(): after = lax.ppermute(strips, 'blocks', second)  4.85 us
    ppermute x1, waiting for transfers between devices, body(): after = lax.ppermute(strips, 'blocks', second)  4.43 us
    pallas_call x1, Pallas kernels, make_local(): pl.pallas_call(local_kernel, out_shape=(jax.ShapeDtypeStruct(state.shape,...  4.09 us
  transfers between devices with their start and end apart: 4, of which 4 were waited for; matrix products, arithmetic and copies ran while one was open for 0% of the time, Pallas kernels for 9%

profile of v2, /device:TPU:32, one launch (start us, length us, event | category | flops | bytes accessed | tf_op | source)
XLA Modules:
  0.0 77.6 jit_solution(9274533541935106410)
XLA Ops:
  0.6 0.0 copy-start
  0.6 0.0 copy-start.20
  0.7 0.0 copy-start.21
  0.7 0.0 copy-start.22
  0.7 0.0 copy-start.9
  0.7 0.0 copy-start.8
  0.7 0.0 copy-start.12
  0.7 2.4 %strips.1 = (f32[32,2,16,128]{3,2,1,0:T(8,128)S(1)}, f32[32,1024]{1,0:T(8,128)S(1)}) custom-call(f32[32,16,1024]{2,1,0:T(8,128)} %state_ref.3), custom_call_target="tpu_custom_call" | custom-call | tf_op jit(solution)/shard_map/strips/pallas_call | solution.py:314
  3.2 4.8 %collective-permute-start.2 = (f32[32,2,16,128]{3,2,1,0:T(8,128)S(1)}, f32[32,2,16,128]{3,2,1,0:T(8,128)S(1)}, u32[]{:S(2)}, u32[]{:S(2)}) collective-permute-start(f32[32,2,16,128]{3,2,1,0:T(8,128)S(1)} %get-tuple-element.11.own_ref), channel_id=1, source_target_pairs={{0,254},{2,4},{4,2},{6,8},{8,6},{10,12},{12,10},{14,16},{16,14},{1... | collective-permute-start | bytes 1572872 | tf_op jit(solution)/shard_map/ppermute | solution.py:433
  8.0 0.0 collective-permute-start.1
  8.0 0.0 collective-permute-start
  8.0 0.0 copy-done.20
  8.0 0.0 copy-done.21
  8.0 0.0 copy-done.22
  8.1 0.0 copy-start.2
  8.1 0.0 copy-start.3
  8.1 0.0 copy-start.4
  8.1 0.0 copy-start.5
  8.1 0.0 copy-start.6
  8.1 1.2 %collective-permute-done.edge_ref = f32[32,1024]{1,0:T(8,128)S(1)} collective-permute-done((f32[32,1024]{1,0:T(8,128)S(1)}, f32[32,1024]{1,0:T(8,128)S(1)}, u32[]{:S(2)}, u32[]{:S(2)}) %collective-permute-start) | collective-permute-done | bytes 131104 | tf_op jit(solution)/shard_map/ppermute | solution.py:434
  9.4 0.0 copy-done
  9.4 0.0 copy-done.9
  9.4 0.0 copy-done.8
  9.4 0.0 copy-done.12
  9.4 0.0 copy-start.14
  9.4 0.9 %copy-done.14 = bf16[512,256]{1,0:T(8,128)(2,1)S(1)} copy-done((bf16[512,256]{1,0:T(8,128)(2,1)S(1)}, bf16[512,256]{1,0:T(8,128)(2,1)}, u32[]{:S(2)}) %copy-start.14) | copy-done | bytes 262168
  10.3 0.9 %copy-done.15 = bf16[512,256]{1,0:T(8,128)(2,1)S(1)} copy-done((bf16[512,256]{1,0:T(8,128)(2,1)S(1)}, bf16[512,256]{1,0:T(8,128)(2,1)}, u32[]{:S(2)}) %copy-start.15) | copy-done | bytes 262168
  11.3 4.1 %local.1 = (f32[32,16,1024]{2,1,0:T(8,128)S(1)}, f32[32,8,16,128]{3,2,1,0:T(8,128)S(1)}) custom-call(f32[16]{0:T(128)S(1)} %copy-done.8, f32[16]{0:T(128)S(1)} %copy-done.9, f32[16]{0:T(128)S(1)} %copy-done.12, f32[32,16,1024]{2,1,0:T(8,128)S(1)} %copy-done, f32[32,1024]{1,0:T(8,128)S(1)} %collective-permute-done.edge_ref, bf16[512,256]{1,0:T(8,128)(2,1)S(1)} %copy-done.15, ...), custom_call_target="tpu_custom_call" | custom-call | flops 4000000000 | bytes 8000000 | tf_op jit(solution)/shard_map/local/pallas_call | solution.py:330
  15.4 0.0 copy-start.18
  15.4 1.3 %copy-done.18 = f32[32,16,1024]{2,1,0:T(8,128)} copy-done((f32[32,16,1024]{2,1,0:T(8,128)}, f32[32,16,1024]{2,1,0:T(8,128)S(1)}, u32[]{:S(2)}) %copy-start.18) | copy-done | bytes 2097176
  16.7 4.4 %collective-permute-done.2.next_ref = f32[32,2,16,128]{3,2,1,0:T(8,128)S(1)} collective-permute-done((f32[32,2,16,128]{3,2,1,0:T(8,128)S(1)}, f32[32,2,16,128]{3,2,1,0:T(8,128)S(1)}, u32[]{:S(2)}, u32[]{:S(2)}) %collective-permute-start.2) | collective-permute-done | bytes 524320 | tf_op jit(solution)/shard_map/ppermute | solution.py:433
  21.1 0.4 collective-permute-done.1.prev_ref
  21.5 0.0 copy-done.2
  21.5 0.0 copy-done.3
  21.5 0.0 copy-done.4
  21.5 0.0 copy-done.5
  21.5 0.0 copy-done.6
  21.5 5.3 %pack.1 = (f32[128,16,128]{2,1,0:T(8,128)}, bf16[512,1024]{1,0:T(8,128)(2,1)S(1)}) custom-call(s32[4,32]{1,0:T(4,128)S(1)} %fusion.8.code_ref, s32[2,128]{1,0:T(2,128)S(1)} %bitcast.39, f32[16]{0:T(128)S(1)} %copy-done.8, f32[16]{0:T(128)S(1)} %copy-done.9, f32[32,8,16,128]{3,2,1,0:T(8,128)S(1)} %get-tuple-element.10.base_ref, ...), custom_call_target="tpu_custom_call" | custom-call | flops 1000000000 | bytes 8000000 | tf_op jit(solution)/shard_map/pack/pallas_call | solution.py:349
  26.8 1.0 %copy-done.10 = bf16[512,1024]{1,0:T(8,128)(2,1)} copy-done((bf16[512,1024]{1,0:T(8,128)(2,1)}, bf16[512,1024]{1,0:T(8,128)(2,1)S(1)}, u32[]{:S(2)}) %copy-start.10) | copy-done | bytes 1048600
  27.8 14.3 %all-to-all-start = ((f32[128,16,128]{2,1,0:T(8,128)}), f32[128,16,128]{2,1,0:T(8,128)S(1)}, u32[]{:S(2)}, u32[]{:S(2)}) async-start(f32[128,16,128]{2,1,0:T(8,128)} %get-tuple-element.13), calls=%async_computation | async-start | bytes 2097152 | tf_op jit(solution)/shard_map/all_to_all | solution.py:439
  42.8 0.0 copy-done.16
  42.9 0.0 copy-start.13
  42.9 1.2 %copy-done.13 = bf16[512,1024]{1,0:T(8,128)(2,1)S(1)} copy-done((bf16[512,1024]{1,0:T(8,128)(2,1)S(1)}, bf16[512,1024]{1,0:T(8,128)(2,1)}, u32[]{:S(2)}) %copy-start.13) | copy-done | bytes 1048600
  44.1 1.6 %copy-done.19 = f32[32,16,1024]{2,1,0:T(8,128)S(1)} copy-done((f32[32,16,1024]{2,1,0:T(8,128)S(1)}, f32[32,16,1024]{2,1,0:T(8,128)}, u32[]{:S(2)}) %copy-start.19) | copy-done | bytes 2097176
  45.7 2.7 %finish.1 = f32[32,16,1024]{2,1,0:T(8,128)} custom-call(f32[32,16,1024]{2,1,0:T(8,128)S(1)} %copy-done.19, bf16[512,1024]{1,0:T(8,128)(2,1)S(1)} %copy-done.11, bf16[512,1024]{1,0:T(8,128)(2,1)S(1)} %copy-done.13, bf16[256,128]{1,0:T(8,128)(2,1)S(1)} %copy-done.17, bf16[256,128]{1,0:T(8,128)(2,1)S(1)} %copy-done.16), custom_call_target="tpu_custom_call" | custom-call | flops 2000000000 | bytes 8000000 | tf_op jit(solution)/shard_map/finish/pallas_call | solution.py:370
  48.4 24.3 %all-to-all-done.recv_ref = f32[128,16,128]{2,1,0:T(8,128)S(1)} async-done(((f32[128,16,128]{2,1,0:T(8,128)}), f32[128,16,128]{2,1,0:T(8,128)S(1)}, u32[]{:S(2)}, u32[]{:S(2)}) %all-to-all-start) | async-done | bytes 1048608 | tf_op jit(solution)/shard_map/all_to_all | solution.py:439
  72.7 0.0 copy-done.1
  72.7 4.9 %refine.1 = bf16[192,16,1024]{2,1,0:T(8,128)(2,1)} custom-call(s32[1,192]{1,0:T(1,128)S(1)} %copy-done.7, s32[1]{0:T(128)S(6)} %copy.22.count_ref, f32[128,16,128]{2,1,0:T(8,128)S(1)} %all-to-all-done.recv_ref, bf16[256,1024]{1,0:T(8,128)(2,1)S(1)} %copy-done.1), custom_call_target="tpu_custom_call" | custom-call | tf_op jit(solution)/shard_map/refine/pallas_call | solution.py:392
  (12 shorter events, 0.0 us)
Async XLA Ops:
  0.6 8.7 %copy-start = (f32[32,16,1024]{2,1,0:T(8,128)S(1)}, f32[32,16,1024]{2,1,0:T(8,128)}, u32[]{:S(2)}) copy-start(f32[32,16,1024]{2,1,0:T(8,128)} %state_ref.3) | copy-start | bytes 6291460
  0.6 7.4 %copy-start.20 = (s32[32,4]{0,1:T(4,128)S(1)}, s32[32,4]{0,1:T(4,128)}, u32[]{:S(2)}) copy-start(s32[32,4]{0,1:T(4,128)} %param.26) | copy-start | bytes 1540
  0.7 7.4 %copy-start.21 = (s32[32,4]{0,1:T(4,128)S(1)}, s32[32,4]{0,1:T(4,128)}, u32[]{:S(2)}) copy-start(s32[32,4]{0,1:T(4,128)} %param.25) | copy-start | bytes 1540
  0.7 7.4 %copy-start.22 = (s32[32,4]{0,1:T(4,128)S(1)}, s32[32,4]{0,1:T(4,128)}, u32[]{:S(2)}) copy-start(s32[32,4]{0,1:T(4,128)} %param.24) | copy-start | bytes 1540
  0.7 8.7 %copy-start.9 = (f32[16]{0:T(128)S(1)}, f32[16]{0:T(128)}, u32[]{:S(2)}) copy-start(f32[16]{0:T(128)} %ccol_ref.3) | copy-start | bytes 196
  0.7 8.7 %copy-start.8 = (f32[16]{0:T(128)S(1)}, f32[16]{0:T(128)}, u32[]{:S(2)}) copy-start(f32[16]{0:T(128)} %crow_ref.3) | copy-start | bytes 196
  0.7 8.7 %copy-start.12 = (f32[16]{0:T(128)S(1)}, f32[16]{0:T(128)}, u32[]{:S(2)}) copy-start(f32[16]{0:T(128)} %mix_ref.1) | copy-start | bytes 196
  3.2 18.0 %collective-permute-start.2 = (f32[32,2,16,128]{3,2,1,0:T(8,128)S(1)}, f32[32,2,16,128]{3,2,1,0:T(8,128)S(1)}, u32[]{:S(2)}, u32[]{:S(2)}) collective-permute-start(f32[32,2,16,128]{3,2,1,0:T(8,128)S(1)} %get-tuple-element.11.own_ref), channel_id=1, source_target_pairs={{0,254},{2,4},{4,2},{6,8},{8,6},{10,12},{12,10},{14,16},{16,14},{1... | collective-permute-start | bytes 1572872 | tf_op jit(solution)/shard_map/ppermute | solution.py:433
  8.0 13.5 %collective-permute-start.1 = (f32[32,2,16,128]{3,2,1,0:T(8,128)S(1)}, f32[32,2,16,128]{3,2,1,0:T(8,128)}, u32[]{:S(2)}, u32[]{:S(2)}) collective-permute-start(f32[32,2,16,128]{3,2,1,0:T(8,128)S(1)} %get-tuple-element.11.own_ref), channel_id=1, source_target_pairs={{0,2},{2,0},{4,6},{6,4},{8,10},{10,8},{12,14},{14,12},{16,18},{18,... | collective-permute-start | bytes 1572872 | tf_op jit(solution)/shard_map/ppermute | solution.py:432
  8.0 1.3 %collective-permute-start = (f32[32,1024]{1,0:T(8,128)S(1)}, f32[32,1024]{1,0:T(8,128)S(1)}, u32[]{:S(2)}, u32[]{:S(2)}) collective-permute-start(f32[32,1024]{1,0:T(8,128)S(1)} %get-tuple-element.8), channel_id=1, source_target_pairs={{0,1},{1,0},{2,3},{3,2},{4,5},{5,4},{6,7},{7,6},{8,9},{9,8},{10,11... | collective-permute-start | bytes 393224 | tf_op jit(solution)/shard_map/ppermute | solution.py:434
  8.1 13.4 %copy-start.2 = (bf16[256,512]{1,0:T(8,128)(2,1)S(1)}, bf16[256,512]{1,0:T(8,128)(2,1)}, u32[]{:S(2)}) copy-start(bf16[256,512]{1,0:T(8,128)(2,1)} %constant.103.clone.col1_ref) | copy-start | bytes 786436
  8.1 13.4 %copy-start.3 = (bf16[256,512]{1,0:T(8,128)(2,1)S(1)}, bf16[256,512]{1,0:T(8,128)(2,1)}, u32[]{:S(2)}) copy-start(bf16[256,512]{1,0:T(8,128)(2,1)} %constant.102.clone.col0_ref) | copy-start | bytes 786436
  8.1 13.4 %copy-start.4 = (bf16[256,256]{1,0:T(8,128)(2,1)S(1)}, bf16[256,256]{1,0:T(8,128)(2,1)}, u32[]{:S(2)}) copy-start(bf16[256,256]{1,0:T(8,128)(2,1)} %constant.105.clone.row1_ref) | copy-start | bytes 393220
  8.1 13.4 %copy-start.5 = (bf16[256,256]{1,0:T(8,128)(2,1)S(1)}, bf16[256,256]{1,0:T(8,128)(2,1)}, u32[]{:S(2)}) copy-start(bf16[256,256]{1,0:T(8,128)(2,1)} %constant.104.clone.row0_ref) | copy-start | bytes 393220
  8.1 13.4 %copy-start.6 = (s32[1,128,2]{1,2,0:T(2,128)S(1)}, s32[1,128,2]{1,2,0:T(2,128)}, u32[]{:S(2)}) copy-start(s32[1,128,2]{1,2,0:T(2,128)} %param.27) | copy-start | bytes 3076
  9.4 1.0 %copy-start.14 = (bf16[512,256]{1,0:T(8,128)(2,1)S(1)}, bf16[512,256]{1,0:T(8,128)(2,1)}, u32[]{:S(2)}) copy-start(bf16[512,256]{1,0:T(8,128)(2,1)} %constant.101.clone.win_ref) | copy-start | bytes 786436
  10.3 0.9 %copy-start.15 = (bf16[512,256]{1,0:T(8,128)(2,1)S(1)}, bf16[512,256]{1,0:T(8,128)(2,1)}, u32[]{:S(2)}) copy-start(bf16[512,256]{1,0:T(8,128)(2,1)} %constant.100.clone.sten_ref) | copy-start | bytes 786436
  15.4 1.3 %copy-start.18 = (f32[32,16,1024]{2,1,0:T(8,128)}, f32[32,16,1024]{2,1,0:T(8,128)S(1)}, u32[]{:S(2)}) copy-start(f32[32,16,1024]{2,1,0:T(8,128)S(1)} %get-tuple-element.9.base_ref) | copy-start | bytes 6291460
  26.8 1.0 %copy-start.10 = (bf16[512,1024]{1,0:T(8,128)(2,1)}, bf16[512,1024]{1,0:T(8,128)(2,1)S(1)}, u32[]{:S(2)}) copy-start(bf16[512,1024]{1,0:T(8,128)(2,1)S(1)} %get-tuple-element.12.ghosts_ref) | copy-start | bytes 3145732
  27.8 15.0 %copy-start.16 = (bf16[256,128]{1,0:T(8,128)(2,1)S(1)}, bf16[256,128]{1,0:T(8,128)(2,1)}, u32[]{:S(2)}) copy-start(bf16[256,128]{1,0:T(8,128)(2,1)} %constant.108.clone.row1_ref) | copy-start | bytes 196612
  27.8 15.0 %copy-start.17 = (bf16[256,128]{1,0:T(8,128)(2,1)S(1)}, bf16[256,128]{1,0:T(8,128)(2,1)}, u32[]{:S(2)}) copy-start(bf16[256,128]{1,0:T(8,128)(2,1)} %constant.107.clone.row0_ref) | copy-start | bytes 196612
  27.8 15.0 %copy-start.11 = (bf16[512,1024]{1,0:T(8,128)(2,1)S(1)}, bf16[512,1024]{1,0:T(8,128)(2,1)}, u32[]{:S(2)}) copy-start(bf16[512,1024]{1,0:T(8,128)(2,1)} %copy-done.10) | copy-start | bytes 3145732
  27.8 44.8 %all-to-all-start = ((f32[128,16,128]{2,1,0:T(8,128)}), f32[128,16,128]{2,1,0:T(8,128)S(1)}, u32[]{:S(2)}, u32[]{:S(2)}) async-start(f32[128,16,128]{2,1,0:T(8,128)} %get-tuple-element.13), calls=%async_computation | async-start | bytes 2097152 | tf_op jit(solution)/shard_map/all_to_all | solution.py:439
  42.9 1.2 %copy-start.13 = (bf16[512,1024]{1,0:T(8,128)(2,1)S(1)}, bf16[512,1024]{1,0:T(8,128)(2,1)}, u32[]{:S(2)}) copy-start(bf16[512,1024]{1,0:T(8,128)(2,1)} %constant.106.clone.col_ref) | copy-start | bytes 3145732
  44.1 1.6 %copy-start.19 = (f32[32,16,1024]{2,1,0:T(8,128)S(1)}, f32[32,16,1024]{2,1,0:T(8,128)}, u32[]{:S(2)}) copy-start(f32[32,16,1024]{2,1,0:T(8,128)} %copy-done.18) | copy-start | bytes 6291460
  45.7 27.0 %copy-start.1 = (bf16[256,1024]{1,0:T(8,128)(2,1)S(1)}, bf16[256,1024]{1,0:T(8,128)(2,1)}, u32[]{:S(2)}) copy-start(bf16[256,1024]{1,0:T(8,128)(2,1)} %constant.109.clone.table_ref) | copy-start | bytes 1572868
  45.7 27.0 %copy-start.7 = (s32[1,192]{1,0:T(1,128)S(1)}, s32[1,192]{1,0:T(1,128)}, u32[]{:S(2)}) copy-start(s32[1,192]{1,0:T(1,128)} %slot_ref.1) | copy-start | bytes 2308

commit v3 on v2

--- a/solution.py
+++ b/solution.py
@@ -1,3 +1,5 @@
+import functools
+
 import jax
 import jax.numpy as jnp
 import ml_dtypes
@@ -8,7 +10,8 @@
 from jax.sharding import PartitionSpec as P
 
 CHUNK = 8
-PACK = 16
+PACK = 128
+REFINE = (32, 32, 32, 32, 32, 32)
 VMEM_LIMIT = 24 * 1024 * 1024
 
 
@@ -105,7 +108,7 @@
     return jnp.dot(a, b, preferred_element_type=jnp.float32)
 
 
-def strips_kernel(state_ref, strips_ref, edge_ref, held, sems):
+def strips_kernel(state_ref, rows_ref, cols_ref, edge_ref, held, sems):
     slab = lax.axis_index("slab")
     count, lev = state_ref.shape[0], state_ref.shape[1]
     steps = count // CHUNK
@@ -127,9 +130,9 @@
         x = held[part]
         tail = x[:, :, 896:].reshape(rows, 128)
         tail = jnp.where((lane // 32) % 2 == 0, pltpu.roll(tail, 96, 1), pltpu.roll(tail, 32, 1))
-        strips_ref[part, 0] = jnp.where(lane < 64, x[:, :, :128].reshape(rows, 128), tail).reshape(CHUNK, lev, 128)
+        rows_ref[part] = jnp.where(lane < 64, x[:, :, :128].reshape(rows, 128), tail).reshape(CHUNK, lev, 128)
         high, low = split(x.reshape(rows, 1024))
-        strips_ref[part, 1] = (dot(high, pick) + dot(low, pick)).reshape(CHUNK, lev, 128)
+        cols_ref[part] = (dot(high, pick) + dot(low, pick)).reshape(CHUNK, lev, 128)
         edge_ref[part] = jnp.where(slab == 0, x[:, lev - 1, :], x[:, 0, :])
 
 
@@ -186,57 +189,61 @@
     lax.fori_loop(0, count // CHUNK, step, 0)
 
 
+def collect_strips(near_refs, near):
+    for i, ref in enumerate(near_refs):
+        near[i // 2, i % 2] = ref[...]
+
+
+def gather_ghosts(i, code_ref, a_row, a_col, near, ghosts_ref):
+    lev = near.shape[3]
+    half = lax.broadcasted_iota(jnp.int32, (lev, 128), 1) // 64
+    rows = CHUNK * lev
+    for s in range(4):
+        parts = []
+        for n in range(CHUNK):
+            code = code_ref[s, i * CHUNK + n]
+            x = near[(code >> 3) & 3, (code >> 2) & 1, code >> 5]
+            x = jnp.where((code & 2) == 0, x, pltpu.roll(x, 64, 1))
+            parts.append(jnp.where(half == (code & 1), x, 0.0))
+        x = jnp.stack(parts) * (a_row if s < 2 else a_col)
+        high, low = split(x.reshape(rows, 128))
+        ghosts_ref[:, s * 256 : s * 256 + 128] = high
+        ghosts_ref[:, s * 256 + 128 : s * 256 + 256] = low
+
+
 def pack_kernel(
     code_ref,
     send_ref,
     crow_ref,
     ccol_ref,
     base_ref,
-    prev_ref,
-    own_ref,
-    next_ref,
+    prev_rows,
+    prev_cols,
+    own_rows,
+    own_cols,
+    next_rows,
+    next_cols,
     col0_ref,
     col1_ref,
     row0_ref,
     row1_ref,
     pay_ref,
-    ghosts_ref,
     near,
     wins,
+    *ghosts,
 ):
-    count, lev = own_ref.shape[0], own_ref.shape[2]
-    near[0:count] = prev_ref[...]
-    near[count : 2 * count] = own_ref[...]
-    near[2 * count :] = next_ref[...]
+    count, lev = own_rows.shape[:2]
+    half = lax.broadcasted_iota(jnp.int32, (lev, 128), 1) // 64
+    collect_strips((prev_rows, prev_cols, own_rows, own_cols, next_rows, next_cols), near)
     a_row = levels_of(crow_ref, lev) * (1.0 / 12.0)
     a_col = levels_of(ccol_ref, lev) * (1.0 / 12.0)
-    half = lax.broadcasted_iota(jnp.int32, (lev, 128), 1) // 64
-    rows = CHUNK * lev
-
-    def gather(i, carry):
-        for s in range(4):
-            parts = []
-            for n in range(CHUNK):
-                code = code_ref[s, i * CHUNK + n]
-                x = near[code >> 3, (code >> 2) & 1]
-                x = jnp.where((code & 2) == 0, x, pltpu.roll(x, 64, 1))
-                parts.append(jnp.where(half == (code & 1), x, 0.0))
-            x = jnp.stack(parts) * (a_row if s < 2 else a_col)
-            high, low = split(x.reshape(rows, 128))
-            at = pl.ds(pl.multiple_of(i * rows, rows), rows)
-            ghosts_ref[at, s * 256 : s * 256 + 128] = high
-            ghosts_ref[at, s * 256 + 128 : s * 256 + 256] = low
-        return carry
-
-    lax.fori_loop(0, count // CHUNK, gather, 0)
-
-    def add(i, carry):
-        blocks = pl.ds(pl.multiple_of(i * CHUNK, CHUNK), CHUNK)
-        at = pl.ds(pl.multiple_of(i * rows, rows), rows)
-        row0 = dot(ghosts_ref[at, 0:256], row0_ref[...]).reshape(CHUNK, lev, 256)
-        row1 = dot(ghosts_ref[at, 256:512], row1_ref[...]).reshape(CHUNK, lev, 256)
+    for i, held in enumerate(ghosts):
+        gather_ghosts(i, code_ref, a_row, a_col, near, held)
+        blocks = slice(i * CHUNK, i * CHUNK + CHUNK)
+        row0 = dot(held[:, 0:256], row0_ref[...]).reshape(CHUNK, lev, 256)
+        row1 = dot(held[:, 256:512], row1_ref[...]).reshape(CHUNK, lev, 256)
         for h, col_ref in enumerate((col0_ref, col1_ref)):
-            c = dot(ghosts_ref[at, 512 + 256 * h : 768 + 256 * h], col_ref[...]).reshape(CHUNK, lev, 512)
+            c = dot(held[:, 512 + 256 * h : 768 + 256 * h], col_ref[...]).reshape(CHUNK, lev, 512)
             for j in range(4):
                 v = base_ref[blocks, 2 * j + h] + c[:, :, 128 * j : 128 * j + 128]
                 if j == 0:
@@ -244,9 +251,6 @@
                 if j == 3:
                     v = v + row1[:, :, 128 * h : 128 * h + 128]
                 wins[blocks, 2 * j + h] = v
-        return carry
-
-    lax.fori_loop(0, count // CHUNK, add, 0)
 
     def pack(d, carry):
         parts = []
@@ -260,43 +264,63 @@
     lax.fori_loop(0, pay_ref.shape[0], pack, 0, unroll=PACK)
 
 
-def finish_kernel(base_ref, ghosts_ref, col_ref, row0_ref, row1_ref, out_ref):
-    blocks, lev = base_ref.shape[0], base_ref.shape[1]
-    c = dot(ghosts_ref[:, 512:1024], col_ref[...]).reshape(blocks, lev, 1024)
+def finish_kernel(
+    code_ref,
+    crow_ref,
+    ccol_ref,
+    base_ref,
+    prev_rows,
+    prev_cols,
+    own_rows,
+    own_cols,
+    next_rows,
+    next_cols,
+    col_ref,
+    row0_ref,
+    row1_ref,
+    out_ref,
+    near,
+    held,
+):
+    lev = own_rows.shape[1]
+    blocks = base_ref.shape[0]
+    i = pl.program_id(0)
+
+    @pl.when(i == 0)
+    def _():
+        collect_strips((prev_rows, prev_cols, own_rows, own_cols, next_rows, next_cols), near)
+
+    a_row = levels_of(crow_ref, lev) * (1.0 / 12.0)
+    a_col = levels_of(ccol_ref, lev) * (1.0 / 12.0)
+    gather_ghosts(i, code_ref, a_row, a_col, near, held)
+    c = dot(held[:, 512:1024], col_ref[...]).reshape(blocks, lev, 1024)
     out_ref[...] = base_ref[...] + c
-    out_ref[:, :, :128] += dot(ghosts_ref[:, 0:256], row0_ref[...]).reshape(blocks, lev, 128)
-    out_ref[:, :, 896:] += dot(ghosts_ref[:, 256:512], row1_ref[...]).reshape(blocks, lev, 128)
-
-
-def refine_kernel(slot_ref, count_ref, recv_ref, table_ref, out_ref, parents, held, sems):
+    out_ref[:, :, :128] += dot(held[:, 0:256], row0_ref[...]).reshape(blocks, lev, 128)
+    out_ref[:, :, 896:] += dot(held[:, 256:512], row1_ref[...]).reshape(blocks, lev, 128)
+
+
+def refine_kernel(sizes, slot_ref, count_ref, recv_ref, table_ref, out_ref, held, sems, *parents):
     lev = recv_ref.shape[1]
-    steps = sems.shape[0]
-    size = out_ref.shape[0] // steps
     half = lax.broadcasted_iota(jnp.int32, (lev, 128), 1) // 64
     live = count_ref[0]
-
-    def copy(i):
-        part = pl.ds(i * size, size)
-        return pltpu.make_async_copy(held.at[part], out_ref.at[part], sems.at[i])
-
-    def step(i, carry):
-        start = i * size
-        for f in range(size):
-            slot = slot_ref[0, start + f]
+    copies, start = [], 0
+    for i, size in enumerate(sizes):
+        for n in range(size):
+            slot = slot_ref[0, start + n]
             x = recv_ref[slot >> 1]
             x = jnp.where(half == (slot & 1), x, pltpu.roll(x, 64, 1))
-            x = jnp.where(start + f < live, x, 0.0)
+            x = jnp.where(start + n < live, x, 0.0)
             high, low = split(x)
-            parents[f * lev : (f + 1) * lev, :128] = high
-            parents[f * lev : (f + 1) * lev, 128:] = low
-        fine = dot(parents[...], table_ref[...])
-        held[pl.ds(start, size)] = fine.astype(jnp.bfloat16).reshape(size, lev, 1024)
-        copy(i).start()
-        return carry
-
-    lax.fori_loop(0, steps, step, 0)
-    for i in range(steps):
-        copy(i).wait()
+            parents[i][n * lev : (n + 1) * lev, :128] = high
+            parents[i][n * lev : (n + 1) * lev, 128:] = low
+        part = pl.ds(start, size)
+        fine = dot(parents[i][...], table_ref[...])
+        held[part] = fine.astype(jnp.bfloat16).reshape(size, lev, 1024)
+        copies.append(pltpu.make_async_copy(held.at[part], out_ref.at[part], sems.at[i]))
+        copies[i].start()
+        start += size
+    for copy in copies:
+        copy.wait()
 
 
 VMEM = pl.BlockSpec(memory_space=pltpu.VMEM)
@@ -311,14 +335,12 @@
 
 def make_strips(state):
     count, lev = state.shape[:2]
+    strip = jax.ShapeDtypeStruct((count, lev, 128), jnp.float32)
     return pl.pallas_call(
         strips_kernel,
-        out_shape=(
-            jax.ShapeDtypeStruct((count, 2, lev, 128), jnp.float32),
-            jax.ShapeDtypeStruct((count, 1024), jnp.float32),
-        ),
+        out_shape=(strip, strip, jax.ShapeDtypeStruct((count, 1024), jnp.float32)),
         in_specs=[HBM],
-        out_specs=(VMEM, VMEM),
+        out_specs=(VMEM, VMEM, VMEM),
         scratch_shapes=[pltpu.VMEM(state.shape, jnp.float32), pltpu.SemaphoreType.DMA((count // CHUNK,))],
         compiler_params=PARAMS,
         name="strips",
@@ -330,7 +352,7 @@
     return pl.pallas_call(
         local_kernel,
         out_shape=(
-            jax.ShapeDtypeStruct(state.shape, jnp.float32),
+            pltpu.HBM(state.shape, jnp.float32),
             jax.ShapeDtypeStruct((count, 8, lev, 128), jnp.float32),
         ),
         in_specs=[SMEM] * 3 + [VMEM] * 4,
@@ -348,15 +370,13 @@
     maps = cols + [sides[0][:, :256], sides[1][:, 768:]]
     return pl.pallas_call(
         pack_kernel,
-        out_shape=(
-            jax.ShapeDtypeStruct((send.shape[1], lev, 128), jnp.float32),
-            jax.ShapeDtypeStruct((count * lev, 1024), jnp.bfloat16),
-        ),
-        in_specs=[SMEM] * 4 + [VMEM] * 8,
-        out_specs=(VMEM, VMEM),
+        out_shape=jax.ShapeDtypeStruct((send.shape[1], lev, 128), jnp.float32),
+        in_specs=[SMEM] * 4 + [VMEM] * 11,
+        out_specs=VMEM,
         scratch_shapes=[
-            pltpu.VMEM((3 * count, 2, lev, 128), jnp.float32),
+            pltpu.VMEM((3, 2, count, lev, 128), jnp.float32),
             pltpu.VMEM((count, 8, lev, 128), jnp.float32),
+            *[pltpu.VMEM((CHUNK * lev, 1024), jnp.bfloat16)] * (count // CHUNK),
         ],
         compiler_params=PARAMS,
         cost_estimate=cost(10**9, 8 * 10**6),
@@ -364,40 +384,42 @@
     )(code, send, *coefs[:2], base, *nearby, *[jnp.asarray(m) for m in maps])
 
 
-def make_advanced(base, ghosts):
+def make_advanced(code, coefs, base, nearby):
     count, lev = base.shape[:2]
     maps = [np.concatenate([ghost_map(2), ghost_map(3)], 0), ghost_map(0)[:, :128], ghost_map(1)[:, 896:]]
+    block = pl.BlockSpec((CHUNK, lev, 1024), lambda i: (i, 0, 0))
     return pl.pallas_call(
         finish_kernel,
         grid=(count // CHUNK,),
         out_shape=jax.ShapeDtypeStruct(base.shape, jnp.float32),
-        in_specs=[
-            pl.BlockSpec((CHUNK, lev, 1024), lambda i: (i, 0, 0)),
-            pl.BlockSpec((CHUNK * lev, 1024), lambda i: (i, 0)),
-            VMEM,
-            VMEM,
-            VMEM,
+        in_specs=[SMEM] * 3 + [block] + [VMEM] * 9,
+        out_specs=block,
+        scratch_shapes=[
+            pltpu.VMEM((3, 2, count, lev, 128), jnp.float32),
+            pltpu.VMEM((CHUNK * lev, 1024), jnp.bfloat16),
         ],
-        out_specs=pl.BlockSpec((CHUNK, lev, 1024), lambda i: (i, 0, 0)),
         compiler_params=PARAMS,
         cost_estimate=cost(2 * 10**9, 8 * 10**6),
         name="finish",
-    )(base, ghosts, *[jnp.asarray(m) for m in maps])
+    )(code, *coefs[:2], base, *nearby, *[jnp.asarray(m) for m in maps])
 
 
 def make_refined(slots, live, received):
     fine = slots.shape[1]
     lev = received.shape[1]
-    size = next(n for n in (24, 16, 8, 6, 4, 2, 1) if fine % n == 0)
+    sizes = []
+    for size in REFINE + (fine,) * fine:
+        if sum(sizes) < fine:
+            sizes.append(min(size, fine - sum(sizes)))
     return pl.pallas_call(
-        refine_kernel,
+        functools.partial(refine_kernel, tuple(sizes)),
         out_shape=jax.ShapeDtypeStruct((fine, lev, 1024), jnp.bfloat16),
         in_specs=[SMEM, SMEM, VMEM, VMEM],
         out_specs=HBM,
         scratch_shapes=[
-            pltpu.VMEM((size * lev, 256), jnp.bfloat16),
             pltpu.VMEM((fine, lev, 1024), jnp.bfloat16),
-            pltpu.SemaphoreType.DMA((fine // size,)),
+            pltpu.SemaphoreType.DMA((len(sizes),)),
+            *[pltpu.VMEM((size * lev, 256), jnp.bfloat16) for size in sizes],
         ],
         compiler_params=PARAMS,
         name="refine",
@@ -406,10 +428,9 @@
 
 def ghost_codes(nbr_block, nbr_side, nbr_flip, count, peers, here):
     rel = (nbr_block // count - here + 1 + peers) % peers
-    rel = jnp.where(here % 2 == 0, 2 - rel, rel)
+    rel = jnp.where(here % 2 == 0, rel, 2 - rel)
     swap = (nbr_side % 2) ^ nbr_flip
-    near = rel * count + nbr_block % count
-    return near * 8 + (nbr_side // 2) * 4 + swap * 2 + nbr_flip
+    return nbr_block % count * 32 + rel * 8 + nbr_side // 2 * 4 + swap * 2 + nbr_flip
 
 
 def body(
@@ -426,18 +447,19 @@
 ):
     peers = lax.axis_size("blocks")
     here = lax.axis_index("blocks")
-    strips, edge = make_strips(state)
-    first = [(i, i ^ 1) for i in range(peers)]
-    second = [(i, (i + (1 if i % 2 else -1)) % peers) for i in range(peers)]
-    before = lax.ppermute(strips, "blocks", first)
-    after = lax.ppermute(strips, "blocks", second)
+    rows, cols, edge = make_strips(state)
+    first = [(i, (i + (1 if i % 2 else -1)) % peers) for i in range(peers)]
+    second = [(i, i ^ 1) for i in range(peers)]
+    other = [lax.ppermute(s, "blocks", first) for s in (rows, cols)]
+    after = [lax.ppermute(s, "blocks", second) for s in (rows, cols)]
+    nearby = (*other, rows, cols, *after)
     edge = lax.ppermute(edge, "slab", [(0, 1), (1, 0)])
     coefs = (courant_row, courant_col, mixing)
     base, wins = make_local(coefs, state, edge)
     code = ghost_codes(nbr_block.T, nbr_side.T, nbr_flip.T, state.shape[0], peers, here)
-    payload, ghosts = make_payload(code, send_idx[0].T, coefs, wins, (before, strips, after))
+    payload = make_payload(code, send_idx[0].T, coefs, wins, nearby)
     received = lax.all_to_all(payload, "blocks", split_axis=0, concat_axis=0, tiled=True)
-    advanced = make_advanced(base, ghosts)
+    advanced = make_advanced(code, coefs, base, nearby)
     return advanced, make_refined(fine_slot, fine_count, received)
 
 

time: 77.9 us -> 74.9 us (0.961)
  waiting for transfers between devices: 30.3 us -> 25.6 us
  starting transfers between devices: 19.2 us -> 21.9 us
  local copies, waits for them, and re-layouts: 7.09 us -> 4.77 us
    ppermute x2 -> x4, starting transfers between devices: 4.85 us -> 7.83 us  [the longest x2 6.24 us: body(): other = [lax.ppermute(s, 'blocks', first) for s in (rows, cols)]]
    ppermute x2 -> x4, waiting for transfers between devices: 4.79 us -> 2.33 us  [the longest x2 2.33 us: body(): other = [lax.ppermute(s, 'blocks', first) for s in (rows, cols)]]
    unnamed x46 -> x34, local copies, waits for them, and re-layouts: 7.09 us -> 4.77 us
    all_to_all x1, waiting for transfers between devices: 24.3 us -> 22.6 us  [body(): lax.all_to_all(payload, 'blocks', split_axis=0, concat_axis=0, tiled=True)]
    pallas_call x1, Pallas kernels: 2.67 us -> 4.11 us  [make_advanced(): pl.pallas_call(finish_kernel, grid=(count // CHUNK,), out_shape=jax.Shape...]
    pallas_call x4, Pallas kernels: 16.8 us -> 15.9 us  [the longest x1 5.72 us: make_local(): pl.pallas_call(local_kernel, out_shape=(pltpu.HBM(state.shape, jnp.float3...]
  transfers between devices with their start and end apart: 4 -> 6, of which waited for: 4 -> 3; matrix products, arithmetic and copies ran while one was open for 0% -> 1% of each run, Pallas kernels for 9% -> 13%
where the time goes in v3:
time: 74.9 us; the launch traced here: 74.4 us
  waiting for transfers between devices  25.6 us (34%)
  starting transfers between devices  21.9 us (29%)
  Pallas kernels  20 us (27%)
  local copies, waits for them, and re-layouts  4.77 us (6%)
  between operations  1.45 us (2%)
    all_to_all x1, waiting for transfers between devices, body(): lax.all_to_all(payload, 'blocks', split_axis=0, concat_axis=0, tiled=True)  22.6 us
    all_to_all x1, starting transfers between devices, body(): lax.all_to_all(payload, 'blocks', split_axis=0, concat_axis=0, tiled=True)  14 us
    ppermute x2, starting transfers between devices, body(): other = [lax.ppermute(s, 'blocks', first) for s in (rows, cols)]  6.24 us
    pallas_call x1, Pallas kernels, make_local(): pl.pallas_call(local_kernel, out_shape=(pltpu.HBM(state.shape, jnp.float3...  5.72 us
    unnamed x34, local copies, waits for them, and re-layouts  4.77 us
    pallas_call x1, Pallas kernels, make_advanced(): pl.pallas_call(finish_kernel, grid=(count // CHUNK,), out_shape=jax.Shape...  4.11 us
    pallas_call x1, Pallas kernels, make_payload(): pl.pallas_call(pack_kernel, out_shape=jax.ShapeDtypeStruct((send.shape[1]...  4 us
    pallas_call x1, Pallas kernels, make_refined(): pl.pallas_call(functools.partial(refine_kernel, tuple(sizes)), out_shape=...  3.76 us
  transfers between devices with their start and end apart: 6, of which 3 were waited for; matrix products, arithmetic and copies ran while one was open for 1% of the time, Pallas kernels for 13%

profile of v3, /device:TPU:32, one launch (start us, length us, event | category | flops | bytes accessed | tf_op | source)
XLA Modules:
  0.0 74.4 jit_solution(9532624567278683504)
XLA Ops:
  0.6 0.0 copy-start
  0.6 0.0 copy-start.9
  0.7 0.0 copy-start.8
  0.7 0.0 copy-start.10
  0.7 2.5 %strips.1 = (f32[32,16,128]{2,1,0:T(8,128)S(1)}, f32[32,16,128]{2,1,0:T(8,128)S(1)}, f32[32,1024]{1,0:T(8,128)S(1)}) custom-call(f32[32,16,1024]{2,1,0:T(8,128)} %state_ref.3), custom_call_target="tpu_custom_call" | custom-call | tf_op jit(solution)/shard_map/strips/pallas_call | solution.py:339
  3.1 1.6 %collective-permute-start.3 = (f32[32,16,128]{2,1,0:T(8,128)S(1)}, f32[32,16,128]{2,1,0:T(8,128)S(1)}, u32[]{:S(2)}, u32[]{:S(2)}) collective-permute-start(f32[32,16,128]{2,1,0:T(8,128)S(1)} %get-tuple-element.9.own_rows), channel_id=1, source_target_pairs={{0,2},{2,0},{4,6},{6,4},{8,10},{10,8},{12,14},{14,12},{16,18},{18,... | collective-permute-start | bytes 786440 | tf_op jit(solution)/shard_map/ppermute | solution.py:454
  4.7 4.1 %collective-permute-start.1 = (f32[32,16,128]{2,1,0:T(8,128)S(1)}, f32[32,16,128]{2,1,0:T(8,128)S(1)}, u32[]{:S(2)}, u32[]{:S(2)}) collective-permute-start(f32[32,16,128]{2,1,0:T(8,128)S(1)} %get-tuple-element.9.own_rows), channel_id=1, source_target_pairs={{0,254},{2,4},{4,2},{6,8},{8,6},{10,12},{12,10},{14,16},{16,14},{1... | collective-permute-start | bytes 786440 | tf_op jit(solution)/shard_map/ppermute | solution.py:453
  8.8 0.0 collective-permute-start.4
  8.8 2.2 %collective-permute-start.2 = (f32[32,16,128]{2,1,0:T(8,128)S(1)}, f32[32,16,128]{2,1,0:T(8,128)}, u32[]{:S(2)}, u32[]{:S(2)}) collective-permute-start(f32[32,16,128]{2,1,0:T(8,128)S(1)} %get-tuple-element.10.own_cols), channel_id=1, source_target_pairs={{0,254},{2,4},{4,2},{6,8},{8,6},{10,12},{12,10},{14,16},{16,14},{1... | collective-permute-start | bytes 786440 | tf_op jit(solution)/shard_map/ppermute | solution.py:453
  11.0 0.0 collective-permute-start
  11.0 0.7 fusion.4.code_ref
  11.7 0.0 copy-start.2
  11.7 0.0 copy-start.3
  11.7 0.0 copy-start.4
  11.7 0.0 copy-start.5
  11.8 0.0 copy-start.6
  11.8 0.7 collective-permute-done.edge_ref
  12.4 0.0 copy-done
  12.4 0.0 copy-done.9
  12.4 0.0 copy-done.8
  12.5 0.0 copy-done.10
  12.5 0.0 copy-start.12
  12.5 0.9 %copy-done.12 = bf16[512,256]{1,0:T(8,128)(2,1)S(1)} copy-done((bf16[512,256]{1,0:T(8,128)(2,1)S(1)}, bf16[512,256]{1,0:T(8,128)(2,1)}, u32[]{:S(2)}) %copy-start.12) | copy-done | bytes 262168
  13.4 0.0 copy-start.13
  13.4 0.9 %copy-done.13 = bf16[512,256]{1,0:T(8,128)(2,1)S(1)} copy-done((bf16[512,256]{1,0:T(8,128)(2,1)S(1)}, bf16[512,256]{1,0:T(8,128)(2,1)}, u32[]{:S(2)}) %copy-start.13) | copy-done | bytes 262168
  14.4 5.7 %local.1 = (f32[32,16,1024]{2,1,0:T(8,128)}, f32[32,8,16,128]{3,2,1,0:T(8,128)S(1)}) custom-call(f32[16]{0:T(128)S(1)} %copy-done.8, f32[16]{0:T(128)S(1)} %copy-done.9, f32[16]{0:T(128)S(1)} %copy-done.10, f32[32,16,1024]{2,1,0:T(8,128)S(1)} %copy-done, f32[32,1024]{1,0:T(8,128)} %collective-permute-done.edge_ref, bf16[512,256]{1,0:T(8,128)(2,1)S(1)} %copy-done.13, ...), custom_call_target="tpu_custom_call" | custom-call | flops 4000000000 | bytes 8000000 | tf_op jit(solution)/shard_map/local/pallas_call | solution.py:352
  20.1 0.0 collective-permute-done.3.next_rows
  20.1 0.0 collective-permute-done.1.prev_rows
  20.1 0.0 collective-permute-done.4.next_cols
  20.1 2.3 %collective-permute-done.2.prev_cols = f32[32,16,128]{2,1,0:T(8,128)} collective-permute-done((f32[32,16,128]{2,1,0:T(8,128)S(1)}, f32[32,16,128]{2,1,0:T(8,128)}, u32[]{:S(2)}, u32[]{:S(2)}) %collective-permute-start.2) | collective-permute-done | bytes 262176 | tf_op jit(solution)/shard_map/ppermute | solution.py:453
  22.4 0.0 copy-done.2
  22.4 0.0 copy-done.3
  22.4 0.0 copy-done.4
  22.4 0.0 copy-done.5
  22.4 0.0 copy-done.6
  22.5 4.0 %pack.1 = f32[128,16,128]{2,1,0:T(8,128)} custom-call(s32[4,32]{1,0:T(4,128)S(1)} %fusion.4.code_ref, s32[2,128]{1,0:T(2,128)S(1)} %bitcast.39, f32[16]{0:T(128)S(1)} %copy-done.8, f32[16]{0:T(128)S(1)} %copy-done.9, f32[32,8,16,128]{3,2,1,0:T(8,128)S(1)} %get-tuple-element.11.base_ref, f32[32,16,128]{2,1,0:T(8,128)S(1)} %collective-permute-done.1.prev_rows, ...), custom_call_target="tpu_custom_call" | custom-call | flops 1000000000 | bytes 8000000 | tf_op jit(solution)/shard_map/pack/pallas_call | solution.py:371
  26.5 0.0 copy-start.14
  26.5 14.0 %all-to-all-start = ((f32[128,16,128]{2,1,0:T(8,128)}), f32[128,16,128]{2,1,0:T(8,128)S(1)}, u32[]{:S(2)}, u32[]{:S(2)}) async-start(f32[128,16,128]{2,1,0:T(8,128)} %pack.1), calls=%async_computation | async-start | bytes 2097152 | tf_op jit(solution)/shard_map/all_to_all | solution.py:461
  41.2 0.0 copy-done.14
  41.2 0.0 copy-done.15
  41.2 0.0 copy-start.11
  41.2 1.2 %copy-done.11 = bf16[512,1024]{1,0:T(8,128)(2,1)S(1)} copy-done((bf16[512,1024]{1,0:T(8,128)(2,1)S(1)}, bf16[512,1024]{1,0:T(8,128)(2,1)}, u32[]{:S(2)}) %copy-start.11) | copy-done | bytes 1048600
  42.4 1.6 %copy-done.16 = f32[32,16,1024]{2,1,0:T(8,128)S(1)} copy-done((f32[32,16,1024]{2,1,0:T(8,128)S(1)}, f32[32,16,1024]{2,1,0:T(8,128)}, u32[]{:S(2)}) %copy-start.16) | copy-done | bytes 2097176
  44.0 4.1 %finish.1 = f32[32,16,1024]{2,1,0:T(8,128)} custom-call(s32[4,32]{1,0:T(4,128)S(1)} %fusion.4.code_ref, f32[16]{0:T(128)S(1)} %copy-done.8, f32[16]{0:T(128)S(1)} %copy-done.9, f32[32,16,1024]{2,1,0:T(8,128)S(1)} %copy-done.16, f32[32,16,128]{2,1,0:T(8,128)S(1)} %collective-permute-done.1.prev_rows, f32[32,16,128]{2,1,0:T(8,128)} %collective-permute-done.2.prev_cols, ...), custom_call_target="tpu_custom_call" | custom-call | flops 2000000000 | bytes 8000000 | tf_op jit(solution)/shard_map/finish/pallas_call | solution.py:391
  48.1 22.6 %all-to-all-done.recv_ref = f32[128,16,128]{2,1,0:T(8,128)S(1)} async-done(((f32[128,16,128]{2,1,0:T(8,128)}), f32[128,16,128]{2,1,0:T(8,128)S(1)}, u32[]{:S(2)}, u32[]{:S(2)}) %all-to-all-start) | async-done | bytes 1048608 | tf_op jit(solution)/shard_map/all_to_all | solution.py:461
  70.7 0.0 copy-done.1
  70.7 0.0 copy-done.7
  70.7 3.8 %refine.1 = bf16[192,16,1024]{2,1,0:T(8,128)(2,1)} custom-call(s32[1,192]{1,0:T(1,128)S(1)} %copy-done.7, s32[1]{0:T(128)S(6)} %copy.22.count_ref, f32[128,16,128]{2,1,0:T(8,128)S(1)} %all-to-all-done.recv_ref, bf16[256,1024]{1,0:T(8,128)(2,1)S(1)} %copy-done.1), custom_call_target="tpu_custom_call" | custom-call | tf_op jit(solution)/shard_map/refine/pallas_call | solution.py:414
  (4 shorter events, 0.0 us)
Async XLA Ops:
  0.6 11.8 %copy-start = (f32[32,16,1024]{2,1,0:T(8,128)S(1)}, f32[32,16,1024]{2,1,0:T(8,128)}, u32[]{:S(2)}) copy-start(f32[32,16,1024]{2,1,0:T(8,128)} %state_ref.3) | copy-start | bytes 6291460
  0.6 11.8 %copy-start.9 = (f32[16]{0:T(128)S(1)}, f32[16]{0:T(128)}, u32[]{:S(2)}) copy-start(f32[16]{0:T(128)} %ccol_ref.5) | copy-start | bytes 196
  0.7 11.8 %copy-start.8 = (f32[16]{0:T(128)S(1)}, f32[16]{0:T(128)}, u32[]{:S(2)}) copy-start(f32[16]{0:T(128)} %crow_ref.5) | copy-start | bytes 196
  0.7 11.8 %copy-start.10 = (f32[16]{0:T(128)S(1)}, f32[16]{0:T(128)}, u32[]{:S(2)}) copy-start(f32[16]{0:T(128)} %mix_ref.1) | copy-start | bytes 196
  3.1 17.0 %collective-permute-start.3 = (f32[32,16,128]{2,1,0:T(8,128)S(1)}, f32[32,16,128]{2,1,0:T(8,128)S(1)}, u32[]{:S(2)}, u32[]{:S(2)}) collective-permute-start(f32[32,16,128]{2,1,0:T(8,128)S(1)} %get-tuple-element.9.own_rows), channel_id=1, source_target_pairs={{0,2},{2,0},{4,6},{6,4},{8,10},{10,8},{12,14},{14,12},{16,18},{18,... | collective-permute-start | bytes 786440 | tf_op jit(solution)/shard_map/ppermute | solution.py:454
  4.7 15.4 %collective-permute-start.1 = (f32[32,16,128]{2,1,0:T(8,128)S(1)}, f32[32,16,128]{2,1,0:T(8,128)S(1)}, u32[]{:S(2)}, u32[]{:S(2)}) collective-permute-start(f32[32,16,128]{2,1,0:T(8,128)S(1)} %get-tuple-element.9.own_rows), channel_id=1, source_target_pairs={{0,254},{2,4},{4,2},{6,8},{8,6},{10,12},{12,10},{14,16},{16,14},{1... | collective-permute-start | bytes 786440 | tf_op jit(solution)/shard_map/ppermute | solution.py:453
  8.8 11.3 %collective-permute-start.4 = (f32[32,16,128]{2,1,0:T(8,128)S(1)}, f32[32,16,128]{2,1,0:T(8,128)S(1)}, u32[]{:S(2)}, u32[]{:S(2)}) collective-permute-start(f32[32,16,128]{2,1,0:T(8,128)S(1)} %get-tuple-element.10.own_cols), channel_id=1, source_target_pairs={{0,2},{2,0},{4,6},{6,4},{8,10},{10,8},{12,14},{14,12},{16,18},{18,... | collective-permute-start | bytes 786440 | tf_op jit(solution)/shard_map/ppermute | solution.py:454
  8.8 13.6 %collective-permute-start.2 = (f32[32,16,128]{2,1,0:T(8,128)S(1)}, f32[32,16,128]{2,1,0:T(8,128)}, u32[]{:S(2)}, u32[]{:S(2)}) collective-permute-start(f32[32,16,128]{2,1,0:T(8,128)S(1)} %get-tuple-element.10.own_cols), channel_id=1, source_target_pairs={{0,254},{2,4},{4,2},{6,8},{8,6},{10,12},{12,10},{14,16},{16,14},{1... | collective-permute-start | bytes 786440 | tf_op jit(solution)/shard_map/ppermute | solution.py:453
  11.0 1.5 %collective-permute-start = (f32[32,1024]{1,0:T(8,128)S(1)}, f32[32,1024]{1,0:T(8,128)}, u32[]{:S(2)}, u32[]{:S(2)}) collective-permute-start(f32[32,1024]{1,0:T(8,128)S(1)} %get-tuple-element.7), channel_id=1, source_target_pairs={{0,1},{1,0},{2,3},{3,2},{4,5},{5,4},{6,7},{7,6},{8,9},{9,8},{10,11... | collective-permute-start | bytes 393224 | tf_op jit(solution)/shard_map/ppermute | solution.py:456
  11.7 10.7 %copy-start.2 = (bf16[256,512]{1,0:T(8,128)(2,1)S(1)}, bf16[256,512]{1,0:T(8,128)(2,1)}, u32[]{:S(2)}) copy-start(bf16[256,512]{1,0:T(8,128)(2,1)} %constant.103.clone.col1_ref) | copy-start | bytes 786436
  11.7 10.7 %copy-start.3 = (bf16[256,512]{1,0:T(8,128)(2,1)S(1)}, bf16[256,512]{1,0:T(8,128)(2,1)}, u32[]{:S(2)}) copy-start(bf16[256,512]{1,0:T(8,128)(2,1)} %constant.102.clone.col0_ref) | copy-start | bytes 786436
  11.7 10.7 %copy-start.4 = (bf16[256,256]{1,0:T(8,128)(2,1)S(1)}, bf16[256,256]{1,0:T(8,128)(2,1)}, u32[]{:S(2)}) copy-start(bf16[256,256]{1,0:T(8,128)(2,1)} %constant.105.clone.row1_ref) | copy-start | bytes 393220
  11.7 10.7 %copy-start.5 = (bf16[256,256]{1,0:T(8,128)(2,1)S(1)}, bf16[256,256]{1,0:T(8,128)(2,1)}, u32[]{:S(2)}) copy-start(bf16[256,256]{1,0:T(8,128)(2,1)} %constant.104.clone.row0_ref) | copy-start | bytes 393220
  11.8 10.7 %copy-start.6 = (s32[1,128,2]{1,2,0:T(2,128)S(1)}, s32[1,128,2]{1,2,0:T(2,128)}, u32[]{:S(2)}) copy-start(s32[1,128,2]{1,2,0:T(2,128)} %param.27) | copy-start | bytes 3076
  12.5 1.0 %copy-start.12 = (bf16[512,256]{1,0:T(8,128)(2,1)S(1)}, bf16[512,256]{1,0:T(8,128)(2,1)}, u32[]{:S(2)}) copy-start(bf16[512,256]{1,0:T(8,128)(2,1)} %constant.101.clone.win_ref) | copy-start | bytes 786436
  13.4 0.9 %copy-start.13 = (bf16[512,256]{1,0:T(8,128)(2,1)S(1)}, bf16[512,256]{1,0:T(8,128)(2,1)}, u32[]{:S(2)}) copy-start(bf16[512,256]{1,0:T(8,128)(2,1)} %constant.100.clone.sten_ref) | copy-start | bytes 786436
  26.5 14.7 %copy-start.14 = (bf16[256,128]{1,0:T(8,128)(2,1)S(1)}, bf16[256,128]{1,0:T(8,128)(2,1)}, u32[]{:S(2)}) copy-start(bf16[256,128]{1,0:T(8,128)(2,1)} %constant.108.clone.row1_ref) | copy-start | bytes 196612
  26.5 14.7 %copy-start.15 = (bf16[256,128]{1,0:T(8,128)(2,1)S(1)}, bf16[256,128]{1,0:T(8,128)(2,1)}, u32[]{:S(2)}) copy-start(bf16[256,128]{1,0:T(8,128)(2,1)} %constant.107.clone.row0_ref) | copy-start | bytes 196612
  26.5 44.2 %all-to-all-start = ((f32[128,16,128]{2,1,0:T(8,128)}), f32[128,16,128]{2,1,0:T(8,128)S(1)}, u32[]{:S(2)}, u32[]{:S(2)}) async-start(f32[128,16,128]{2,1,0:T(8,128)} %pack.1), calls=%async_computation | async-start | bytes 2097152 | tf_op jit(solution)/shard_map/all_to_all | solution.py:461
  41.2 1.2 %copy-start.11 = (bf16[512,1024]{1,0:T(8,128)(2,1)S(1)}, bf16[512,1024]{1,0:T(8,128)(2,1)}, u32[]{:S(2)}) copy-start(bf16[512,1024]{1,0:T(8,128)(2,1)} %constant.106.clone.col_ref) | copy-start | bytes 3145732
  42.4 1.6 %copy-start.16 = (f32[32,16,1024]{2,1,0:T(8,128)S(1)}, f32[32,16,1024]{2,1,0:T(8,128)}, u32[]{:S(2)}) copy-start(f32[32,16,1024]{2,1,0:T(8,128)} %get-tuple-element.8.base_ref) | copy-start | bytes 6291460
  44.0 26.7 %copy-start.1 = (bf16[256,1024]{1,0:T(8,128)(2,1)S(1)}, bf16[256,1024]{1,0:T(8,128)(2,1)}, u32[]{:S(2)}) copy-start(bf16[256,1024]{1,0:T(8,128)(2,1)} %constant.109.clone.table_ref) | copy-start | bytes 1572868
  44.0 26.7 %copy-start.7 = (s32[1,192]{1,0:T(1,128)S(1)}, s32[1,192]{1,0:T(1,128)}, u32[]{:S(2)}) copy-start(s32[1,192]{1,0:T(1,128)} %slot_ref.1) | copy-start | bytes 2308

commit v4 on v3

--- a/solution.py
+++ b/solution.py
@@ -10,7 +10,6 @@
 from jax.sharding import PartitionSpec as P
 
 CHUNK = 8
-PACK = 128
 REFINE = (32, 32, 32, 32, 32, 32)
 VMEM_LIMIT = 24 * 1024 * 1024
 
@@ -108,31 +107,36 @@
     return jnp.dot(a, b, preferred_element_type=jnp.float32)
 
 
-def strips_kernel(state_ref, rows_ref, cols_ref, edge_ref, held, sems):
+def rows_kernel(state_ref, rows_ref, held, sems):
+    count, lev = state_ref.shape[0], state_ref.shape[1]
+    copies = []
+    for i in range(4):
+        part = pl.ds(i // 2 * (count // 2), count // 2)
+        lanes = pl.ds(i % 2 * 896, 128)
+        copies.append(pltpu.make_async_copy(state_ref.at[part, :, lanes], held.at[i % 2, part], sems.at[i]))
+        copies[i].start()
+    for copy in copies:
+        copy.wait()
+    lane = lax.broadcasted_iota(jnp.int32, (count * lev, 128), 1)
+    tail = held[1].reshape(count * lev, 128)
+    tail = jnp.where((lane // 32) % 2 == 0, pltpu.roll(tail, 96, 1), pltpu.roll(tail, 32, 1))
+    rows_ref[...] = jnp.where(lane < 64, held[0].reshape(count * lev, 128), tail).reshape(count, lev, 128)
+
+
+def cols_kernel(state_ref, cols_ref, edge_ref):
     slab = lax.axis_index("slab")
     count, lev = state_ref.shape[0], state_ref.shape[1]
-    steps = count // CHUNK
-    copies = []
-    for i in range(steps):
-        part = pl.ds(i * CHUNK, CHUNK)
-        copies.append(pltpu.make_async_copy(state_ref.at[part], held.at[part], sems.at[i]))
-        copies[i].start()
     cell = lax.broadcasted_iota(jnp.int32, (1024, 128), 0)
     to = lax.broadcasted_iota(jnp.int32, (1024, 128), 1)
     line = to // 32
     line = jnp.where(line < 2, line, 33 - line)
     pick = jnp.where((cell // 32 == to % 32) & (cell % 32 == line), 1.0, 0.0).astype(jnp.bfloat16)
-    rows = CHUNK * lev
-    lane = lax.broadcasted_iota(jnp.int32, (rows, 128), 1)
-    for i in range(steps):
-        copies[i].wait()
-        part = slice(i * CHUNK, i * CHUNK + CHUNK)
-        x = held[part]
-        tail = x[:, :, 896:].reshape(rows, 128)
-        tail = jnp.where((lane // 32) % 2 == 0, pltpu.roll(tail, 96, 1), pltpu.roll(tail, 32, 1))
-        rows_ref[part] = jnp.where(lane < 64, x[:, :, :128].reshape(rows, 128), tail).reshape(CHUNK, lev, 128)
-        high, low = split(x.reshape(rows, 1024))
-        cols_ref[part] = (dot(high, pick) + dot(low, pick)).reshape(CHUNK, lev, 128)
+    size = 2 * CHUNK
+    for i in range(count // size):
+        part = slice(i * size, i * size + size)
+        x = state_ref[part]
+        high, low = split(x.reshape(size * lev, 1024))
+        cols_ref[part] = (dot(high, pick) + dot(low, pick)).reshape(size, lev, 128)
         edge_ref[part] = jnp.where(slab == 0, x[:, lev - 1, :], x[:, 0, :])
 
 
@@ -144,9 +148,9 @@
     return out
 
 
-def local_kernel(crow_ref, ccol_ref, mix_ref, state_ref, edge_ref, sten_ref, win_ref, base_ref, wins_ref):
+def local_part(blocks, crow_ref, ccol_ref, mix_ref, state_ref, edge_ref, sten_ref):
     slab = lax.axis_index("slab")
-    count, lev = state_ref.shape[0], state_ref.shape[1]
+    lev = state_ref.shape[1]
     a_row = levels_of(crow_ref, lev) * (1.0 / 12.0)
     a_col = levels_of(ccol_ref, lev) * (1.0 / 12.0)
     mix = levels_of(mix_ref, lev)
@@ -154,32 +158,79 @@
     lane = lax.broadcasted_iota(jnp.int32, (rows, 128), 1)
     level = lax.broadcasted_iota(jnp.int32, (CHUNK, lev, 128), 1)
     zero = jnp.zeros((rows, 128), jnp.float32)
+    tiles = [state_ref[blocks, :, 128 * j : 128 * j + 128] for j in range(8)]
+    flat = [t.reshape(rows, 128) for t in tiles]
+    left = []
+    for j in range(8):
+        other = jnp.where(lane < 64, flat[j + 1] if j < 7 else zero, flat[j - 1] if j else zero)
+        left.append(jnp.concatenate(split(flat[j]) + split(other), 1))
+    diff = dot(jnp.concatenate(left, 0), sten_ref[...])
+    done = []
+    for j in range(8):
+        x = tiles[j]
+        edge = edge_ref[blocks, 128 * j : 128 * j + 128][:, None, :]
+        below = jnp.where(level == 0, jnp.where(slab == 0, 0.0, edge), pltpu.roll(x, 1, 1))
+        above = jnp.where(level == lev - 1, jnp.where(slab == 0, edge, 0.0), pltpu.roll(x, lev - 1, 1))
+        vert = above - 2.0 * x + below
+        d = diff[rows * j : rows * j + rows].reshape(CHUNK, lev, 256)
+        done.append(x + a_row * d[:, :, :128] + a_col * d[:, :, 128:] + mix * vert)
+    return done
+
+
+def local_kernel(
+    crow_ref,
+    ccol_ref,
+    mix_ref,
+    block_ref,
+    side_ref,
+    flip_ref,
+    state_ref,
+    edge_ref,
+    sten_ref,
+    win_ref,
+    wins_ref,
+    code_ref,
+    base_ref,
+    sten,
+    win,
+    kept,
+    sems,
+    base_sems,
+):
+    copies = []
+    for i, (ref, held) in enumerate(((sten_ref, sten), (win_ref, win))):
+        for n in range(2):
+            part = pl.ds(n * 256, 256)
+            copies.append(pltpu.make_async_copy(ref.at[part], held.at[part], sems.at[2 * i + n]))
+            copies[-1].start()
+    count, lev = state_ref.shape[0], state_ref.shape[1]
+    here, peers = lax.axis_index("blocks"), lax.axis_size("blocks")
+    block, side, flip = block_ref[...], side_ref[...], flip_ref[...]
+    rel = (block >> 5) - here + 1
+    rel = jnp.where(rel < 0, rel + peers, rel)
+    rel = jnp.where(rel >= peers, rel - peers, rel)
+    rel = jnp.where((here & 1) == 0, rel, 2 - rel)
+    swap = (side & 1) ^ flip
+    code_ref[...] = (block & 31) * 32 + rel * 8 + (side >> 1) * 4 + swap * 2 + flip
+    for copy in copies:
+        copy.wait()
+    rows = CHUNK * lev
+
+    def base_copy(i):
+        blocks = pl.ds(i * CHUNK, CHUNK)
+        return pltpu.make_async_copy(kept.at[blocks], base_ref.at[blocks], base_sems.at[i])
 
     def step(i, carry):
         blocks = pl.ds(pl.multiple_of(i * CHUNK, CHUNK), CHUNK)
-        tiles = [state_ref[blocks, :, 128 * j : 128 * j + 128] for j in range(8)]
-        flat = [t.reshape(rows, 128) for t in tiles]
-        left = []
+        done = local_part(blocks, crow_ref, ccol_ref, mix_ref, state_ref, edge_ref, sten)
         for j in range(8):
-            other = jnp.where(lane < 64, flat[j + 1] if j < 7 else zero, flat[j - 1] if j else zero)
-            left.append(jnp.concatenate(split(flat[j]) + split(other), 1))
-        diff = dot(jnp.concatenate(left, 0), sten_ref[...])
-        done = []
-        for j in range(8):
-            lanes = slice(128 * j, 128 * j + 128)
-            x = tiles[j]
-            edge = edge_ref[blocks, lanes][:, None, :]
-            below = jnp.where(level == 0, jnp.where(slab == 0, 0.0, edge), pltpu.roll(x, 1, 1))
-            above = jnp.where(level == lev - 1, jnp.where(slab == 0, edge, 0.0), pltpu.roll(x, lev - 1, 1))
-            vert = above - 2.0 * x + below
-            d = diff[rows * j : rows * j + rows].reshape(CHUNK, lev, 256)
-            out = x + a_row * d[:, :, :128] + a_col * d[:, :, 128:] + mix * vert
-            base_ref[blocks, :, lanes] = out
-            done.append(out.reshape(rows, 128))
+            kept[blocks, :, 128 * j : 128 * j + 128] = done[j]
+        base_copy(i).start()
         pairs = []
         for j in range(4):
-            pairs.append(jnp.concatenate(split(jnp.concatenate(done[2 * j : 2 * j + 2], 1)), 1))
-        w = dot(jnp.concatenate(pairs, 0), win_ref[...])
+            pair = [t.reshape(rows, 128) for t in done[2 * j : 2 * j + 2]]
+            pairs.append(jnp.concatenate(split(jnp.concatenate(pair, 1)), 1))
+        w = dot(jnp.concatenate(pairs, 0), win[...])
         for j in range(4):
             v = w[rows * j : rows * j + rows].reshape(CHUNK, lev, 256)
             wins_ref[blocks, 2 * j] = v[:, :, :128]
@@ -187,6 +238,8 @@
         return carry
 
     lax.fori_loop(0, count // CHUNK, step, 0)
+    for i in range(count // CHUNK):
+        base_copy(i).wait()
 
 
 def collect_strips(near_refs, near):
@@ -228,8 +281,12 @@
     row0_ref,
     row1_ref,
     pay_ref,
+    ghosts_ref,
     near,
     wins,
+    held_pay,
+    pay_sems,
+    ghost_sems,
     *ghosts,
 ):
     count, lev = own_rows.shape[:2]
@@ -237,8 +294,12 @@
     collect_strips((prev_rows, prev_cols, own_rows, own_cols, next_rows, next_cols), near)
     a_row = levels_of(crow_ref, lev) * (1.0 / 12.0)
     a_col = levels_of(ccol_ref, lev) * (1.0 / 12.0)
+    copies = []
     for i, held in enumerate(ghosts):
         gather_ghosts(i, code_ref, a_row, a_col, near, held)
+        rows = pl.ds(i * CHUNK * lev, CHUNK * lev)
+        copies.append(pltpu.make_async_copy(held, ghosts_ref.at[rows], ghost_sems.at[i]))
+        copies[i].start()
         blocks = slice(i * CHUNK, i * CHUNK + CHUNK)
         row0 = dot(held[:, 0:256], row0_ref[...]).reshape(CHUNK, lev, 256)
         row1 = dot(held[:, 256:512], row1_ref[...]).reshape(CHUNK, lev, 256)
@@ -252,51 +313,35 @@
                     v = v + row1[:, :, 128 * h : 128 * h + 128]
                 wins[blocks, 2 * j + h] = v
 
-    def pack(d, carry):
-        parts = []
-        for k in range(2):
-            w = send_ref[k, d]
-            x = wins[w >> 4, (w >> 1) & 7]
-            parts.append(jnp.where((w & 1) == k, x, pltpu.roll(x, 64, 1)))
-        pay_ref[d] = jnp.where(half == 0, parts[0], parts[1])
-        return carry
-
-    lax.fori_loop(0, pay_ref.shape[0], pack, 0, unroll=PACK)
-
-
-def finish_kernel(
-    code_ref,
-    crow_ref,
-    ccol_ref,
-    base_ref,
-    prev_rows,
-    prev_cols,
-    own_rows,
-    own_cols,
-    next_rows,
-    next_cols,
-    col_ref,
-    row0_ref,
-    row1_ref,
-    out_ref,
-    near,
-    held,
-):
-    lev = own_rows.shape[1]
-    blocks = base_ref.shape[0]
-    i = pl.program_id(0)
-
-    @pl.when(i == 0)
-    def _():
-        collect_strips((prev_rows, prev_cols, own_rows, own_cols, next_rows, next_cols), near)
-
-    a_row = levels_of(crow_ref, lev) * (1.0 / 12.0)
-    a_col = levels_of(ccol_ref, lev) * (1.0 / 12.0)
-    gather_ghosts(i, code_ref, a_row, a_col, near, held)
-    c = dot(held[:, 512:1024], col_ref[...]).reshape(blocks, lev, 1024)
-    out_ref[...] = base_ref[...] + c
-    out_ref[:, :, :128] += dot(held[:, 0:256], row0_ref[...]).reshape(blocks, lev, 128)
-    out_ref[:, :, 896:] += dot(held[:, 256:512], row1_ref[...]).reshape(blocks, lev, 128)
+    size = pay_ref.shape[0] // pay_sems.shape[0]
+    for i in range(pay_sems.shape[0]):
+        for d in range(i * size, i * size + size):
+            parts = []
+            for k in range(2):
+                w = send_ref[k, d]
+                x = wins[w >> 4, (w >> 1) & 7]
+                parts.append(jnp.where((w & 1) == k, x, pltpu.roll(x, 64, 1)))
+            held_pay[d] = jnp.where(half == 0, parts[0], parts[1])
+        part = pl.ds(i * size, size)
+        copies.append(pltpu.make_async_copy(held_pay.at[part], pay_ref.at[part], pay_sems.at[i]))
+        copies[-1].start()
+    for copy in copies:
+        copy.wait()
+
+
+def finish_kernel(base_ref, ghosts_ref, col_ref, row0_ref, row1_ref, out_ref):
+    blocks, lev = base_ref.shape[:2]
+    c = dot(ghosts_ref[:, 512:1024], col_ref[...])
+    row0 = dot(ghosts_ref[:, 0:256], row0_ref[...])
+    row1 = dot(ghosts_ref[:, 256:512], row1_ref[...])
+    for j in range(8):
+        v = c[:, 128 * j : 128 * j + 128]
+        if j == 0:
+            v = v + row0
+        if j == 7:
+            v = v + row1
+        lanes = slice(128 * j, 128 * j + 128)
+        out_ref[:, :, lanes] = base_ref[:, :, lanes] + v.reshape(blocks, lev, 128)
 
 
 def refine_kernel(sizes, slot_ref, count_ref, recv_ref, table_ref, out_ref, held, sems, *parents):
@@ -333,49 +378,78 @@
     return pl.CostEstimate(flops=flops, bytes_accessed=size, transcendentals=0)
 
 
-def make_strips(state):
+def make_rows(state):
     count, lev = state.shape[:2]
-    strip = jax.ShapeDtypeStruct((count, lev, 128), jnp.float32)
     return pl.pallas_call(
-        strips_kernel,
-        out_shape=(strip, strip, jax.ShapeDtypeStruct((count, 1024), jnp.float32)),
+        rows_kernel,
+        out_shape=jax.ShapeDtypeStruct((count, lev, 128), jnp.float32),
         in_specs=[HBM],
-        out_specs=(VMEM, VMEM, VMEM),
-        scratch_shapes=[pltpu.VMEM(state.shape, jnp.float32), pltpu.SemaphoreType.DMA((count // CHUNK,))],
+        out_specs=VMEM,
+        scratch_shapes=[pltpu.VMEM((2, count, lev, 128), jnp.float32), pltpu.SemaphoreType.DMA((4,))],
         compiler_params=PARAMS,
-        name="strips",
+        name="rows",
     )(pltpu.with_memory_space_constraint(state, pltpu.HBM))
 
 
-def make_local(coefs, state, edge):
+def make_cols(state):
     count, lev = state.shape[:2]
+    return pl.pallas_call(
+        cols_kernel,
+        out_shape=(
+            jax.ShapeDtypeStruct((count, lev, 128), jnp.float32),
+            jax.ShapeDtypeStruct((count, 1024), jnp.float32),
+        ),
+        in_specs=[VMEM],
+        out_specs=(VMEM, VMEM),
+        compiler_params=PARAMS,
+        name="cols",
+    )(state)
+
+
+def make_local(coefs, tables, state, edge):
+    count, lev = state.shape[:2]
+    maps = [pltpu.with_memory_space_constraint(jnp.asarray(m), pltpu.HBM) for m in (stencil_map(), window_map())]
     return pl.pallas_call(
         local_kernel,
         out_shape=(
+            jax.ShapeDtypeStruct((count, 8, lev, 128), jnp.float32),
+            jax.ShapeDtypeStruct(tables[0].shape, jnp.int32),
             pltpu.HBM(state.shape, jnp.float32),
-            jax.ShapeDtypeStruct((count, 8, lev, 128), jnp.float32),
         ),
-        in_specs=[SMEM] * 3 + [VMEM] * 4,
-        out_specs=(VMEM, VMEM),
+        in_specs=[SMEM] * 3 + [VMEM] * 5 + [HBM] * 2,
+        out_specs=(VMEM, VMEM, HBM),
+        scratch_shapes=[
+            pltpu.VMEM(maps[0].shape, jnp.bfloat16),
+            pltpu.VMEM(maps[1].shape, jnp.bfloat16),
+            pltpu.VMEM(state.shape, jnp.float32),
+            pltpu.SemaphoreType.DMA((4,)),
+            pltpu.SemaphoreType.DMA((count // CHUNK,)),
+        ],
         compiler_params=PARAMS,
-        cost_estimate=cost(4 * 10**9, 8 * 10**6),
+        cost_estimate=cost(10**3, 10**3),
         name="local",
-    )(*coefs, state, edge, jnp.asarray(stencil_map()), jnp.asarray(window_map()))
+    )(*coefs, *tables, state, edge, *maps)
 
 
 def make_payload(code, send, coefs, base, nearby):
-    count, lev = base.shape[0], base.shape[2]
+    count, lev, peers = base.shape[0], base.shape[2], send.shape[1]
     sides = [window_order(ghost_map(s)) for s in range(4)]
     cols = [m.reshape(256, 4, 256)[:, :, 128 * h : 128 * h + 128].reshape(256, 512) for h, m in enumerate(sides[2:])]
     maps = cols + [sides[0][:, :256], sides[1][:, 768:]]
     return pl.pallas_call(
         pack_kernel,
-        out_shape=jax.ShapeDtypeStruct((send.shape[1], lev, 128), jnp.float32),
+        out_shape=(
+            pltpu.HBM((peers, lev, 128), jnp.float32),
+            pltpu.HBM((count * lev, 1024), jnp.bfloat16),
+        ),
         in_specs=[SMEM] * 4 + [VMEM] * 11,
-        out_specs=VMEM,
+        out_specs=(HBM, HBM),
         scratch_shapes=[
             pltpu.VMEM((3, 2, count, lev, 128), jnp.float32),
             pltpu.VMEM((count, 8, lev, 128), jnp.float32),
+            pltpu.VMEM((peers, lev, 128), jnp.float32),
+            pltpu.SemaphoreType.DMA((4,)),
+            pltpu.SemaphoreType.DMA((count // CHUNK,)),
             *[pltpu.VMEM((CHUNK * lev, 1024), jnp.bfloat16)] * (count // CHUNK),
         ],
         compiler_params=PARAMS,
@@ -384,7 +458,7 @@
     )(code, send, *coefs[:2], base, *nearby, *[jnp.asarray(m) for m in maps])
 
 
-def make_advanced(code, coefs, base, nearby):
+def make_advanced(base, ghosts):
     count, lev = base.shape[:2]
     maps = [np.concatenate([ghost_map(2), ghost_map(3)], 0), ghost_map(0)[:, :128], ghost_map(1)[:, 896:]]
     block = pl.BlockSpec((CHUNK, lev, 1024), lambda i: (i, 0, 0))
@@ -392,16 +466,16 @@
         finish_kernel,
         grid=(count // CHUNK,),
         out_shape=jax.ShapeDtypeStruct(base.shape, jnp.float32),
-        in_specs=[SMEM] * 3 + [block] + [VMEM] * 9,
+        in_specs=[block, pl.BlockSpec((CHUNK * lev, 1024), lambda i: (i, 0))] + [VMEM] * 3,
         out_specs=block,
-        scratch_shapes=[
-            pltpu.VMEM((3, 2, count, lev, 128), jnp.float32),
-            pltpu.VMEM((CHUNK * lev, 1024), jnp.bfloat16),
-        ],
         compiler_params=PARAMS,
         cost_estimate=cost(2 * 10**9, 8 * 10**6),
         name="finish",
-    )(code, *coefs[:2], base, *nearby, *[jnp.asarray(m) for m in maps])
+    )(
+        pltpu.with_memory_space_constraint(base, pltpu.HBM),
+        pltpu.with_memory_space_constraint(ghosts, pltpu.HBM),
+        *[jnp.asarray(m) for m in maps],
+    )
 
 
 def make_refined(slots, live, received):
@@ -426,13 +500,6 @@
     )(slots, live, received, jnp.asarray(refine_table()))
 
 
-def ghost_codes(nbr_block, nbr_side, nbr_flip, count, peers, here):
-    rel = (nbr_block // count - here + 1 + peers) % peers
-    rel = jnp.where(here % 2 == 0, rel, 2 - rel)
-    swap = (nbr_side % 2) ^ nbr_flip
-    return nbr_block % count * 32 + rel * 8 + nbr_side // 2 * 4 + swap * 2 + nbr_flip
-
-
 def body(
     state,
     courant_row,
@@ -446,20 +513,21 @@
     fine_count,
 ):
     peers = lax.axis_size("blocks")
-    here = lax.axis_index("blocks")
-    rows, cols, edge = make_strips(state)
     first = [(i, (i + (1 if i % 2 else -1)) % peers) for i in range(peers)]
     second = [(i, i ^ 1) for i in range(peers)]
-    other = [lax.ppermute(s, "blocks", first) for s in (rows, cols)]
-    after = [lax.ppermute(s, "blocks", second) for s in (rows, cols)]
-    nearby = (*other, rows, cols, *after)
+    rows = make_rows(state)
+    cols, edge = make_cols(state)
+    near_rows = lax.ppermute(rows, "blocks", second)
+    near_cols = lax.ppermute(cols, "blocks", second)
+    far_rows = lax.ppermute(rows, "blocks", first)
+    far_cols = lax.ppermute(cols, "blocks", first)
+    nearby = (far_rows, far_cols, rows, cols, near_rows, near_cols)
     edge = lax.ppermute(edge, "slab", [(0, 1), (1, 0)])
     coefs = (courant_row, courant_col, mixing)
-    base, wins = make_local(coefs, state, edge)
-    code = ghost_codes(nbr_block.T, nbr_side.T, nbr_flip.T, state.shape[0], peers, here)
-    payload = make_payload(code, send_idx[0].T, coefs, wins, nearby)
+    wins, code, base = make_local(coefs, (nbr_block.T, nbr_side.T, nbr_flip.T), state, edge)
+    payload, ghosts = make_payload(code, send_idx[0].T, coefs, wins, nearby)
     received = lax.all_to_all(payload, "blocks", split_axis=0, concat_axis=0, tiled=True)
-    advanced = make_advanced(code, coefs, base, nearby)
+    advanced = make_advanced(base, ghosts)
     return advanced, make_refined(fine_slot, fine_count, received)
 
 

time: 74.9 us -> 73.5 us (0.981)
  local copies, waits for them, and re-layouts: 4.77 us -> 0.1 us
  waiting for transfers between devices: 25.6 us -> 29.1 us
    unnamed x34, local copies, waits for them, and re-layouts: 4.77 us -> 0.1 us
    all_to_all x1, waiting for transfers between devices: 22.6 us -> 24.8 us  [body(): lax.all_to_all(payload, 'blocks', split_axis=0, concat_axis=0, tiled=True)]
    pallas_call x3 -> x4, Pallas kernels: 12.2 us -> 12 us  [the longest x1 5.92 us: make_local(): pl.pallas_call(local_kernel, out_shape=(jax.ShapeDtypeStruct((count, 8, l...]
  transfers between devices with their start and end apart: 6 -> 6, of which waited for: 3 -> 3; matrix products, arithmetic and copies ran while one was open for 1% -> 0% of each run, Pallas kernels for 13% -> 16%
where the time goes in v4:
time: 73.5 us; the launch traced here: 73.2 us
  waiting for transfers between devices  29.1 us (40%)
  starting transfers between devices  22 us (30%)
  Pallas kernels  20.4 us (28%)
  between operations  1.56 us (2%)
    all_to_all x1, waiting for transfers between devices, body(): lax.all_to_all(payload, 'blocks', split_axis=0, concat_axis=0, tiled=True)  24.8 us
    all_to_all x1, starting transfers between devices, body(): lax.all_to_all(payload, 'blocks', split_axis=0, concat_axis=0, tiled=True)  14 us
    pallas_call x1, Pallas kernels, make_local(): pl.pallas_call(local_kernel, out_shape=(jax.ShapeDtypeStruct((count, 8, l...  5.92 us
    pallas_call x1, Pallas kernels, make_advanced(): pl.pallas_call(finish_kernel, grid=(count // CHUNK,), out_shape=jax.Shape...  4.63 us
    ppermute x1, starting transfers between devices, body(): far_rows = lax.ppermute(rows, 'blocks', first)  4.09 us
    pallas_call x1, Pallas kernels, make_payload(): pl.pallas_call(pack_kernel, out_shape=(pltpu.HBM((peers, lev, 128), jnp.f...  3.76 us
    pallas_call x1, Pallas kernels, make_refined(): pl.pallas_call(functools.partial(refine_kernel, tuple(sizes)), out_shape=...  3.76 us
    ppermute x1, waiting for transfers between devices, body(): far_cols = lax.ppermute(cols, 'blocks', first)  2.92 us
  transfers between devices with their start and end apart: 6, of which 3 were waited for; matrix products, arithmetic and copies ran while one was open for 0% of the time, Pallas kernels for 16%

profile of v4, /device:TPU:32, one launch (start us, length us, event | category | flops | bytes accessed | tf_op | source)
XLA Modules:
  0.0 73.2 jit_solution(12763903118658257464)
XLA Ops:
  0.6 0.0 copy-start
  0.6 0.0 copy-start.10
  0.7 0.0 copy-start.9
  0.7 0.0 copy-start.8
  0.7 0.0 copy-start.7
  0.7 0.0 copy-start.6
  0.7 0.0 copy-start.13
  0.7 1.5 %rows.1.own_rows = f32[32,16,128]{2,1,0:T(8,128)S(1)} custom-call(f32[32,16,1024]{2,1,0:T(8,128)} %state_ref.5), custom_call_target="tpu_custom_call" | custom-call | tf_op jit(solution)/shard_map/rows/pallas_call | solution.py:383
  2.2 0.0 copy-start.2
  2.2 0.0 copy-start.3
  2.2 0.0 copy-start.4
  2.2 0.0 copy-start.5
  2.2 0.0 copy-start.11
  2.2 1.6 %collective-permute-start.3 = (f32[32,16,128]{2,1,0:T(8,128)S(1)}, f32[32,16,128]{2,1,0:T(8,128)S(1)}, u32[]{:S(2)}, u32[]{:S(2)}) collective-permute-start(f32[32,16,128]{2,1,0:T(8,128)S(1)} %rows.1.own_rows), channel_id=1, source_target_pairs={{0,2},{2,0},{4,6},{6,4},{8,10},{10,8},{12,14},{14,12},{16,18},{18,... | collective-permute-start | bytes 786440 | tf_op jit(solution)/shard_map/ppermute | solution.py:520
  3.8 4.1 %collective-permute-start.1 = (f32[32,16,128]{2,1,0:T(8,128)S(1)}, f32[32,16,128]{2,1,0:T(8,128)S(1)}, u32[]{:S(2)}, u32[]{:S(2)}) collective-permute-start(f32[32,16,128]{2,1,0:T(8,128)S(1)} %rows.1.own_rows), channel_id=1, source_target_pairs={{0,254},{2,4},{4,2},{6,8},{8,6},{10,12},{12,10},{14,16},{16,14},{1... | collective-permute-start | bytes 786440 | tf_op jit(solution)/shard_map/ppermute | solution.py:522
  7.9 0.0 copy-done
  7.9 0.9 %cols.1 = (f32[32,16,128]{2,1,0:T(8,128)S(1)}, f32[32,1024]{1,0:T(8,128)S(1)}) custom-call(f32[32,16,1024]{2,1,0:T(8,128)S(1)} %copy-done), custom_call_target="tpu_custom_call" | custom-call | tf_op jit(solution)/shard_map/cols/pallas_call | solution.py:396
  8.8 0.1 collective-permute-start.4
  8.9 2.2 %collective-permute-start.2 = (f32[32,16,128]{2,1,0:T(8,128)S(1)}, f32[32,16,128]{2,1,0:T(8,128)S(1)}, u32[]{:S(2)}, u32[]{:S(2)}) collective-permute-start(f32[32,16,128]{2,1,0:T(8,128)S(1)} %get-tuple-element.13.own_cols), channel_id=1, source_target_pairs={{0,254},{2,4},{4,2},{6,8},{8,6},{10,12},{12,10},{14,16},{16,14},{1... | collective-permute-start | bytes 786440 | tf_op jit(solution)/shard_map/ppermute | solution.py:523
  11.2 0.0 collective-permute-start
  11.2 1.3 %collective-permute-done.edge_ref = f32[32,1024]{1,0:T(8,128)S(1)} collective-permute-done((f32[32,1024]{1,0:T(8,128)S(1)}, f32[32,1024]{1,0:T(8,128)S(1)}, u32[]{:S(2)}, u32[]{:S(2)}) %collective-permute-start) | collective-permute-done | bytes 131104 | tf_op jit(solution)/shard_map/ppermute | solution.py:525
  12.5 0.0 copy-done.10
  12.5 0.0 copy-done.9
  12.5 0.0 copy-done.8
  12.5 0.0 copy-done.7
  12.5 0.0 copy-done.6
  12.5 0.0 copy-done.13
  12.5 5.9 %local.1 = (f32[32,8,16,128]{3,2,1,0:T(8,128)S(1)}, s32[4,32]{1,0:T(4,128)S(1)}, f32[32,16,1024]{2,1,0:T(8,128)}) custom-call(f32[16]{0:T(128)S(1)} %copy-done.9, f32[16]{0:T(128)S(1)} %copy-done.10, f32[16]{0:T(128)S(1)} %copy-done.13, s32[4,32]{1,0:T(4,128)S(1)} %bitcast.6, s32[4,32]{1,0:T(4,128)S(1)} %bitcast.7, s32[4,32]{1,0:T(4,128)S(1)} %bitcast.8, ...), custom_call_target="tpu_custom_call" | custom-call | flops 1000 | bytes 1000 | tf_op jit(solution)/shard_map/local/pallas_call | solution.py:412
  18.5 0.0 collective-permute-done.3.next_rows
  18.5 0.0 collective-permute-done.1.prev_rows
  18.5 0.0 collective-permute-done.4.next_cols
  18.5 2.9 %collective-permute-done.2.prev_cols = f32[32,16,128]{2,1,0:T(8,128)S(1)} collective-permute-done((f32[32,16,128]{2,1,0:T(8,128)S(1)}, f32[32,16,128]{2,1,0:T(8,128)S(1)}, u32[]{:S(2)}, u32[]{:S(2)}) %collective-permute-start.2) | collective-permute-done | bytes 262176 | tf_op jit(solution)/shard_map/ppermute | solution.py:523
  21.4 0.0 copy-done.2
  21.4 0.0 copy-done.3
  21.5 3.8 %pack.1 = (f32[128,16,128]{2,1,0:T(8,128)}, bf16[512,1024]{1,0:T(8,128)(2,1)}) custom-call(s32[4,32]{1,0:T(4,128)S(1)} %get-tuple-element.11.code_ref, s32[2,128]{1,0:T(2,128)S(1)} %bitcast.9, f32[16]{0:T(128)S(1)} %copy-done.9, f32[16]{0:T(128)S(1)} %copy-done.10, f32[32,8,16,128]{3,2,1,0:T(8,128)S(1)} %get-tuple-element.12.base_ref, ...), custom_call_target="tpu_custom_call" | custom-call | flops 1000000000 | bytes 8000000 | tf_op jit(solution)/shard_map/pack/pallas_call | solution.py:439
  25.2 0.0 copy-start.14
  25.2 0.0 copy-start.15
  25.3 0.0 copy-start.16
  25.3 14.0 %all-to-all-start = ((f32[128,16,128]{2,1,0:T(8,128)}), f32[128,16,128]{2,1,0:T(8,128)S(1)}, u32[]{:S(2)}, u32[]{:S(2)}) async-start(f32[128,16,128]{2,1,0:T(8,128)} %get-tuple-element.15), calls=%async_computation | async-start | bytes 2097152 | tf_op jit(solution)/shard_map/all_to_all | solution.py:529
  40.0 0.0 copy-done.14
  40.0 0.0 copy-done.15
  40.0 0.0 copy-done.16
  40.0 0.0 copy-start.1
  40.0 0.0 copy-start.12
  40.0 4.6 %finish.1 = f32[32,16,1024]{2,1,0:T(8,128)} custom-call(f32[32,16,1024]{2,1,0:T(8,128)} %get-tuple-element.10.base_ref, bf16[512,1024]{1,0:T(8,128)(2,1)} %get-tuple-element.14.ghosts_ref, bf16[512,1024]{1,0:T(8,128)(2,1)S(1)} %copy-done.14, bf16[256,128]{1,0:T(8,128)(2,1)S(1)} %copy-done.16, bf16[256,128]{1,0:T(8,128)(2,1)S(1)} %copy-done.15), custom_call_target="tpu_custom_call" | custom-call | flops 2000000000 | bytes 8000000 | tf_op jit(solution)/shard_map/finish/pallas_call | solution.py:465
  44.7 24.8 %all-to-all-done.recv_ref = f32[128,16,128]{2,1,0:T(8,128)S(1)} async-done(((f32[128,16,128]{2,1,0:T(8,128)}), f32[128,16,128]{2,1,0:T(8,128)S(1)}, u32[]{:S(2)}, u32[]{:S(2)}) %all-to-all-start) | async-done | bytes 1048608 | tf_op jit(solution)/shard_map/all_to_all | solution.py:529
  69.5 0.0 copy-done.1
  69.5 3.8 %refine.1 = bf16[192,16,1024]{2,1,0:T(8,128)(2,1)} custom-call(s32[1,192]{1,0:T(1,128)S(1)} %copy-done.12, s32[1]{0:T(128)S(6)} %copy.22.count_ref, f32[128,16,128]{2,1,0:T(8,128)S(1)} %all-to-all-done.recv_ref, bf16[256,1024]{1,0:T(8,128)(2,1)S(1)} %copy-done.1), custom_call_target="tpu_custom_call" | custom-call | tf_op jit(solution)/shard_map/refine/pallas_call | solution.py:488
  (4 shorter events, 0.0 us)
Async XLA Ops:
  0.6 7.3 %copy-start = (f32[32,16,1024]{2,1,0:T(8,128)S(1)}, f32[32,16,1024]{2,1,0:T(8,128)}, u32[]{:S(2)}) copy-start(f32[32,16,1024]{2,1,0:T(8,128)} %state_ref.5) | copy-start | bytes 6291460
  0.6 11.9 %copy-start.10 = (f32[16]{0:T(128)S(1)}, f32[16]{0:T(128)}, u32[]{:S(2)}) copy-start(f32[16]{0:T(128)} %ccol_ref.3) | copy-start | bytes 196
  0.7 11.9 %copy-start.9 = (f32[16]{0:T(128)S(1)}, f32[16]{0:T(128)}, u32[]{:S(2)}) copy-start(f32[16]{0:T(128)} %crow_ref.3) | copy-start | bytes 196
  0.7 11.8 %copy-start.8 = (s32[32,4]{0,1:T(4,128)S(1)}, s32[32,4]{0,1:T(4,128)}, u32[]{:S(2)}) copy-start(s32[32,4]{0,1:T(4,128)} %param.26) | copy-start | bytes 1540
  0.7 11.8 %copy-start.7 = (s32[32,4]{0,1:T(4,128)S(1)}, s32[32,4]{0,1:T(4,128)}, u32[]{:S(2)}) copy-start(s32[32,4]{0,1:T(4,128)} %param.25) | copy-start | bytes 1540
  0.7 11.8 %copy-start.6 = (s32[32,4]{0,1:T(4,128)S(1)}, s32[32,4]{0,1:T(4,128)}, u32[]{:S(2)}) copy-start(s32[32,4]{0,1:T(4,128)} %param.24) | copy-start | bytes 1540
  0.7 11.8 %copy-start.13 = (f32[16]{0:T(128)S(1)}, f32[16]{0:T(128)}, u32[]{:S(2)}) copy-start(f32[16]{0:T(128)} %mix_ref.1) | copy-start | bytes 196
  2.2 19.2 %copy-start.2 = (bf16[256,512]{1,0:T(8,128)(2,1)S(1)}, bf16[256,512]{1,0:T(8,128)(2,1)}, u32[]{:S(2)}) copy-start(bf16[256,512]{1,0:T(8,128)(2,1)} %constant.23.clone.col1_ref) | copy-start | bytes 786436
  2.2 19.2 %copy-start.3 = (bf16[256,512]{1,0:T(8,128)(2,1)S(1)}, bf16[256,512]{1,0:T(8,128)(2,1)}, u32[]{:S(2)}) copy-start(bf16[256,512]{1,0:T(8,128)(2,1)} %constant.22.clone.col0_ref) | copy-start | bytes 786436
  2.2 19.2 %copy-start.4 = (bf16[256,256]{1,0:T(8,128)(2,1)S(1)}, bf16[256,256]{1,0:T(8,128)(2,1)}, u32[]{:S(2)}) copy-start(bf16[256,256]{1,0:T(8,128)(2,1)} %constant.25.clone.row1_ref) | copy-start | bytes 393220
  2.2 19.2 %copy-start.5 = (bf16[256,256]{1,0:T(8,128)(2,1)S(1)}, bf16[256,256]{1,0:T(8,128)(2,1)}, u32[]{:S(2)}) copy-start(bf16[256,256]{1,0:T(8,128)(2,1)} %constant.24.clone.row0_ref) | copy-start | bytes 393220
  2.2 19.2 %copy-start.11 = (s32[1,128,2]{1,2,0:T(2,128)S(1)}, s32[1,128,2]{1,2,0:T(2,128)}, u32[]{:S(2)}) copy-start(s32[1,128,2]{1,2,0:T(2,128)} %param.27) | copy-start | bytes 3076
  2.2 16.2 %collective-permute-start.3 = (f32[32,16,128]{2,1,0:T(8,128)S(1)}, f32[32,16,128]{2,1,0:T(8,128)S(1)}, u32[]{:S(2)}, u32[]{:S(2)}) collective-permute-start(f32[32,16,128]{2,1,0:T(8,128)S(1)} %rows.1.own_rows), channel_id=1, source_target_pairs={{0,2},{2,0},{4,6},{6,4},{8,10},{10,8},{12,14},{14,12},{16,18},{18,... | collective-permute-start | bytes 786440 | tf_op jit(solution)/shard_map/ppermute | solution.py:520
  3.8 14.7 %collective-permute-start.1 = (f32[32,16,128]{2,1,0:T(8,128)S(1)}, f32[32,16,128]{2,1,0:T(8,128)S(1)}, u32[]{:S(2)}, u32[]{:S(2)}) collective-permute-start(f32[32,16,128]{2,1,0:T(8,128)S(1)} %rows.1.own_rows), channel_id=1, source_target_pairs={{0,254},{2,4},{4,2},{6,8},{8,6},{10,12},{12,10},{14,16},{16,14},{1... | collective-permute-start | bytes 786440 | tf_op jit(solution)/shard_map/ppermute | solution.py:522
  8.8 9.7 %collective-permute-start.4 = (f32[32,16,128]{2,1,0:T(8,128)S(1)}, f32[32,16,128]{2,1,0:T(8,128)S(1)}, u32[]{:S(2)}, u32[]{:S(2)}) collective-permute-start(f32[32,16,128]{2,1,0:T(8,128)S(1)} %get-tuple-element.13.own_cols), channel_id=1, source_target_pairs={{0,2},{2,0},{4,6},{6,4},{8,10},{10,8},{12,14},{14,12},{16,18},{18,... | collective-permute-start | bytes 786440 | tf_op jit(solution)/shard_map/ppermute | solution.py:521
  8.9 12.5 %collective-permute-start.2 = (f32[32,16,128]{2,1,0:T(8,128)S(1)}, f32[32,16,128]{2,1,0:T(8,128)S(1)}, u32[]{:S(2)}, u32[]{:S(2)}) collective-permute-start(f32[32,16,128]{2,1,0:T(8,128)S(1)} %get-tuple-element.13.own_cols), channel_id=1, source_target_pairs={{0,254},{2,4},{4,2},{6,8},{8,6},{10,12},{12,10},{14,16},{16,14},{1... | collective-permute-start | bytes 786440 | tf_op jit(solution)/shard_map/ppermute | solution.py:523
  11.2 1.3 %collective-permute-start = (f32[32,1024]{1,0:T(8,128)S(1)}, f32[32,1024]{1,0:T(8,128)S(1)}, u32[]{:S(2)}, u32[]{:S(2)}) collective-permute-start(f32[32,1024]{1,0:T(8,128)S(1)} %get-tuple-element.9), channel_id=1, source_target_pairs={{0,1},{1,0},{2,3},{3,2},{4,5},{5,4},{6,7},{7,6},{8,9},{9,8},{10,11... | collective-permute-start | bytes 393224 | tf_op jit(solution)/shard_map/ppermute | solution.py:525
  25.2 14.7 %copy-start.14 = (bf16[512,1024]{1,0:T(8,128)(2,1)S(1)}, bf16[512,1024]{1,0:T(8,128)(2,1)}, u32[]{:S(2)}) copy-start(bf16[512,1024]{1,0:T(8,128)(2,1)} %constant.26.clone.col_ref) | copy-start | bytes 3145732
  25.2 14.7 %copy-start.15 = (bf16[256,128]{1,0:T(8,128)(2,1)S(1)}, bf16[256,128]{1,0:T(8,128)(2,1)}, u32[]{:S(2)}) copy-start(bf16[256,128]{1,0:T(8,128)(2,1)} %constant.28.clone.row1_ref) | copy-start | bytes 196612
  25.3 14.7 %copy-start.16 = (bf16[256,128]{1,0:T(8,128)(2,1)S(1)}, bf16[256,128]{1,0:T(8,128)(2,1)}, u32[]{:S(2)}) copy-start(bf16[256,128]{1,0:T(8,128)(2,1)} %constant.27.clone.row0_ref) | copy-start | bytes 196612
  25.3 44.2 %all-to-all-start = ((f32[128,16,128]{2,1,0:T(8,128)}), f32[128,16,128]{2,1,0:T(8,128)S(1)}, u32[]{:S(2)}, u32[]{:S(2)}) async-start(f32[128,16,128]{2,1,0:T(8,128)} %get-tuple-element.15), calls=%async_computation | async-start | bytes 2097152 | tf_op jit(solution)/shard_map/all_to_all | solution.py:529
  40.0 29.5 %copy-start.1 = (bf16[256,1024]{1,0:T(8,128)(2,1)S(1)}, bf16[256,1024]{1,0:T(8,128)(2,1)}, u32[]{:S(2)}) copy-start(bf16[256,1024]{1,0:T(8,128)(2,1)} %constant.29.clone.table_ref) | copy-start | bytes 1572868
  40.0 29.5 %copy-start.12 = (s32[1,192]{1,0:T(1,128)S(1)}, s32[1,192]{1,0:T(1,128)}, u32[]{:S(2)}) copy-start(s32[1,192]{1,0:T(1,128)} %slot_ref.1) | copy-start | bytes 2308

commit v5 on v4

--- a/solution.py
+++ b/solution.py
@@ -107,36 +107,31 @@
     return jnp.dot(a, b, preferred_element_type=jnp.float32)
 
 
-def rows_kernel(state_ref, rows_ref, held, sems):
-    count, lev = state_ref.shape[0], state_ref.shape[1]
-    copies = []
-    for i in range(4):
-        part = pl.ds(i // 2 * (count // 2), count // 2)
-        lanes = pl.ds(i % 2 * 896, 128)
-        copies.append(pltpu.make_async_copy(state_ref.at[part, :, lanes], held.at[i % 2, part], sems.at[i]))
-        copies[i].start()
-    for copy in copies:
-        copy.wait()
-    lane = lax.broadcasted_iota(jnp.int32, (count * lev, 128), 1)
-    tail = held[1].reshape(count * lev, 128)
-    tail = jnp.where((lane // 32) % 2 == 0, pltpu.roll(tail, 96, 1), pltpu.roll(tail, 32, 1))
-    rows_ref[...] = jnp.where(lane < 64, held[0].reshape(count * lev, 128), tail).reshape(count, lev, 128)
-
-
-def cols_kernel(state_ref, cols_ref, edge_ref):
+def strips_kernel(state_ref, strips_ref, edge_ref, held, sems):
     slab = lax.axis_index("slab")
     count, lev = state_ref.shape[0], state_ref.shape[1]
+    size = count // sems.shape[0]
+    copies = []
+    for i in range(sems.shape[0]):
+        part = pl.ds(i * size, size)
+        copies.append(pltpu.make_async_copy(state_ref.at[part], held.at[part], sems.at[i]))
+        copies[i].start()
     cell = lax.broadcasted_iota(jnp.int32, (1024, 128), 0)
     to = lax.broadcasted_iota(jnp.int32, (1024, 128), 1)
     line = to // 32
     line = jnp.where(line < 2, line, 33 - line)
     pick = jnp.where((cell // 32 == to % 32) & (cell % 32 == line), 1.0, 0.0).astype(jnp.bfloat16)
-    size = 2 * CHUNK
-    for i in range(count // size):
+    rows = size * lev
+    lane = lax.broadcasted_iota(jnp.int32, (rows, 128), 1)
+    for i in range(sems.shape[0]):
+        copies[i].wait()
         part = slice(i * size, i * size + size)
-        x = state_ref[part]
-        high, low = split(x.reshape(size * lev, 1024))
-        cols_ref[part] = (dot(high, pick) + dot(low, pick)).reshape(size, lev, 128)
+        x = held[part]
+        tail = x[:, :, 896:].reshape(rows, 128)
+        tail = jnp.where((lane // 32) % 2 == 0, pltpu.roll(tail, 96, 1), pltpu.roll(tail, 32, 1))
+        strips_ref[part, 0] = jnp.where(lane < 64, x[:, :, :128].reshape(rows, 128), tail).reshape(size, lev, 128)
+        high, low = split(x.reshape(rows, 1024))
+        strips_ref[part, 1] = (dot(high, pick) + dot(low, pick)).reshape(size, lev, 128)
         edge_ref[part] = jnp.where(slab == 0, x[:, lev - 1, :], x[:, 0, :])
 
 
@@ -184,12 +179,14 @@
     block_ref,
     side_ref,
     flip_ref,
+    strips_ref,
     state_ref,
     edge_ref,
     sten_ref,
     win_ref,
     wins_ref,
     code_ref,
+    later_ref,
     base_ref,
     sten,
     win,
@@ -209,9 +206,10 @@
     rel = (block >> 5) - here + 1
     rel = jnp.where(rel < 0, rel + peers, rel)
     rel = jnp.where(rel >= peers, rel - peers, rel)
-    rel = jnp.where((here & 1) == 0, rel, 2 - rel)
+    rel = jnp.where((here & 1) == 0, 2 - rel, rel)
     swap = (side & 1) ^ flip
     code_ref[...] = (block & 31) * 32 + rel * 8 + (side >> 1) * 4 + swap * 2 + flip
+    later_ref[...] = strips_ref[...]
     for copy in copies:
         copy.wait()
     rows = CHUNK * lev
@@ -243,8 +241,14 @@
 
 
 def collect_strips(near_refs, near):
-    for i, ref in enumerate(near_refs):
-        near[i // 2, i % 2] = ref[...]
+    slab = lax.axis_index("slab")
+    near[1] = near_refs[2][...]
+    for owner, refs in ((0, near_refs[:2]), (2, near_refs[3:])):
+        for which in range(2):
+
+            @pl.when(slab == 1 - which)
+            def _():
+                near[owner] = refs[which][...]
 
 
 def gather_ghosts(i, code_ref, a_row, a_col, near, ghosts_ref):
@@ -255,7 +259,7 @@
         parts = []
         for n in range(CHUNK):
             code = code_ref[s, i * CHUNK + n]
-            x = near[(code >> 3) & 3, (code >> 2) & 1, code >> 5]
+            x = near[(code >> 3) & 3, code >> 5, (code >> 2) & 1]
             x = jnp.where((code & 2) == 0, x, pltpu.roll(x, 64, 1))
             parts.append(jnp.where(half == (code & 1), x, 0.0))
         x = jnp.stack(parts) * (a_row if s < 2 else a_col)
@@ -270,12 +274,11 @@
     crow_ref,
     ccol_ref,
     base_ref,
-    prev_rows,
-    prev_cols,
-    own_rows,
-    own_cols,
-    next_rows,
-    next_cols,
+    near_early,
+    near_late,
+    own_ref,
+    far_early,
+    far_late,
     col0_ref,
     col1_ref,
     row0_ref,
@@ -289,9 +292,9 @@
     ghost_sems,
     *ghosts,
 ):
-    count, lev = own_rows.shape[:2]
+    lev = own_ref.shape[2]
     half = lax.broadcasted_iota(jnp.int32, (lev, 128), 1) // 64
-    collect_strips((prev_rows, prev_cols, own_rows, own_cols, next_rows, next_cols), near)
+    collect_strips((near_early, near_late, own_ref, far_early, far_late), near)
     a_row = levels_of(crow_ref, lev) * (1.0 / 12.0)
     a_col = levels_of(ccol_ref, lev) * (1.0 / 12.0)
     copies = []
@@ -378,35 +381,23 @@
     return pl.CostEstimate(flops=flops, bytes_accessed=size, transcendentals=0)
 
 
-def make_rows(state):
+def make_strips(state):
     count, lev = state.shape[:2]
     return pl.pallas_call(
-        rows_kernel,
-        out_shape=jax.ShapeDtypeStruct((count, lev, 128), jnp.float32),
-        in_specs=[HBM],
-        out_specs=VMEM,
-        scratch_shapes=[pltpu.VMEM((2, count, lev, 128), jnp.float32), pltpu.SemaphoreType.DMA((4,))],
-        compiler_params=PARAMS,
-        name="rows",
-    )(pltpu.with_memory_space_constraint(state, pltpu.HBM))
-
-
-def make_cols(state):
-    count, lev = state.shape[:2]
-    return pl.pallas_call(
-        cols_kernel,
+        strips_kernel,
         out_shape=(
-            jax.ShapeDtypeStruct((count, lev, 128), jnp.float32),
+            jax.ShapeDtypeStruct((count, 2, lev, 128), jnp.float32),
             jax.ShapeDtypeStruct((count, 1024), jnp.float32),
         ),
-        in_specs=[VMEM],
+        in_specs=[HBM],
         out_specs=(VMEM, VMEM),
+        scratch_shapes=[pltpu.VMEM(state.shape, jnp.float32), pltpu.SemaphoreType.DMA((2,))],
         compiler_params=PARAMS,
-        name="cols",
-    )(state)
-
-
-def make_local(coefs, tables, state, edge):
+        name="strips",
+    )(pltpu.with_memory_space_constraint(state, pltpu.HBM))
+
+
+def make_local(coefs, tables, strips, state, edge):
     count, lev = state.shape[:2]
     maps = [pltpu.with_memory_space_constraint(jnp.asarray(m), pltpu.HBM) for m in (stencil_map(), window_map())]
     return pl.pallas_call(
@@ -414,10 +405,11 @@
         out_shape=(
             jax.ShapeDtypeStruct((count, 8, lev, 128), jnp.float32),
             jax.ShapeDtypeStruct(tables[0].shape, jnp.int32),
+            jax.ShapeDtypeStruct(strips.shape, jnp.float32),
             pltpu.HBM(state.shape, jnp.float32),
         ),
-        in_specs=[SMEM] * 3 + [VMEM] * 5 + [HBM] * 2,
-        out_specs=(VMEM, VMEM, HBM),
+        in_specs=[SMEM] * 3 + [VMEM] * 6 + [HBM] * 2,
+        out_specs=(VMEM, VMEM, VMEM, HBM),
         scratch_shapes=[
             pltpu.VMEM(maps[0].shape, jnp.bfloat16),
             pltpu.VMEM(maps[1].shape, jnp.bfloat16),
@@ -428,7 +420,7 @@
         compiler_params=PARAMS,
         cost_estimate=cost(10**3, 10**3),
         name="local",
-    )(*coefs, *tables, state, edge, *maps)
+    )(*coefs, *tables, strips, state, edge, *maps)
 
 
 def make_payload(code, send, coefs, base, nearby):
@@ -442,10 +434,10 @@
             pltpu.HBM((peers, lev, 128), jnp.float32),
             pltpu.HBM((count * lev, 1024), jnp.bfloat16),
         ),
-        in_specs=[SMEM] * 4 + [VMEM] * 11,
+        in_specs=[SMEM] * 4 + [VMEM] * 10,
         out_specs=(HBM, HBM),
         scratch_shapes=[
-            pltpu.VMEM((3, 2, count, lev, 128), jnp.float32),
+            pltpu.VMEM((3, count, 2, lev, 128), jnp.float32),
             pltpu.VMEM((count, 8, lev, 128), jnp.float32),
             pltpu.VMEM((peers, lev, 128), jnp.float32),
             pltpu.SemaphoreType.DMA((4,)),
@@ -513,18 +505,23 @@
     fine_count,
 ):
     peers = lax.axis_size("blocks")
-    first = [(i, (i + (1 if i % 2 else -1)) % peers) for i in range(peers)]
-    second = [(i, i ^ 1) for i in range(peers)]
-    rows = make_rows(state)
-    cols, edge = make_cols(state)
-    near_rows = lax.ppermute(rows, "blocks", second)
-    near_cols = lax.ppermute(cols, "blocks", second)
-    far_rows = lax.ppermute(rows, "blocks", first)
-    far_cols = lax.ppermute(cols, "blocks", first)
-    nearby = (far_rows, far_cols, rows, cols, near_rows, near_cols)
+    far = [(i, (i + (1 if i % 2 else -1)) % peers) for i in range(peers)]
+    near = [(i, i ^ 1) for i in range(peers)]
+
+    def exchange(x, pairs, slab):
+        return lax.ppermute(x, ("blocks", "slab"), [(2 * i + slab, 2 * j + slab) for i, j in pairs])
+
+    strips, edge = make_strips(state)
     edge = lax.ppermute(edge, "slab", [(0, 1), (1, 0)])
     coefs = (courant_row, courant_col, mixing)
-    wins, code, base = make_local(coefs, (nbr_block.T, nbr_side.T, nbr_flip.T), state, edge)
+    wins, code, later, base = make_local(coefs, (nbr_block.T, nbr_side.T, nbr_flip.T), strips, state, edge)
+    nearby = (
+        exchange(strips, near, 1),
+        exchange(later, near, 0),
+        strips,
+        exchange(strips, far, 1),
+        exchange(later, far, 0),
+    )
     payload, ghosts = make_payload(code, send_idx[0].T, coefs, wins, nearby)
     received = lax.all_to_all(payload, "blocks", split_axis=0, concat_axis=0, tiled=True)
     advanced = make_advanced(base, ghosts)

time: 73.5 us -> 72.1 us (0.981)
  waiting for transfers between devices: 29.1 us -> 27.1 us
    all_to_all x1, waiting for transfers between devices: 24.8 us -> 18 us  [body(): lax.all_to_all(payload, 'blocks', split_axis=0, concat_axis=0, tiled=True)]
    ppermute x4, waiting for transfers between devices: 2.93 us -> 9.13 us  [exchange(): lax.ppermute(x, ('blocks', 'slab'), [(2 * i + slab, 2 * j + slab) for i,...]
    ppermute x4, starting transfers between devices: 8 us -> 10.1 us  [exchange(): lax.ppermute(x, ('blocks', 'slab'), [(2 * i + slab, 2 * j + slab) for i,...]
    all_to_all x1, starting transfers between devices: 14 us -> 12.3 us  [body(): lax.all_to_all(payload, 'blocks', split_axis=0, concat_axis=0, tiled=True)]
    ppermute x1, waiting for transfers between devices: 1.35 us -> 0.01 us  [body(): edge = lax.ppermute(edge, 'slab', [(0, 1), (1, 0)])]
    pallas_call x2 -> x1, Pallas kernels: 2.36 us -> 2.32 us  [make_strips(): pl.pallas_call(strips_kernel, out_shape=(jax.ShapeDtypeStruct((count, 2,...]
  transfers between devices with their start and end apart: 6 -> 6, of which waited for: 3 -> 3; matrix products, arithmetic and copies ran while one was open for 0% -> 0% of each run, Pallas kernels for 16% -> 15%
where the time goes in v5:
time: 72.1 us; the launch traced here: 71.8 us
  waiting for transfers between devices  27.1 us (38%)
  starting transfers between devices  22.5 us (31%)
  Pallas kernels  20.5 us (28%)
  between operations  1.61 us (2%)
    all_to_all x1, waiting for transfers between devices, body(): lax.all_to_all(payload, 'blocks', split_axis=0, concat_axis=0, tiled=True)  18 us
    all_to_all x1, starting transfers between devices, body(): lax.all_to_all(payload, 'blocks', split_axis=0, concat_axis=0, tiled=True)  12.3 us
    ppermute x4, starting transfers between devices, exchange(): lax.ppermute(x, ('blocks', 'slab'), [(2 * i + slab, 2 * j + slab) for i,...  10.1 us
    ppermute x4, waiting for transfers between devices, exchange(): lax.ppermute(x, ('blocks', 'slab'), [(2 * i + slab, 2 * j + slab) for i,...  9.13 us
    pallas_call x1, Pallas kernels, make_local(): pl.pallas_call(local_kernel, out_shape=(jax.ShapeDtypeStruct((count, 8, l...  5.91 us
    pallas_call x1, Pallas kernels, make_advanced(): pl.pallas_call(finish_kernel, grid=(count // CHUNK,), out_shape=jax.Shape...  4.63 us
    pallas_call x1, Pallas kernels, make_payload(): pl.pallas_call(pack_kernel, out_shape=(pltpu.HBM((peers, lev, 128), jnp.f...  3.82 us
    pallas_call x1, Pallas kernels, make_refined(): pl.pallas_call(functools.partial(refine_kernel, tuple(sizes)), out_shape=...  3.78 us
  transfers between devices with their start and end apart: 6, of which 3 were waited for; matrix products, arithmetic and copies ran while one was open for 0% of the time, Pallas kernels for 15%

profile of v5, /device:TPU:32, one launch (start us, length us, event | category | flops | bytes accessed | tf_op | source)
XLA Modules:
  0.0 71.8 jit_solution(11151205830872106701)
XLA Ops:
  0.6 0.0 copy-start
  0.6 0.0 copy-start.7
  0.7 0.0 copy-start.6
  0.7 0.0 copy-start.10
  0.7 0.0 copy-start.9
  0.7 0.0 copy-start.8
  0.7 0.0 copy-start.13
  0.7 2.3 %strips.1 = (f32[32,2,16,128]{3,2,1,0:T(8,128)S(1)}, f32[32,1024]{1,0:T(8,128)S(1)}) custom-call(f32[32,16,1024]{2,1,0:T(8,128)} %state_ref.3), custom_call_target="tpu_custom_call" | custom-call | tf_op jit(solution)/shard_map/strips/pallas_call | solution.py:386
  3.0 0.0 copy-start.2
  3.0 0.0 copy-start.3
  3.1 0.0 copy-start.4
  3.1 0.0 copy-start.5
  3.1 0.0 copy-start.11
  3.1 0.1 collective-permute-start
  3.2 0.8 %collective-permute-start.3 = (f32[32,2,16,128]{3,2,1,0:T(8,128)S(1)}, f32[32,2,16,128]{3,2,1,0:T(8,128)S(1)}, u32[]{:S(2)}, u32[]{:S(2)}) collective-permute-start(f32[32,2,16,128]{3,2,1,0:T(8,128)S(1)} %get-tuple-element.10.strips_ref.own_ref), channel_id=1, source_target_pairs={{1,255},{3,5},{5,3},{7,9},{9,7},{11,13},{13,11},{15,17},{17,15},{1... | collective-permute-start | bytes 1572872 | tf_op jit(solution)/shard_map/ppermute | solution.py:512
  4.0 0.7 collective-permute-start.1
  4.7 0.0 collective-permute-done.edge_ref
  4.7 0.0 copy-done
  4.7 0.0 copy-done.7
  4.8 0.0 copy-done.6
  4.8 0.0 copy-done.10
  4.8 0.0 copy-done.9
  4.8 0.0 copy-done.8
  4.8 0.0 copy-done.13
  4.8 5.9 %local.1 = (f32[32,8,16,128]{3,2,1,0:T(8,128)S(1)}, s32[4,32]{1,0:T(4,128)S(1)}, f32[32,2,16,128]{3,2,1,0:T(8,128)S(1)}, f32[32,16,1024]{2,1,0:T(8,128)}) custom-call(f32[16]{0:T(128)S(1)} %copy-done.6, f32[16]{0:T(128)S(1)} %copy-done.7, f32[16]{0:T(128)S(1)} %copy-done.13, s32[4,32]{1,0:T(4,128)S(1)} %bitcast.6, s32[4,32]{1,0:T(4,128)S(1)} %bitcast.7, ...), custom_call_target="tpu_custom_call" | custom-call | flops 1000 | bytes 1000 | tf_op jit(solution)/shard_map/local/pallas_call | solution.py:403
  10.7 6.7 %collective-permute-start.4 = (f32[32,2,16,128]{3,2,1,0:T(8,128)S(1)}, f32[32,2,16,128]{3,2,1,0:T(8,128)S(1)}, u32[]{:S(2)}, u32[]{:S(2)}) collective-permute-start(f32[32,2,16,128]{3,2,1,0:T(8,128)S(1)} %get-tuple-element.15), channel_id=1, source_target_pairs={{0,254},{2,4},{4,2},{6,8},{8,6},{10,12},{12,10},{14,16},{16,14},{1... | collective-permute-start | bytes 1572872 | tf_op jit(solution)/shard_map/ppermute | solution.py:512
  17.4 1.9 %collective-permute-start.2 = (f32[32,2,16,128]{3,2,1,0:T(8,128)S(1)}, f32[32,2,16,128]{3,2,1,0:T(8,128)S(1)}, u32[]{:S(2)}, u32[]{:S(2)}) collective-permute-start(f32[32,2,16,128]{3,2,1,0:T(8,128)S(1)} %get-tuple-element.15), channel_id=1, source_target_pairs={{0,2},{2,0},{4,6},{6,4},{8,10},{10,8},{12,14},{14,12},{16,18},{18,... | collective-permute-start | bytes 1572872 | tf_op jit(solution)/shard_map/ppermute | solution.py:512
  19.3 0.0 collective-permute-done.3.far_early
  19.3 0.0 collective-permute-done.1.near_early
  19.3 6.7 %collective-permute-done.4.far_late = f32[32,2,16,128]{3,2,1,0:T(8,128)S(1)} collective-permute-done((f32[32,2,16,128]{3,2,1,0:T(8,128)S(1)}, f32[32,2,16,128]{3,2,1,0:T(8,128)S(1)}, u32[]{:S(2)}, u32[]{:S(2)}) %collective-permute-start.4) | collective-permute-done | bytes 524320 | tf_op jit(solution)/shard_map/ppermute | solution.py:512
  26.0 2.5 %collective-permute-done.2.near_late = f32[32,2,16,128]{3,2,1,0:T(8,128)S(1)} collective-permute-done((f32[32,2,16,128]{3,2,1,0:T(8,128)S(1)}, f32[32,2,16,128]{3,2,1,0:T(8,128)S(1)}, u32[]{:S(2)}, u32[]{:S(2)}) %collective-permute-start.2) | collective-permute-done | bytes 524320 | tf_op jit(solution)/shard_map/ppermute | solution.py:512
  28.5 0.0 copy-done.2
  28.5 0.0 copy-done.3
  28.5 0.0 copy-done.4
  28.5 3.8 %pack.1 = (f32[128,16,128]{2,1,0:T(8,128)}, bf16[512,1024]{1,0:T(8,128)(2,1)}) custom-call(s32[4,32]{1,0:T(4,128)S(1)} %get-tuple-element.13.code_ref, s32[2,128]{1,0:T(2,128)S(1)} %bitcast.9, f32[16]{0:T(128)S(1)} %copy-done.6, f32[16]{0:T(128)S(1)} %copy-done.7, f32[32,8,16,128]{3,2,1,0:T(8,128)S(1)} %get-tuple-element.14.base_ref, ...), custom_call_target="tpu_custom_call" | custom-call | flops 1000000000 | bytes 8000000 | tf_op jit(solution)/shard_map/pack/pallas_call | solution.py:431
  32.3 0.0 copy-start.14
  32.3 0.0 copy-start.15
  32.4 0.0 copy-start.16
  32.4 12.3 %all-to-all-start = ((f32[128,16,128]{2,1,0:T(8,128)}), f32[128,16,128]{2,1,0:T(8,128)S(1)}, u32[]{:S(2)}, u32[]{:S(2)}) async-start(f32[128,16,128]{2,1,0:T(8,128)} %get-tuple-element.17), calls=%async_computation | async-start | bytes 2097152 | tf_op jit(solution)/shard_map/all_to_all | solution.py:526
  45.3 0.0 copy-done.14
  45.3 0.0 copy-done.15
  45.3 0.0 copy-done.16
  45.3 0.0 copy-start.1
  45.3 0.0 copy-start.12
  45.4 4.6 %finish.1 = f32[32,16,1024]{2,1,0:T(8,128)} custom-call(f32[32,16,1024]{2,1,0:T(8,128)} %get-tuple-element.12.base_ref, bf16[512,1024]{1,0:T(8,128)(2,1)} %get-tuple-element.16.ghosts_ref, bf16[512,1024]{1,0:T(8,128)(2,1)S(1)} %copy-done.14, bf16[256,128]{1,0:T(8,128)(2,1)S(1)} %copy-done.16, bf16[256,128]{1,0:T(8,128)(2,1)S(1)} %copy-done.15), custom_call_target="tpu_custom_call" | custom-call | flops 2000000000 | bytes 8000000 | tf_op jit(solution)/shard_map/finish/pallas_call | solution.py:457
  50.0 18.0 %all-to-all-done.recv_ref = f32[128,16,128]{2,1,0:T(8,128)S(1)} async-done(((f32[128,16,128]{2,1,0:T(8,128)}), f32[128,16,128]{2,1,0:T(8,128)S(1)}, u32[]{:S(2)}, u32[]{:S(2)}) %all-to-all-start) | async-done | bytes 1048608 | tf_op jit(solution)/shard_map/all_to_all | solution.py:526
  68.0 0.0 copy-done.1
  68.0 3.8 %refine.1 = bf16[192,16,1024]{2,1,0:T(8,128)(2,1)} custom-call(s32[1,192]{1,0:T(1,128)S(1)} %copy-done.12, s32[1]{0:T(128)S(6)} %copy.22.count_ref, f32[128,16,128]{2,1,0:T(8,128)S(1)} %all-to-all-done.recv_ref, bf16[256,1024]{1,0:T(8,128)(2,1)S(1)} %copy-done.1), custom_call_target="tpu_custom_call" | custom-call | tf_op jit(solution)/shard_map/refine/pallas_call | solution.py:480
  (3 shorter events, 0.0 us)
Async XLA Ops:
  0.6 4.1 %copy-start = (f32[32,16,1024]{2,1,0:T(8,128)S(1)}, f32[32,16,1024]{2,1,0:T(8,128)}, u32[]{:S(2)}) copy-start(f32[32,16,1024]{2,1,0:T(8,128)} %state_ref.3) | copy-start | bytes 6291460
  0.6 4.1 %copy-start.7 = (f32[16]{0:T(128)S(1)}, f32[16]{0:T(128)}, u32[]{:S(2)}) copy-start(f32[16]{0:T(128)} %ccol_ref.3) | copy-start | bytes 196
  0.7 4.1 %copy-start.6 = (f32[16]{0:T(128)S(1)}, f32[16]{0:T(128)}, u32[]{:S(2)}) copy-start(f32[16]{0:T(128)} %crow_ref.3) | copy-start | bytes 196
  0.7 4.1 %copy-start.10 = (s32[32,4]{0,1:T(4,128)S(1)}, s32[32,4]{0,1:T(4,128)}, u32[]{:S(2)}) copy-start(s32[32,4]{0,1:T(4,128)} %param.26) | copy-start | bytes 1540
  0.7 4.1 %copy-start.9 = (s32[32,4]{0,1:T(4,128)S(1)}, s32[32,4]{0,1:T(4,128)}, u32[]{:S(2)}) copy-start(s32[32,4]{0,1:T(4,128)} %param.25) | copy-start | bytes 1540
  0.7 4.1 %copy-start.8 = (s32[32,4]{0,1:T(4,128)S(1)}, s32[32,4]{0,1:T(4,128)}, u32[]{:S(2)}) copy-start(s32[32,4]{0,1:T(4,128)} %param.24) | copy-start | bytes 1540
  0.7 4.1 %copy-start.13 = (f32[16]{0:T(128)S(1)}, f32[16]{0:T(128)}, u32[]{:S(2)}) copy-start(f32[16]{0:T(128)} %mix_ref.1) | copy-start | bytes 196
  3.0 25.4 %copy-start.2 = (bf16[256,512]{1,0:T(8,128)(2,1)S(1)}, bf16[256,512]{1,0:T(8,128)(2,1)}, u32[]{:S(2)}) copy-start(bf16[256,512]{1,0:T(8,128)(2,1)} %constant.23.clone.col1_ref) | copy-start | bytes 786436
  3.0 25.4 %copy-start.3 = (bf16[256,512]{1,0:T(8,128)(2,1)S(1)}, bf16[256,512]{1,0:T(8,128)(2,1)}, u32[]{:S(2)}) copy-start(bf16[256,512]{1,0:T(8,128)(2,1)} %constant.22.clone.col0_ref) | copy-start | bytes 786436
  3.1 25.4 %copy-start.4 = (bf16[256,256]{1,0:T(8,128)(2,1)S(1)}, bf16[256,256]{1,0:T(8,128)(2,1)}, u32[]{:S(2)}) copy-start(bf16[256,256]{1,0:T(8,128)(2,1)} %constant.25.clone.row1_ref) | copy-start | bytes 393220
  3.1 25.4 %copy-start.5 = (bf16[256,256]{1,0:T(8,128)(2,1)S(1)}, bf16[256,256]{1,0:T(8,128)(2,1)}, u32[]{:S(2)}) copy-start(bf16[256,256]{1,0:T(8,128)(2,1)} %constant.24.clone.row0_ref) | copy-start | bytes 393220
  3.1 25.4 %copy-start.11 = (s32[1,128,2]{1,2,0:T(2,128)S(1)}, s32[1,128,2]{1,2,0:T(2,128)}, u32[]{:S(2)}) copy-start(s32[1,128,2]{1,2,0:T(2,128)} %param.27) | copy-start | bytes 3076
  3.1 1.6 %collective-permute-start = (f32[32,1024]{1,0:T(8,128)S(1)}, f32[32,1024]{1,0:T(8,128)S(1)}, u32[]{:S(2)}, u32[]{:S(2)}) collective-permute-start(f32[32,1024]{1,0:T(8,128)S(1)} %get-tuple-element.11), channel_id=1, source_target_pairs={{0,1},{1,0},{2,3},{3,2},{4,5},{5,4},{6,7},{7,6},{8,9},{9,8},{10,11... | collective-permute-start | bytes 393224 | tf_op jit(solution)/shard_map/ppermute | solution.py:515
  3.2 16.1 %collective-permute-start.3 = (f32[32,2,16,128]{3,2,1,0:T(8,128)S(1)}, f32[32,2,16,128]{3,2,1,0:T(8,128)S(1)}, u32[]{:S(2)}, u32[]{:S(2)}) collective-permute-start(f32[32,2,16,128]{3,2,1,0:T(8,128)S(1)} %get-tuple-element.10.strips_ref.own_ref), channel_id=1, source_target_pairs={{1,255},{3,5},{5,3},{7,9},{9,7},{11,13},{13,11},{15,17},{17,15},{1... | collective-permute-start | bytes 1572872 | tf_op jit(solution)/shard_map/ppermute | solution.py:512
  4.0 15.3 %collective-permute-start.1 = (f32[32,2,16,128]{3,2,1,0:T(8,128)S(1)}, f32[32,2,16,128]{3,2,1,0:T(8,128)S(1)}, u32[]{:S(2)}, u32[]{:S(2)}) collective-permute-start(f32[32,2,16,128]{3,2,1,0:T(8,128)S(1)} %get-tuple-element.10.strips_ref.own_ref), channel_id=1, source_target_pairs={{1,3},{3,1},{5,7},{7,5},{9,11},{11,9},{13,15},{15,13},{17,19},{19,... | collective-permute-start | bytes 1572872 | tf_op jit(solution)/shard_map/ppermute | solution.py:512
  10.7 15.3 %collective-permute-start.4 = (f32[32,2,16,128]{3,2,1,0:T(8,128)S(1)}, f32[32,2,16,128]{3,2,1,0:T(8,128)S(1)}, u32[]{:S(2)}, u32[]{:S(2)}) collective-permute-start(f32[32,2,16,128]{3,2,1,0:T(8,128)S(1)} %get-tuple-element.15), channel_id=1, source_target_pairs={{0,254},{2,4},{4,2},{6,8},{8,6},{10,12},{12,10},{14,16},{16,14},{1... | collective-permute-start | bytes 1572872 | tf_op jit(solution)/shard_map/ppermute | solution.py:512
  17.4 11.1 %collective-permute-start.2 = (f32[32,2,16,128]{3,2,1,0:T(8,128)S(1)}, f32[32,2,16,128]{3,2,1,0:T(8,128)S(1)}, u32[]{:S(2)}, u32[]{:S(2)}) collective-permute-start(f32[32,2,16,128]{3,2,1,0:T(8,128)S(1)} %get-tuple-element.15), channel_id=1, source_target_pairs={{0,2},{2,0},{4,6},{6,4},{8,10},{10,8},{12,14},{14,12},{16,18},{18,... | collective-permute-start | bytes 1572872 | tf_op jit(solution)/shard_map/ppermute | solution.py:512
  32.3 13.0 %copy-start.14 = (bf16[512,1024]{1,0:T(8,128)(2,1)S(1)}, bf16[512,1024]{1,0:T(8,128)(2,1)}, u32[]{:S(2)}) copy-start(bf16[512,1024]{1,0:T(8,128)(2,1)} %constant.26.clone.col_ref) | copy-start | bytes 3145732
  32.3 13.0 %copy-start.15 = (bf16[256,128]{1,0:T(8,128)(2,1)S(1)}, bf16[256,128]{1,0:T(8,128)(2,1)}, u32[]{:S(2)}) copy-start(bf16[256,128]{1,0:T(8,128)(2,1)} %constant.28.clone.row1_ref) | copy-start | bytes 196612
  32.4 13.0 %copy-start.16 = (bf16[256,128]{1,0:T(8,128)(2,1)S(1)}, bf16[256,128]{1,0:T(8,128)(2,1)}, u32[]{:S(2)}) copy-start(bf16[256,128]{1,0:T(8,128)(2,1)} %constant.27.clone.row0_ref) | copy-start | bytes 196612
  32.4 35.6 %all-to-all-start = ((f32[128,16,128]{2,1,0:T(8,128)}), f32[128,16,128]{2,1,0:T(8,128)S(1)}, u32[]{:S(2)}, u32[]{:S(2)}) async-start(f32[128,16,128]{2,1,0:T(8,128)} %get-tuple-element.17), calls=%async_computation | async-start | bytes 2097152 | tf_op jit(solution)/shard_map/all_to_all | solution.py:526
  45.3 22.7 %copy-start.1 = (bf16[256,1024]{1,0:T(8,128)(2,1)S(1)}, bf16[256,1024]{1,0:T(8,128)(2,1)}, u32[]{:S(2)}) copy-start(bf16[256,1024]{1,0:T(8,128)(2,1)} %constant.29.clone.table_ref) | copy-start | bytes 1572868
  45.3 22.7 %copy-start.12 = (s32[1,192]{1,0:T(1,128)S(1)}, s32[1,192]{1,0:T(1,128)}, u32[]{:S(2)}) copy-start(s32[1,192]{1,0:T(1,128)} %slot_ref.1) | copy-start | bytes 2308

commit v6 on v5

--- a/solution.py
+++ b/solution.py
@@ -172,21 +172,26 @@
     return done
 
 
+def ghost_codes(block, side, flip):
+    here, peers = lax.axis_index("blocks"), lax.axis_size("blocks")
+    rel = (block >> 5) - here + 1
+    rel = jnp.where(rel < 0, rel + peers, rel)
+    rel = jnp.where(rel >= peers, rel - peers, rel)
+    rel = jnp.where((here & 1) == 0, 2 - rel, rel)
+    swap = (side & 1) ^ flip
+    return (block & 31) * 32 + rel * 8 + (side >> 1) * 4 + swap * 2 + flip
+
+
 def local_kernel(
+    start,
     crow_ref,
     ccol_ref,
     mix_ref,
-    block_ref,
-    side_ref,
-    flip_ref,
-    strips_ref,
     state_ref,
     edge_ref,
     sten_ref,
     win_ref,
     wins_ref,
-    code_ref,
-    later_ref,
     base_ref,
     sten,
     win,
@@ -200,29 +205,22 @@
             part = pl.ds(n * 256, 256)
             copies.append(pltpu.make_async_copy(ref.at[part], held.at[part], sems.at[2 * i + n]))
             copies[-1].start()
-    count, lev = state_ref.shape[0], state_ref.shape[1]
-    here, peers = lax.axis_index("blocks"), lax.axis_size("blocks")
-    block, side, flip = block_ref[...], side_ref[...], flip_ref[...]
-    rel = (block >> 5) - here + 1
-    rel = jnp.where(rel < 0, rel + peers, rel)
-    rel = jnp.where(rel >= peers, rel - peers, rel)
-    rel = jnp.where((here & 1) == 0, 2 - rel, rel)
-    swap = (side & 1) ^ flip
-    code_ref[...] = (block & 31) * 32 + rel * 8 + (side >> 1) * 4 + swap * 2 + flip
-    later_ref[...] = strips_ref[...]
+    count, lev = kept.shape[0], kept.shape[1]
+    rows = CHUNK * lev
     for copy in copies:
         copy.wait()
-    rows = CHUNK * lev
 
     def base_copy(i):
-        blocks = pl.ds(i * CHUNK, CHUNK)
-        return pltpu.make_async_copy(kept.at[blocks], base_ref.at[blocks], base_sems.at[i])
-
-    def step(i, carry):
-        blocks = pl.ds(pl.multiple_of(i * CHUNK, CHUNK), CHUNK)
-        done = local_part(blocks, crow_ref, ccol_ref, mix_ref, state_ref, edge_ref, sten)
+        here = pl.ds(i * CHUNK, CHUNK)
+        there = pl.ds(start + i * CHUNK, CHUNK)
+        return pltpu.make_async_copy(kept.at[here], base_ref.at[there], base_sems.at[i])
+
+    for i in range(count // CHUNK):
+        here = slice(i * CHUNK, i * CHUNK + CHUNK)
+        there = slice(start + i * CHUNK, start + i * CHUNK + CHUNK)
+        done = local_part(there, crow_ref, ccol_ref, mix_ref, state_ref, edge_ref, sten)
         for j in range(8):
-            kept[blocks, :, 128 * j : 128 * j + 128] = done[j]
+            kept[here, :, 128 * j : 128 * j + 128] = done[j]
         base_copy(i).start()
         pairs = []
         for j in range(4):
@@ -231,13 +229,39 @@
         w = dot(jnp.concatenate(pairs, 0), win[...])
         for j in range(4):
             v = w[rows * j : rows * j + rows].reshape(CHUNK, lev, 256)
-            wins_ref[blocks, 2 * j] = v[:, :, :128]
-            wins_ref[blocks, 2 * j + 1] = v[:, :, 128:]
-        return carry
-
-    lax.fori_loop(0, count // CHUNK, step, 0)
+            wins_ref[here, 2 * j] = v[:, :, :128]
+            wins_ref[here, 2 * j + 1] = v[:, :, 128:]
     for i in range(count // CHUNK):
         base_copy(i).wait()
+
+
+def first_local_kernel(
+    crow_ref,
+    ccol_ref,
+    mix_ref,
+    block_ref,
+    side_ref,
+    flip_ref,
+    strips_ref,
+    state_ref,
+    edge_ref,
+    sten_ref,
+    win_ref,
+    wins_ref,
+    base_ref,
+    code_ref,
+    later_ref,
+    *scratch,
+):
+    code_ref[...] = ghost_codes(block_ref[...], side_ref[...], flip_ref[...])
+    later_ref[...] = strips_ref[...]
+    refs = (crow_ref, ccol_ref, mix_ref, state_ref, edge_ref, sten_ref, win_ref, wins_ref, base_ref)
+    local_kernel(0, *refs, *scratch)
+
+
+def second_local_kernel(crow_ref, ccol_ref, mix_ref, state_ref, edge_ref, sten_ref, win_ref, kept_ref, *refs):
+    half = state_ref.shape[0] // 2
+    local_kernel(half, crow_ref, ccol_ref, mix_ref, state_ref, edge_ref, sten_ref, win_ref, *refs)
 
 
 def collect_strips(near_refs, near):
@@ -273,7 +297,8 @@
     send_ref,
     crow_ref,
     ccol_ref,
-    base_ref,
+    base0_ref,
+    base1_ref,
     near_early,
     near_late,
     own_ref,
@@ -304,20 +329,22 @@
         copies.append(pltpu.make_async_copy(held, ghosts_ref.at[rows], ghost_sems.at[i]))
         copies[i].start()
         blocks = slice(i * CHUNK, i * CHUNK + CHUNK)
+        base = (base0_ref, base1_ref)[2 * i // len(ghosts)]
+        mine = slice(blocks.start % base.shape[0], blocks.start % base.shape[0] + CHUNK)
         row0 = dot(held[:, 0:256], row0_ref[...]).reshape(CHUNK, lev, 256)
         row1 = dot(held[:, 256:512], row1_ref[...]).reshape(CHUNK, lev, 256)
         for h, col_ref in enumerate((col0_ref, col1_ref)):
             c = dot(held[:, 512 + 256 * h : 768 + 256 * h], col_ref[...]).reshape(CHUNK, lev, 512)
             for j in range(4):
-                v = base_ref[blocks, 2 * j + h] + c[:, :, 128 * j : 128 * j + 128]
+                v = base[mine, 2 * j + h] + c[:, :, 128 * j : 128 * j + 128]
                 if j == 0:
                     v = v + row0[:, :, 128 * h : 128 * h + 128]
                 if j == 3:
                     v = v + row1[:, :, 128 * h : 128 * h + 128]
                 wins[blocks, 2 * j + h] = v
 
-    size = pay_ref.shape[0] // pay_sems.shape[0]
-    for i in range(pay_sems.shape[0]):
+    size = max(pay_ref.shape[0] // pay_sems.shape[0], 1)
+    for i in range(pay_ref.shape[0] // size):
         for d in range(i * size, i * size + size):
             parts = []
             for k in range(2):
@@ -397,34 +424,48 @@
     )(pltpu.with_memory_space_constraint(state, pltpu.HBM))
 
 
-def make_local(coefs, tables, strips, state, edge):
-    count, lev = state.shape[:2]
+def make_local(coefs, state, edge, tables=(), strips=None, base=None):
+    count, lev = state.shape[0] // 2, state.shape[1]
     maps = [pltpu.with_memory_space_constraint(jnp.asarray(m), pltpu.HBM) for m in (stencil_map(), window_map())]
-    return pl.pallas_call(
-        local_kernel,
-        out_shape=(
-            jax.ShapeDtypeStruct((count, 8, lev, 128), jnp.float32),
+    out_shape = [jax.ShapeDtypeStruct((count, 8, lev, 128), jnp.float32), pltpu.HBM(state.shape, jnp.float32)]
+    in_specs, out_specs = [SMEM] * 3, [VMEM, HBM]
+    args = [*coefs]
+    aliases = {}
+    if base is None:
+        out_shape += [
             jax.ShapeDtypeStruct(tables[0].shape, jnp.int32),
             jax.ShapeDtypeStruct(strips.shape, jnp.float32),
-            pltpu.HBM(state.shape, jnp.float32),
-        ),
-        in_specs=[SMEM] * 3 + [VMEM] * 6 + [HBM] * 2,
-        out_specs=(VMEM, VMEM, VMEM, HBM),
+        ]
+        out_specs += [VMEM, VMEM]
+        in_specs += [VMEM] * 4
+        args += [*tables, strips]
+    in_specs += [VMEM] * 2 + [HBM] * 2
+    args += [state, edge, *maps]
+    if base is not None:
+        aliases = {len(args): 1}
+        in_specs += [HBM]
+        args += [base]
+    return pl.pallas_call(
+        first_local_kernel if base is None else second_local_kernel,
+        out_shape=tuple(out_shape),
+        in_specs=in_specs,
+        out_specs=tuple(out_specs),
         scratch_shapes=[
             pltpu.VMEM(maps[0].shape, jnp.bfloat16),
             pltpu.VMEM(maps[1].shape, jnp.bfloat16),
-            pltpu.VMEM(state.shape, jnp.float32),
+            pltpu.VMEM((count, *state.shape[1:]), jnp.float32),
             pltpu.SemaphoreType.DMA((4,)),
             pltpu.SemaphoreType.DMA((count // CHUNK,)),
         ],
+        input_output_aliases=aliases,
         compiler_params=PARAMS,
         cost_estimate=cost(10**3, 10**3),
         name="local",
-    )(*coefs, *tables, strips, state, edge, *maps)
-
-
-def make_payload(code, send, coefs, base, nearby):
-    count, lev, peers = base.shape[0], base.shape[2], send.shape[1]
+    )(*args)
+
+
+def make_payload(code, send, coefs, bases, nearby):
+    count, lev, peers = 2 * bases[0].shape[0], bases[0].shape[2], send.shape[1]
     sides = [window_order(ghost_map(s)) for s in range(4)]
     cols = [m.reshape(256, 4, 256)[:, :, 128 * h : 128 * h + 128].reshape(256, 512) for h, m in enumerate(sides[2:])]
     maps = cols + [sides[0][:, :256], sides[1][:, 768:]]
@@ -434,20 +475,20 @@
             pltpu.HBM((peers, lev, 128), jnp.float32),
             pltpu.HBM((count * lev, 1024), jnp.bfloat16),
         ),
-        in_specs=[SMEM] * 4 + [VMEM] * 10,
+        in_specs=[SMEM] * 4 + [VMEM] * 11,
         out_specs=(HBM, HBM),
         scratch_shapes=[
             pltpu.VMEM((3, count, 2, lev, 128), jnp.float32),
             pltpu.VMEM((count, 8, lev, 128), jnp.float32),
             pltpu.VMEM((peers, lev, 128), jnp.float32),
-            pltpu.SemaphoreType.DMA((4,)),
+            pltpu.SemaphoreType.DMA((8,)),
             pltpu.SemaphoreType.DMA((count // CHUNK,)),
             *[pltpu.VMEM((CHUNK * lev, 1024), jnp.bfloat16)] * (count // CHUNK),
         ],
         compiler_params=PARAMS,
         cost_estimate=cost(10**9, 8 * 10**6),
         name="pack",
-    )(code, send, *coefs[:2], base, *nearby, *[jnp.asarray(m) for m in maps])
+    )(code, send, *coefs[:2], *bases, *nearby, *[jnp.asarray(m) for m in maps])
 
 
 def make_advanced(base, ghosts):
@@ -509,12 +550,15 @@
     near = [(i, i ^ 1) for i in range(peers)]
 
     def exchange(x, pairs, slab):
-        return lax.ppermute(x, ("blocks", "slab"), [(2 * i + slab, 2 * j + slab) for i, j in pairs])
+        own = [(2 * i + 1 - slab,) * 2 for i in range(peers)]
+        return lax.ppermute(x, ("blocks", "slab"), [(2 * i + slab, 2 * j + slab) for i, j in pairs] + own)
 
     strips, edge = make_strips(state)
     edge = lax.ppermute(edge, "slab", [(0, 1), (1, 0)])
     coefs = (courant_row, courant_col, mixing)
-    wins, code, later, base = make_local(coefs, (nbr_block.T, nbr_side.T, nbr_flip.T), strips, state, edge)
+    tables = (nbr_block.T, nbr_side.T, nbr_flip.T)
+    wins0, base, code, later = make_local(coefs, state, edge, tables, strips)
+    wins1, base = make_local(coefs, state, edge, base=base)
     nearby = (
         exchange(strips, near, 1),
         exchange(later, near, 0),
@@ -522,7 +566,7 @@
         exchange(strips, far, 1),
         exchange(later, far, 0),
     )
-    payload, ghosts = make_payload(code, send_idx[0].T, coefs, wins, nearby)
+    payload, ghosts = make_payload(code, send_idx[0].T, coefs, (wins0, wins1), nearby)
     received = lax.all_to_all(payload, "blocks", split_axis=0, concat_axis=0, tiled=True)
     advanced = make_advanced(base, ghosts)
     return advanced, make_refined(fine_slot, fine_count, received)

time: 72.1 us -> 73.9 us (1.025)
  Pallas kernels: 20.5 us -> 22.8 us
    ppermute x4, waiting for transfers between devices: 9.13 us -> 4.93 us  [exchange(): lax.ppermute(x, ('blocks', 'slab'), [(2 * i + slab, 2 * j + slab) for i,...]
    all_to_all x1, waiting for transfers between devices: 18 us -> 21.7 us  [body(): lax.all_to_all(payload, 'blocks', split_axis=0, concat_axis=0, tiled=True)]
    pallas_call x1 -> x2, Pallas kernels: 5.91 us -> 8.26 us  [make_local(): pl.pallas_call(first_local_kernel if base is None else second_local_kerne...]
  transfers between devices with their start and end apart: 6 -> 6, of which waited for: 3 -> 3; matrix products, arithmetic and copies ran while one was open for 0% -> 0% of each run, Pallas kernels for 15% -> 18%
where the time goes in v6:
time: 73.9 us; the launch traced here: 73.5 us
  waiting for transfers between devices  26.7 us (36%)
  Pallas kernels  22.8 us (31%)
  starting transfers between devices  22.3 us (30%)
  between operations  1.62 us (2%)
    all_to_all x1, waiting for transfers between devices, body(): lax.all_to_all(payload, 'blocks', split_axis=0, concat_axis=0, tiled=True)  21.7 us
    all_to_all x1, starting transfers between devices, body(): lax.all_to_all(payload, 'blocks', split_axis=0, concat_axis=0, tiled=True)  12.3 us
    ppermute x4, starting transfers between devices, exchange(): lax.ppermute(x, ('blocks', 'slab'), [(2 * i + slab, 2 * j + slab) for i,...  9.97 us
    pallas_call x2, Pallas kernels, make_local(): pl.pallas_call(first_local_kernel if base is None else second_local_kerne...  8.26 us
    ppermute x4, waiting for transfers between devices, exchange(): lax.ppermute(x, ('blocks', 'slab'), [(2 * i + slab, 2 * j + slab) for i,...  4.93 us
    pallas_call x1, Pallas kernels, make_advanced(): pl.pallas_call(finish_kernel, grid=(count // CHUNK,), out_shape=jax.Shape...  4.63 us
    pallas_call x1, Pallas kernels, make_payload(): pl.pallas_call(pack_kernel, out_shape=(pltpu.HBM((peers, lev, 128), jnp.f...  3.83 us
    pallas_call x1, Pallas kernels, make_refined(): pl.pallas_call(functools.partial(refine_kernel, tuple(sizes)), out_shape=...  3.76 us
  transfers between devices with their start and end apart: 6, of which 3 were waited for; matrix products, arithmetic and copies ran while one was open for 0% of the time, Pallas kernels for 18%

profile of v6, /device:TPU:32, one launch (start us, length us, event | category | flops | bytes accessed | tf_op | source)
XLA Modules:
  0.0 73.5 jit_solution(15200451881697914239)
XLA Ops:
  0.6 0.0 copy-start
  0.6 0.0 copy-start.7
  0.7 0.0 copy-start.6
  0.7 0.0 copy-start.8
  0.7 0.0 copy-start.11
  0.7 0.0 copy-start.10
  0.7 0.0 copy-start.9
  0.7 2.3 %strips.1 = (f32[32,2,16,128]{3,2,1,0:T(8,128)S(1)}, f32[32,1024]{1,0:T(8,128)S(1)}) custom-call(f32[32,16,1024]{2,1,0:T(8,128)} %state_ref.5), custom_call_target="tpu_custom_call" | custom-call | tf_op jit(solution)/shard_map/strips/pallas_call | solution.py:413
  3.0 0.1 collective-permute-start
  3.1 0.7 collective-permute-start.3
  3.8 0.7 collective-permute-start.1
  4.5 0.0 collective-permute-done.edge_ref
  4.5 0.0 copy-done
  4.6 0.0 copy-done.7
  4.6 0.0 copy-done.6
  4.6 0.0 copy-done.8
  4.6 0.0 copy-done.11
  4.6 0.0 copy-done.10
  4.6 0.0 copy-done.9
  4.6 4.1 %local.2 = (f32[16,8,16,128]{3,2,1,0:T(8,128)S(1)}, f32[32,16,1024]{2,1,0:T(8,128)}, s32[4,32]{1,0:T(4,128)S(1)}, f32[32,2,16,128]{3,2,1,0:T(8,128)S(1)}) custom-call(f32[16]{0:T(128)S(1)} %copy-done.6, f32[16]{0:T(128)S(1)} %copy-done.7, f32[16]{0:T(128)S(1)} %copy-done.8, s32[4,32]{1,0:T(4,128)S(1)} %bitcast.6, s32[4,32]{1,0:T(4,128)S(1)} %bitcast.7, ...), custom_call_target="tpu_custom_call" | custom-call | flops 1000 | bytes 1000 | tf_op jit(solution)/shard_map/local/pallas_call | solution.py:448
  8.8 6.7 %collective-permute-start.4 = (f32[32,2,16,128]{3,2,1,0:T(8,128)S(1)}, f32[32,2,16,128]{3,2,1,0:T(8,128)S(1)}, u32[]{:S(2)}, u32[]{:S(2)}) collective-permute-start(f32[32,2,16,128]{3,2,1,0:T(8,128)S(1)} %get-tuple-element.19), channel_id=1, source_target_pairs={{0,254},{2,4},{4,2},{6,8},{8,6},{10,12},{12,10},{14,16},{16,14},{1... | collective-permute-start | bytes 1572872 | tf_op jit(solution)/shard_map/ppermute | solution.py:554
  15.4 1.9 %collective-permute-start.2 = (f32[32,2,16,128]{3,2,1,0:T(8,128)S(1)}, f32[32,2,16,128]{3,2,1,0:T(8,128)S(1)}, u32[]{:S(2)}, u32[]{:S(2)}) collective-permute-start(f32[32,2,16,128]{3,2,1,0:T(8,128)S(1)} %get-tuple-element.19), channel_id=1, source_target_pairs={{0,2},{2,0},{4,6},{6,4},{8,10},{10,8},{12,14},{14,12},{16,18},{18,... | collective-permute-start | bytes 1572872 | tf_op jit(solution)/shard_map/ppermute | solution.py:554
  17.4 0.0 copy-start.2
  17.4 0.0 copy-start.3
  17.4 0.0 copy-start.4
  17.4 0.0 copy-start.5
  17.4 0.0 copy-start.12
  17.4 4.1 %local.3 = (f32[16,8,16,128]{3,2,1,0:T(8,128)S(1)}, f32[32,16,1024]{2,1,0:T(8,128)}) custom-call(f32[16]{0:T(128)S(1)} %copy-done.6, f32[16]{0:T(128)S(1)} %copy-done.7, f32[16]{0:T(128)S(1)} %copy-done.8, f32[32,16,1024]{2,1,0:T(8,128)S(1)} %copy-done, f32[32,1024]{1,0:T(8,128)S(1)} %collective-permute-done.edge_ref, ...), custom_call_target="tpu_custom_call", output_to_operand_aliasing={{1}: (7, {})} | custom-call | flops 1000 | bytes 1000 | tf_op jit(solution)/shard_map/local/pallas_call | solution.py:448
  21.6 0.0 collective-permute-done.3.far_early
  21.6 0.0 collective-permute-done.1.near_early
  21.6 2.5 %collective-permute-done.4.far_late = f32[32,2,16,128]{3,2,1,0:T(8,128)S(1)} collective-permute-done((f32[32,2,16,128]{3,2,1,0:T(8,128)S(1)}, f32[32,2,16,128]{3,2,1,0:T(8,128)S(1)}, u32[]{:S(2)}, u32[]{:S(2)}) %collective-permute-start.4) | collective-permute-done | bytes 524320 | tf_op jit(solution)/shard_map/ppermute | solution.py:554
  24.0 2.5 %collective-permute-done.2.near_late = f32[32,2,16,128]{3,2,1,0:T(8,128)S(1)} collective-permute-done((f32[32,2,16,128]{3,2,1,0:T(8,128)S(1)}, f32[32,2,16,128]{3,2,1,0:T(8,128)S(1)}, u32[]{:S(2)}, u32[]{:S(2)}) %collective-permute-start.2) | collective-permute-done | bytes 524320 | tf_op jit(solution)/shard_map/ppermute | solution.py:554
  26.5 0.0 copy-done.2
  26.5 0.0 copy-done.3
  26.5 0.0 copy-done.4
  26.5 0.0 copy-done.5
  26.5 0.0 copy-done.12
  26.5 3.8 %pack.1 = (f32[128,16,128]{2,1,0:T(8,128)}, bf16[512,1024]{1,0:T(8,128)(2,1)}) custom-call(s32[4,32]{1,0:T(4,128)S(1)} %get-tuple-element.16.code_ref, s32[2,128]{1,0:T(2,128)S(1)} %bitcast.9, f32[16]{0:T(128)S(1)} %copy-done.6, f32[16]{0:T(128)S(1)} %copy-done.7, f32[16,8,16,128]{3,2,1,0:T(8,128)S(1)} %get-tuple-element.17.base0_ref, ...), custom_call_target="tpu_custom_call" | custom-call | flops 1000000000 | bytes 8000000 | tf_op jit(solution)/shard_map/pack/pallas_call | solution.py:472
  30.4 0.0 copy-start.14
  30.4 0.0 copy-start.15
  30.4 0.0 copy-start.16
  30.4 12.3 %all-to-all-start = ((f32[128,16,128]{2,1,0:T(8,128)}), f32[128,16,128]{2,1,0:T(8,128)S(1)}, u32[]{:S(2)}, u32[]{:S(2)}) async-start(f32[128,16,128]{2,1,0:T(8,128)} %get-tuple-element.21), calls=%async_computation | async-start | bytes 2097152 | tf_op jit(solution)/shard_map/all_to_all | solution.py:570
  43.4 0.0 copy-start.1
  43.4 0.0 copy-start.13
  43.4 4.6 %finish.1 = f32[32,16,1024]{2,1,0:T(8,128)} custom-call(f32[32,16,1024]{2,1,0:T(8,128)} %get-tuple-element.15.base_ref, bf16[512,1024]{1,0:T(8,128)(2,1)} %get-tuple-element.20.ghosts_ref, bf16[512,1024]{1,0:T(8,128)(2,1)S(1)} %copy-done.14, bf16[256,128]{1,0:T(8,128)(2,1)S(1)} %copy-done.16, bf16[256,128]{1,0:T(8,128)(2,1)S(1)} %copy-done.15), custom_call_target="tpu_custom_call" | custom-call | flops 2000000000 | bytes 8000000 | tf_op jit(solution)/shard_map/finish/pallas_call | solution.py:498
  48.0 21.7 %all-to-all-done.recv_ref = f32[128,16,128]{2,1,0:T(8,128)S(1)} async-done(((f32[128,16,128]{2,1,0:T(8,128)}), f32[128,16,128]{2,1,0:T(8,128)S(1)}, u32[]{:S(2)}, u32[]{:S(2)}) %all-to-all-start) | async-done | bytes 1048608 | tf_op jit(solution)/shard_map/all_to_all | solution.py:570
  69.7 0.0 copy-done.1
  69.8 3.8 %refine.1 = bf16[192,16,1024]{2,1,0:T(8,128)(2,1)} custom-call(s32[1,192]{1,0:T(1,128)S(1)} %copy-done.13, s32[1]{0:T(128)S(6)} %copy.26.count_ref, f32[128,16,128]{2,1,0:T(8,128)S(1)} %all-to-all-done.recv_ref, bf16[256,1024]{1,0:T(8,128)(2,1)S(1)} %copy-done.1), custom_call_target="tpu_custom_call" | custom-call | tf_op jit(solution)/shard_map/refine/pallas_call | solution.py:521
  (4 shorter events, 0.0 us)
Async XLA Ops:
  0.6 3.9 %copy-start = (f32[32,16,1024]{2,1,0:T(8,128)S(1)}, f32[32,16,1024]{2,1,0:T(8,128)}, u32[]{:S(2)}) copy-start(f32[32,16,1024]{2,1,0:T(8,128)} %state_ref.5) | copy-start | bytes 6291460
  0.6 3.9 %copy-start.7 = (f32[16]{0:T(128)S(1)}, f32[16]{0:T(128)}, u32[]{:S(2)}) copy-start(f32[16]{0:T(128)} %ccol_ref.5) | copy-start | bytes 196
  0.7 3.9 %copy-start.6 = (f32[16]{0:T(128)S(1)}, f32[16]{0:T(128)}, u32[]{:S(2)}) copy-start(f32[16]{0:T(128)} %crow_ref.5) | copy-start | bytes 196
  0.7 3.9 %copy-start.8 = (f32[16]{0:T(128)S(1)}, f32[16]{0:T(128)}, u32[]{:S(2)}) copy-start(f32[16]{0:T(128)} %mix_ref.3) | copy-start | bytes 196
  0.7 3.9 %copy-start.11 = (s32[32,4]{0,1:T(4,128)S(1)}, s32[32,4]{0,1:T(4,128)}, u32[]{:S(2)}) copy-start(s32[32,4]{0,1:T(4,128)} %param.28) | copy-start | bytes 1540
  0.7 3.9 %copy-start.10 = (s32[32,4]{0,1:T(4,128)S(1)}, s32[32,4]{0,1:T(4,128)}, u32[]{:S(2)}) copy-start(s32[32,4]{0,1:T(4,128)} %param.27) | copy-start | bytes 1540
  0.7 3.9 %copy-start.9 = (s32[32,4]{0,1:T(4,128)S(1)}, s32[32,4]{0,1:T(4,128)}, u32[]{:S(2)}) copy-start(s32[32,4]{0,1:T(4,128)} %param.26) | copy-start | bytes 1540
  3.0 1.5 %collective-permute-start = (f32[32,1024]{1,0:T(8,128)S(1)}, f32[32,1024]{1,0:T(8,128)S(1)}, u32[]{:S(2)}, u32[]{:S(2)}) collective-permute-start(f32[32,1024]{1,0:T(8,128)S(1)} %get-tuple-element.12), channel_id=1, source_target_pairs={{0,1},{1,0},{2,3},{3,2},{4,5},{5,4},{6,7},{7,6},{8,9},{9,8},{10,11... | collective-permute-start | bytes 393224 | tf_op jit(solution)/shard_map/ppermute | solution.py:557
  3.1 18.4 %collective-permute-start.3 = (f32[32,2,16,128]{3,2,1,0:T(8,128)S(1)}, f32[32,2,16,128]{3,2,1,0:T(8,128)S(1)}, u32[]{:S(2)}, u32[]{:S(2)}) collective-permute-start(f32[32,2,16,128]{3,2,1,0:T(8,128)S(1)} %get-tuple-element.13.strips_ref.own_ref), channel_id=1, source_target_pairs={{1,255},{3,5},{5,3},{7,9},{9,7},{11,13},{13,11},{15,17},{17,15},{1... | collective-permute-start | bytes 1572872 | tf_op jit(solution)/shard_map/ppermute | solution.py:554
  3.8 17.7 %collective-permute-start.1 = (f32[32,2,16,128]{3,2,1,0:T(8,128)S(1)}, f32[32,2,16,128]{3,2,1,0:T(8,128)S(1)}, u32[]{:S(2)}, u32[]{:S(2)}) collective-permute-start(f32[32,2,16,128]{3,2,1,0:T(8,128)S(1)} %get-tuple-element.13.strips_ref.own_ref), channel_id=1, source_target_pairs={{1,3},{3,1},{5,7},{7,5},{9,11},{11,9},{13,15},{15,13},{17,19},{19,... | collective-permute-start | bytes 1572872 | tf_op jit(solution)/shard_map/ppermute | solution.py:554
  8.8 15.3 %collective-permute-start.4 = (f32[32,2,16,128]{3,2,1,0:T(8,128)S(1)}, f32[32,2,16,128]{3,2,1,0:T(8,128)S(1)}, u32[]{:S(2)}, u32[]{:S(2)}) collective-permute-start(f32[32,2,16,128]{3,2,1,0:T(8,128)S(1)} %get-tuple-element.19), channel_id=1, source_target_pairs={{0,254},{2,4},{4,2},{6,8},{8,6},{10,12},{12,10},{14,16},{16,14},{1... | collective-permute-start | bytes 1572872 | tf_op jit(solution)/shard_map/ppermute | solution.py:554
  15.4 11.1 %collective-permute-start.2 = (f32[32,2,16,128]{3,2,1,0:T(8,128)S(1)}, f32[32,2,16,128]{3,2,1,0:T(8,128)S(1)}, u32[]{:S(2)}, u32[]{:S(2)}) collective-permute-start(f32[32,2,16,128]{3,2,1,0:T(8,128)S(1)} %get-tuple-element.19), channel_id=1, source_target_pairs={{0,2},{2,0},{4,6},{6,4},{8,10},{10,8},{12,14},{14,12},{16,18},{18,... | collective-permute-start | bytes 1572872 | tf_op jit(solution)/shard_map/ppermute | solution.py:554
  17.4 9.1 %copy-start.2 = (bf16[256,512]{1,0:T(8,128)(2,1)S(1)}, bf16[256,512]{1,0:T(8,128)(2,1)}, u32[]{:S(2)}) copy-start(bf16[256,512]{1,0:T(8,128)(2,1)} %constant.23.clone.col1_ref) | copy-start | bytes 786436
  17.4 9.1 %copy-start.3 = (bf16[256,512]{1,0:T(8,128)(2,1)S(1)}, bf16[256,512]{1,0:T(8,128)(2,1)}, u32[]{:S(2)}) copy-start(bf16[256,512]{1,0:T(8,128)(2,1)} %constant.22.clone.col0_ref) | copy-start | bytes 786436
  17.4 9.1 %copy-start.4 = (bf16[256,256]{1,0:T(8,128)(2,1)S(1)}, bf16[256,256]{1,0:T(8,128)(2,1)}, u32[]{:S(2)}) copy-start(bf16[256,256]{1,0:T(8,128)(2,1)} %constant.25.clone.row1_ref) | copy-start | bytes 393220
  17.4 9.1 %copy-start.5 = (bf16[256,256]{1,0:T(8,128)(2,1)S(1)}, bf16[256,256]{1,0:T(8,128)(2,1)}, u32[]{:S(2)}) copy-start(bf16[256,256]{1,0:T(8,128)(2,1)} %constant.24.clone.row0_ref) | copy-start | bytes 393220
  17.4 9.1 %copy-start.12 = (s32[1,128,2]{1,2,0:T(2,128)S(1)}, s32[1,128,2]{1,2,0:T(2,128)}, u32[]{:S(2)}) copy-start(s32[1,128,2]{1,2,0:T(2,128)} %param.29) | copy-start | bytes 3076
  30.4 13.0 %copy-start.14 = (bf16[512,1024]{1,0:T(8,128)(2,1)S(1)}, bf16[512,1024]{1,0:T(8,128)(2,1)}, u32[]{:S(2)}) copy-start(bf16[512,1024]{1,0:T(8,128)(2,1)} %constant.26.clone.col_ref) | copy-start | bytes 3145732
  30.4 13.0 %copy-start.15 = (bf16[256,128]{1,0:T(8,128)(2,1)S(1)}, bf16[256,128]{1,0:T(8,128)(2,1)}, u32[]{:S(2)}) copy-start(bf16[256,128]{1,0:T(8,128)(2,1)} %constant.28.clone.row1_ref) | copy-start | bytes 196612
  30.4 13.0 %copy-start.16 = (bf16[256,128]{1,0:T(8,128)(2,1)S(1)}, bf16[256,128]{1,0:T(8,128)(2,1)}, u32[]{:S(2)}) copy-start(bf16[256,128]{1,0:T(8,128)(2,1)} %constant.27.clone.row0_ref) | copy-start | bytes 196612
  30.4 39.3 %all-to-all-start = ((f32[128,16,128]{2,1,0:T(8,128)}), f32[128,16,128]{2,1,0:T(8,128)S(1)}, u32[]{:S(2)}, u32[]{:S(2)}) async-start(f32[128,16,128]{2,1,0:T(8,128)} %get-tuple-element.21), calls=%async_computation | async-start | bytes 2097152 | tf_op jit(solution)/shard_map/all_to_all | solution.py:570
  43.4 26.4 %copy-start.1 = (bf16[256,1024]{1,0:T(8,128)(2,1)S(1)}, bf16[256,1024]{1,0:T(8,128)(2,1)}, u32[]{:S(2)}) copy-start(bf16[256,1024]{1,0:T(8,128)(2,1)} %constant.29.clone.table_ref) | copy-start | bytes 1572868
  43.4 26.4 %copy-start.13 = (s32[1,192]{1,0:T(1,128)S(1)}, s32[1,192]{1,0:T(1,128)}, u32[]{:S(2)}) copy-start(s32[1,192]{1,0:T(1,128)} %slot_ref.1) | copy-start | bytes 2308

commit v7 on v5

--- a/solution.py
+++ b/solution.py
@@ -143,8 +143,7 @@
     return out
 
 
-def local_part(blocks, crow_ref, ccol_ref, mix_ref, state_ref, edge_ref, sten_ref):
-    slab = lax.axis_index("slab")
+def local_part(blocks, crow_ref, ccol_ref, mix_ref, state_ref, sten_ref):
     lev = state_ref.shape[1]
     a_row = levels_of(crow_ref, lev) * (1.0 / 12.0)
     a_col = levels_of(ccol_ref, lev) * (1.0 / 12.0)
@@ -163,16 +162,67 @@
     done = []
     for j in range(8):
         x = tiles[j]
-        edge = edge_ref[blocks, 128 * j : 128 * j + 128][:, None, :]
-        below = jnp.where(level == 0, jnp.where(slab == 0, 0.0, edge), pltpu.roll(x, 1, 1))
-        above = jnp.where(level == lev - 1, jnp.where(slab == 0, edge, 0.0), pltpu.roll(x, lev - 1, 1))
+        below = jnp.where(level == 0, 0.0, pltpu.roll(x, 1, 1))
+        above = jnp.where(level == lev - 1, 0.0, pltpu.roll(x, lev - 1, 1))
         vert = above - 2.0 * x + below
         d = diff[rows * j : rows * j + rows].reshape(CHUNK, lev, 256)
         done.append(x + a_row * d[:, :, :128] + a_col * d[:, :, 128:] + mix * vert)
     return done
 
 
-def local_kernel(
+def ghost_codes(block, side, flip):
+    here, peers = lax.axis_index("blocks"), lax.axis_size("blocks")
+    rel = (block >> 5) - here + 1
+    rel = jnp.where(rel < 0, rel + peers, rel)
+    rel = jnp.where(rel >= peers, rel - peers, rel)
+    rel = jnp.where((here & 1) == 0, 2 - rel, rel)
+    swap = (side & 1) ^ flip
+    return (block & 31) * 32 + rel * 8 + (side >> 1) * 4 + swap * 2 + flip
+
+
+def window_tiles(bands, win):
+    pairs = [jnp.concatenate(split(band), 1) for band in bands]
+    w = dot(jnp.concatenate(pairs, 0), win[...])
+    rows = bands[0].shape[0]
+    return [w[rows * (t // 2) : rows * (t // 2) + rows, 128 * (t % 2) : 128 * (t % 2) + 128] for t in range(8)]
+
+
+def load_maps(sten_ref, win_ref, sten, win, sems):
+    copies = []
+    for i, (ref, held) in enumerate(((sten_ref, sten), (win_ref, win))):
+        for n in range(2):
+            part = pl.ds(n * 256, 256)
+            copies.append(pltpu.make_async_copy(ref.at[part], held.at[part], sems.at[2 * i + n]))
+            copies[-1].start()
+    for copy in copies:
+        copy.wait()
+
+
+def local_blocks(crow_ref, ccol_ref, mix_ref, state_ref, wins_ref, base_ref, sten, win, kept, base_sems):
+    count, lev = state_ref.shape[0], state_ref.shape[1]
+    rows = CHUNK * lev
+
+    def base_copy(i):
+        blocks = pl.ds(i * CHUNK, CHUNK)
+        return pltpu.make_async_copy(kept.at[blocks], base_ref.at[blocks], base_sems.at[i])
+
+    def stencil(i, carry):
+        blocks = pl.ds(pl.multiple_of(i * CHUNK, CHUNK), CHUNK)
+        done = local_part(blocks, crow_ref, ccol_ref, mix_ref, state_ref, sten)
+        for j in range(8):
+            kept[blocks, :, 128 * j : 128 * j + 128] = done[j]
+        base_copy(i).start()
+        bands = [jnp.concatenate([t.reshape(rows, 128) for t in done[2 * j : 2 * j + 2]], 1) for j in range(4)]
+        for t, tile in enumerate(window_tiles(bands, win)):
+            wins_ref[blocks, t] = tile.reshape(CHUNK, lev, 128)
+        return carry
+
+    lax.fori_loop(0, count // CHUNK, stencil, 0)
+    for i in range(count // CHUNK):
+        base_copy(i).wait()
+
+
+def first_kernel(
     crow_ref,
     ccol_ref,
     mix_ref,
@@ -181,74 +231,74 @@
     flip_ref,
     strips_ref,
     state_ref,
-    edge_ref,
     sten_ref,
     win_ref,
     wins_ref,
+    base_ref,
     code_ref,
-    later_ref,
-    base_ref,
+    ready_ref,
     sten,
     win,
     kept,
     sems,
     base_sems,
 ):
-    copies = []
-    for i, (ref, held) in enumerate(((sten_ref, sten), (win_ref, win))):
-        for n in range(2):
-            part = pl.ds(n * 256, 256)
-            copies.append(pltpu.make_async_copy(ref.at[part], held.at[part], sems.at[2 * i + n]))
-            copies[-1].start()
+    code_ref[...] = ghost_codes(block_ref[...], side_ref[...], flip_ref[...])
+    ready_ref[...] = strips_ref[...]
+
+    @pl.when(lax.axis_index("slab") == 0)
+    def _():
+        load_maps(sten_ref, win_ref, sten, win, sems)
+        local_blocks(crow_ref, ccol_ref, mix_ref, state_ref, wins_ref, base_ref, sten, win, kept, base_sems)
+
+
+def second_kernel(
+    crow_ref,
+    ccol_ref,
+    mix_ref,
+    edge_ref,
+    state_ref,
+    sten_ref,
+    win_ref,
+    done_ref,
+    base_in_ref,
+    wins_ref,
+    base_ref,
+    fix_ref,
+    sten,
+    win,
+    kept,
+    fix,
+    sems,
+    base_sems,
+    fix_sem,
+):
+    slab = lax.axis_index("slab")
     count, lev = state_ref.shape[0], state_ref.shape[1]
-    here, peers = lax.axis_index("blocks"), lax.axis_size("blocks")
-    block, side, flip = block_ref[...], side_ref[...], flip_ref[...]
-    rel = (block >> 5) - here + 1
-    rel = jnp.where(rel < 0, rel + peers, rel)
-    rel = jnp.where(rel >= peers, rel - peers, rel)
-    rel = jnp.where((here & 1) == 0, 2 - rel, rel)
-    swap = (side & 1) ^ flip
-    code_ref[...] = (block & 31) * 32 + rel * 8 + (side >> 1) * 4 + swap * 2 + flip
-    later_ref[...] = strips_ref[...]
-    for copy in copies:
-        copy.wait()
-    rows = CHUNK * lev
-
-    def base_copy(i):
-        blocks = pl.ds(i * CHUNK, CHUNK)
-        return pltpu.make_async_copy(kept.at[blocks], base_ref.at[blocks], base_sems.at[i])
-
-    def step(i, carry):
-        blocks = pl.ds(pl.multiple_of(i * CHUNK, CHUNK), CHUNK)
-        done = local_part(blocks, crow_ref, ccol_ref, mix_ref, state_ref, edge_ref, sten)
-        for j in range(8):
-            kept[blocks, :, 128 * j : 128 * j + 128] = done[j]
-        base_copy(i).start()
-        pairs = []
-        for j in range(4):
-            pair = [t.reshape(rows, 128) for t in done[2 * j : 2 * j + 2]]
-            pairs.append(jnp.concatenate(split(jnp.concatenate(pair, 1)), 1))
-        w = dot(jnp.concatenate(pairs, 0), win[...])
-        for j in range(4):
-            v = w[rows * j : rows * j + rows].reshape(CHUNK, lev, 256)
-            wins_ref[blocks, 2 * j] = v[:, :, :128]
-            wins_ref[blocks, 2 * j + 1] = v[:, :, 128:]
-        return carry
-
-    lax.fori_loop(0, count // CHUNK, step, 0)
-    for i in range(count // CHUNK):
-        base_copy(i).wait()
+    fix[...] = edge_ref[...] * jnp.where(slab == 0, mix_ref[lev - 1], mix_ref[0])
+    fix_copy = pltpu.make_async_copy(fix, fix_ref, fix_sem.at[0])
+    fix_copy.start()
+    load_maps(sten_ref, win_ref, sten, win, sems)
+    edge = window_tiles([fix[:, 256 * j : 256 * j + 256] for j in range(4)], win)
+
+    @pl.when(slab == 1)
+    def _():
+        local_blocks(crow_ref, ccol_ref, mix_ref, state_ref, wins_ref, base_ref, sten, win, kept, base_sems)
+        for t in range(8):
+            wins_ref[:, t, 0, :] += edge[t]
+
+    @pl.when(slab == 0)
+    def _():
+        wins_ref[...] = done_ref[...]
+        for t in range(8):
+            wins_ref[:, t, lev - 1, :] += edge[t]
+
+    fix_copy.wait()
 
 
 def collect_strips(near_refs, near):
-    slab = lax.axis_index("slab")
-    near[1] = near_refs[2][...]
-    for owner, refs in ((0, near_refs[:2]), (2, near_refs[3:])):
-        for which in range(2):
-
-            @pl.when(slab == 1 - which)
-            def _():
-                near[owner] = refs[which][...]
+    for i, ref in enumerate(near_refs):
+        near[i] = ref[...]
 
 
 def gather_ghosts(i, code_ref, a_row, a_col, near, ghosts_ref):
@@ -274,11 +324,9 @@
     crow_ref,
     ccol_ref,
     base_ref,
-    near_early,
-    near_late,
+    near_ref,
     own_ref,
-    far_early,
-    far_late,
+    far_ref,
     col0_ref,
     col1_ref,
     row0_ref,
@@ -294,7 +342,7 @@
 ):
     lev = own_ref.shape[2]
     half = lax.broadcasted_iota(jnp.int32, (lev, 128), 1) // 64
-    collect_strips((near_early, near_late, own_ref, far_early, far_late), near)
+    collect_strips((near_ref, own_ref, far_ref), near)
     a_row = levels_of(crow_ref, lev) * (1.0 / 12.0)
     a_col = levels_of(ccol_ref, lev) * (1.0 / 12.0)
     copies = []
@@ -332,8 +380,10 @@
         copy.wait()
 
 
-def finish_kernel(base_ref, ghosts_ref, col_ref, row0_ref, row1_ref, out_ref):
+def finish_kernel(base_ref, ghosts_ref, fix_ref, col_ref, row0_ref, row1_ref, out_ref):
     blocks, lev = base_ref.shape[:2]
+    level = lax.broadcasted_iota(jnp.int32, (blocks, lev, 128), 1)
+    edge_level = jnp.where(lax.axis_index("slab") == 0, lev - 1, 0)
     c = dot(ghosts_ref[:, 512:1024], col_ref[...])
     row0 = dot(ghosts_ref[:, 0:256], row0_ref[...])
     row1 = dot(ghosts_ref[:, 256:512], row1_ref[...])
@@ -344,7 +394,8 @@
         if j == 7:
             v = v + row1
         lanes = slice(128 * j, 128 * j + 128)
-        out_ref[:, :, lanes] = base_ref[:, :, lanes] + v.reshape(blocks, lev, 128)
+        fix = jnp.where(level == edge_level, fix_ref[:, lanes][:, None, :], 0.0)
+        out_ref[:, :, lanes] = base_ref[:, :, lanes] + fix + v.reshape(blocks, lev, 128)
 
 
 def refine_kernel(sizes, slot_ref, count_ref, recv_ref, table_ref, out_ref, held, sems, *parents):
@@ -397,30 +448,60 @@
     )(pltpu.with_memory_space_constraint(state, pltpu.HBM))
 
 
-def make_local(coefs, tables, strips, state, edge):
+def local_maps():
+    return [pltpu.with_memory_space_constraint(jnp.asarray(m), pltpu.HBM) for m in (stencil_map(), window_map())]
+
+
+def local_scratch(state):
+    return [
+        pltpu.VMEM((512, 256), jnp.bfloat16),
+        pltpu.VMEM((512, 256), jnp.bfloat16),
+        pltpu.VMEM(state.shape, jnp.float32),
+    ]
+
+
+def make_first(coefs, tables, strips, state):
     count, lev = state.shape[:2]
-    maps = [pltpu.with_memory_space_constraint(jnp.asarray(m), pltpu.HBM) for m in (stencil_map(), window_map())]
     return pl.pallas_call(
-        local_kernel,
+        first_kernel,
         out_shape=(
             jax.ShapeDtypeStruct((count, 8, lev, 128), jnp.float32),
+            pltpu.HBM(state.shape, jnp.float32),
             jax.ShapeDtypeStruct(tables[0].shape, jnp.int32),
             jax.ShapeDtypeStruct(strips.shape, jnp.float32),
+        ),
+        in_specs=[SMEM] * 3 + [VMEM] * 5 + [HBM] * 2,
+        out_specs=(VMEM, HBM, VMEM, VMEM),
+        scratch_shapes=local_scratch(state)
+        + [pltpu.SemaphoreType.DMA((4,)), pltpu.SemaphoreType.DMA((count // CHUNK,))],
+        compiler_params=PARAMS,
+        name="first",
+    )(*coefs, *tables, strips, state, *local_maps())
+
+
+def make_second(coefs, edge, state, wins, base):
+    count, lev = state.shape[:2]
+    return pl.pallas_call(
+        second_kernel,
+        out_shape=(
+            jax.ShapeDtypeStruct(wins.shape, jnp.float32),
             pltpu.HBM(state.shape, jnp.float32),
+            pltpu.HBM(edge.shape, jnp.float32),
         ),
-        in_specs=[SMEM] * 3 + [VMEM] * 6 + [HBM] * 2,
-        out_specs=(VMEM, VMEM, VMEM, HBM),
-        scratch_shapes=[
-            pltpu.VMEM(maps[0].shape, jnp.bfloat16),
-            pltpu.VMEM(maps[1].shape, jnp.bfloat16),
-            pltpu.VMEM(state.shape, jnp.float32),
+        in_specs=[SMEM] * 3 + [VMEM] * 2 + [HBM] * 2 + [VMEM, HBM],
+        out_specs=(VMEM, HBM, HBM),
+        scratch_shapes=local_scratch(state)
+        + [
+            pltpu.VMEM(edge.shape, jnp.float32),
             pltpu.SemaphoreType.DMA((4,)),
             pltpu.SemaphoreType.DMA((count // CHUNK,)),
+            pltpu.SemaphoreType.DMA((1,)),
         ],
+        input_output_aliases={8: 1},
         compiler_params=PARAMS,
         cost_estimate=cost(10**3, 10**3),
-        name="local",
-    )(*coefs, *tables, strips, state, edge, *maps)
+        name="second",
+    )(*coefs, edge, state, *local_maps(), wins, base)
 
 
 def make_payload(code, send, coefs, base, nearby):
@@ -434,7 +515,7 @@
             pltpu.HBM((peers, lev, 128), jnp.float32),
             pltpu.HBM((count * lev, 1024), jnp.bfloat16),
         ),
-        in_specs=[SMEM] * 4 + [VMEM] * 10,
+        in_specs=[SMEM] * 4 + [VMEM] * 8,
         out_specs=(HBM, HBM),
         scratch_shapes=[
             pltpu.VMEM((3, count, 2, lev, 128), jnp.float32),
@@ -450,7 +531,7 @@
     )(code, send, *coefs[:2], base, *nearby, *[jnp.asarray(m) for m in maps])
 
 
-def make_advanced(base, ghosts):
+def make_advanced(base, ghosts, fix):
     count, lev = base.shape[:2]
     maps = [np.concatenate([ghost_map(2), ghost_map(3)], 0), ghost_map(0)[:, :128], ghost_map(1)[:, 896:]]
     block = pl.BlockSpec((CHUNK, lev, 1024), lambda i: (i, 0, 0))
@@ -458,7 +539,8 @@
         finish_kernel,
         grid=(count // CHUNK,),
         out_shape=jax.ShapeDtypeStruct(base.shape, jnp.float32),
-        in_specs=[block, pl.BlockSpec((CHUNK * lev, 1024), lambda i: (i, 0))] + [VMEM] * 3,
+        in_specs=[block, pl.BlockSpec((CHUNK * lev, 1024), lambda i: (i, 0)), pl.BlockSpec((CHUNK, 1024), lambda i: (i, 0))]
+        + [VMEM] * 3,
         out_specs=block,
         compiler_params=PARAMS,
         cost_estimate=cost(2 * 10**9, 8 * 10**6),
@@ -466,6 +548,7 @@
     )(
         pltpu.with_memory_space_constraint(base, pltpu.HBM),
         pltpu.with_memory_space_constraint(ghosts, pltpu.HBM),
+        pltpu.with_memory_space_constraint(fix, pltpu.HBM),
         *[jnp.asarray(m) for m in maps],
     )
 
@@ -507,24 +590,15 @@
     peers = lax.axis_size("blocks")
     far = [(i, (i + (1 if i % 2 else -1)) % peers) for i in range(peers)]
     near = [(i, i ^ 1) for i in range(peers)]
-
-    def exchange(x, pairs, slab):
-        return lax.ppermute(x, ("blocks", "slab"), [(2 * i + slab, 2 * j + slab) for i, j in pairs])
-
+    coefs = (courant_row, courant_col, mixing)
     strips, edge = make_strips(state)
+    wins, base, code, strips = make_first(coefs, (nbr_block.T, nbr_side.T, nbr_flip.T), strips, state)
+    nearby = (lax.ppermute(strips, "blocks", near), strips, lax.ppermute(strips, "blocks", far))
     edge = lax.ppermute(edge, "slab", [(0, 1), (1, 0)])
-    coefs = (courant_row, courant_col, mixing)
-    wins, code, later, base = make_local(coefs, (nbr_block.T, nbr_side.T, nbr_flip.T), strips, state, edge)
-    nearby = (
-        exchange(strips, near, 1),
-        exchange(later, near, 0),
-        strips,
-        exchange(strips, far, 1),
-        exchange(later, far, 0),
-    )
+    wins, base, fix = make_second(coefs, edge, state, wins, base)
     payload, ghosts = make_payload(code, send_idx[0].T, coefs, wins, nearby)
     received = lax.all_to_all(payload, "blocks", split_axis=0, concat_axis=0, tiled=True)
-    advanced = make_advanced(base, ghosts)
+    advanced = make_advanced(base, ghosts, fix)
     return advanced, make_refined(fine_slot, fine_count, received)
 
 

time: 72.1 us -> 73.7 us (1.022)
  starting transfers between devices: 22.5 us -> 19 us
  waiting for transfers between devices: 27.1 us -> 30.2 us
  Pallas kernels: 20.5 us -> 22.7 us
    all_to_all x1, waiting for transfers between devices: 18 us -> 23.3 us  [body(): lax.all_to_all(payload, 'blocks', split_axis=0, concat_axis=0, tiled=True)]
    ppermute x4 -> x2, starting transfers between devices: 10.1 us -> 4.85 us  [the longest x1 4.85 us: body(): lax.ppermute(strips, 'blocks', far)]
    ppermute x4 -> x2, waiting for transfers between devices: 9.13 us -> 5.49 us  [the longest x1 4.95 us: body(): lax.ppermute(strips, 'blocks', far)]
    pallas_call x1 -> x2, Pallas kernels: 5.91 us -> 8.11 us  [the longest x1 5.8 us: make_first(): pl.pallas_call(first_kernel, out_shape=(jax.ShapeDtypeStruct((count, 8, l...]
    all_to_all x1, starting transfers between devices: 12.3 us -> 14.2 us  [body(): lax.all_to_all(payload, 'blocks', split_axis=0, concat_axis=0, tiled=True)]
    ppermute x1, waiting for transfers between devices: 0.01 us -> 1.35 us  [body(): edge = lax.ppermute(edge, 'slab', [(0, 1), (1, 0)])]
  transfers between devices with their start and end apart: 6 -> 4, of which waited for: 3 -> 4; matrix products, arithmetic and copies ran while one was open for 0% -> 0% of each run, Pallas kernels for 15% -> 10%
where the time goes in v7:
time: 73.7 us; the launch traced here: 73.5 us
  waiting for transfers between devices  30.2 us (41%)
  Pallas kernels  22.7 us (31%)
  starting transfers between devices  19 us (26%)
  between operations  1.53 us (2%)
    all_to_all x1, waiting for transfers between devices, body(): lax.all_to_all(payload, 'blocks', split_axis=0, concat_axis=0, tiled=True)  23.3 us
    all_to_all x1, starting transfers between devices, body(): lax.all_to_all(payload, 'blocks', split_axis=0, concat_axis=0, tiled=True)  14.2 us
    pallas_call x1, Pallas kernels, make_first(): pl.pallas_call(first_kernel, out_shape=(jax.ShapeDtypeStruct((count, 8, l...  5.8 us
    ppermute x1, waiting for transfers between devices, body(): lax.ppermute(strips, 'blocks', far)  4.95 us
    ppermute x1, starting transfers between devices, body(): lax.ppermute(strips, 'blocks', far)  4.85 us
    pallas_call x1, Pallas kernels, make_advanced(): pl.pallas_call(finish_kernel, grid=(count // CHUNK,), out_shape=jax.Shape...  4.71 us
    pallas_call x1, Pallas kernels, make_refined(): pl.pallas_call(functools.partial(refine_kernel, tuple(sizes)), out_shape=...  3.78 us
    pallas_call x1, Pallas kernels, make_payload(): pl.pallas_call(pack_kernel, out_shape=(pltpu.HBM((peers, lev, 128), jnp.f...  3.74 us
  transfers between devices with their start and end apart: 4, of which 4 were waited for; matrix products, arithmetic and copies ran while one was open for 0% of the time, Pallas kernels for 10%

profile of v7, /device:TPU:32, one launch (start us, length us, event | category | flops | bytes accessed | tf_op | source)
XLA Modules:
  0.0 73.5 jit_solution(18089557523293238792)
XLA Ops:
  0.6 0.0 copy-start
  0.6 0.0 copy-start.7
  0.7 0.0 copy-start.6
  0.7 0.0 copy-start.11
  0.7 0.0 copy-start.10
  0.7 0.0 copy-start.9
  0.7 0.0 copy-start.8
  0.7 2.3 %strips.1 = (f32[32,2,16,128]{3,2,1,0:T(8,128)S(1)}, f32[32,1024]{1,0:T(8,128)S(1)}) custom-call(f32[32,16,1024]{2,1,0:T(8,128)} %state_ref.5), custom_call_target="tpu_custom_call" | custom-call | tf_op jit(solution)/shard_map/strips/pallas_call | solution.py:437
  3.0 0.0 copy-done
  3.0 0.0 copy-done.7
  3.0 0.0 copy-done.6
  3.1 0.0 copy-done.11
  3.1 0.0 copy-done.10
  3.1 0.0 copy-done.9
  3.1 0.0 copy-done.8
  3.1 5.8 %first.1 = (f32[32,8,16,128]{3,2,1,0:T(8,128)S(1)}, f32[32,16,1024]{2,1,0:T(8,128)}, s32[4,32]{1,0:T(4,128)S(1)}, f32[32,2,16,128]{3,2,1,0:T(8,128)S(1)}) custom-call(f32[16]{0:T(128)S(1)} %copy-done.6, f32[16]{0:T(128)S(1)} %copy-done.7, f32[16]{0:T(128)S(1)} %copy-done.11, s32[4,32]{1,0:T(4,128)S(1)} %bitcast.6, s32[4,32]{1,0:T(4,128)S(1)} %bitcast.7, ...), custom_call_target="tpu_custom_call" | custom-call | tf_op jit(solution)/shard_map/first/pallas_call | solution.py:465
  8.9 4.8 %collective-permute-start.2 = (f32[32,2,16,128]{3,2,1,0:T(8,128)S(1)}, f32[32,2,16,128]{3,2,1,0:T(8,128)S(1)}, u32[]{:S(2)}, u32[]{:S(2)}) collective-permute-start(f32[32,2,16,128]{3,2,1,0:T(8,128)S(1)} %get-tuple-element.20.own_ref), channel_id=1, source_target_pairs={{0,254},{2,4},{4,2},{6,8},{8,6},{10,12},{12,10},{14,16},{16,14},{1... | collective-permute-start | bytes 1572872 | tf_op jit(solution)/shard_map/ppermute | solution.py:596
  13.8 0.0 collective-permute-start.1
  13.8 0.0 collective-permute-start
  13.8 1.3 %collective-permute-done.edge_ref = f32[32,1024]{1,0:T(8,128)S(1)} collective-permute-done((f32[32,1024]{1,0:T(8,128)S(1)}, f32[32,1024]{1,0:T(8,128)S(1)}, u32[]{:S(2)}, u32[]{:S(2)}) %collective-permute-start) | collective-permute-done | bytes 131104 | tf_op jit(solution)/shard_map/ppermute | solution.py:597
  15.1 0.0 copy-start.2
  15.1 0.0 copy-start.3
  15.1 0.0 copy-start.4
  15.1 0.0 copy-start.5
  15.1 0.0 copy-start.12
  15.1 2.3 %second.1 = (f32[32,8,16,128]{3,2,1,0:T(8,128)S(1)}, f32[32,16,1024]{2,1,0:T(8,128)}, f32[32,1024]{1,0:T(8,128)}) custom-call(f32[16]{0:T(128)S(1)} %copy-done.6, f32[16]{0:T(128)S(1)} %copy-done.7, f32[16]{0:T(128)S(1)} %copy-done.11, f32[32,1024]{1,0:T(8,128)S(1)} %collective-permute-done.edge_ref, ...), custom_call_target="tpu_custom_call", output_to_operand_aliasing={{1}: (8, {})} | custom-call | flops 1000 | bytes 1000 | tf_op jit(solution)/shard_map/second/pallas_call | solution.py:484
  17.4 5.0 %collective-permute-done.2.far_ref = f32[32,2,16,128]{3,2,1,0:T(8,128)S(1)} collective-permute-done((f32[32,2,16,128]{3,2,1,0:T(8,128)S(1)}, f32[32,2,16,128]{3,2,1,0:T(8,128)S(1)}, u32[]{:S(2)}, u32[]{:S(2)}) %collective-permute-start.2) | collective-permute-done | bytes 524320 | tf_op jit(solution)/shard_map/ppermute | solution.py:596
  22.4 0.5 collective-permute-done.1.near_ref
  22.9 0.0 copy-done.2
  22.9 0.0 copy-done.3
  22.9 0.0 copy-done.4
  22.9 0.0 copy-done.5
  23.0 0.0 copy-done.12
  23.0 3.7 %pack.1 = (f32[128,16,128]{2,1,0:T(8,128)}, bf16[512,1024]{1,0:T(8,128)(2,1)}) custom-call(s32[4,32]{1,0:T(4,128)S(1)} %get-tuple-element.18.code_ref, s32[2,128]{1,0:T(2,128)S(1)} %bitcast.9, f32[16]{0:T(128)S(1)} %copy-done.6, f32[16]{0:T(128)S(1)} %copy-done.7, f32[32,8,16,128]{3,2,1,0:T(8,128)S(1)} %get-tuple-element.19.base_ref, ...), custom_call_target="tpu_custom_call" | custom-call | flops 1000000000 | bytes 8000000 | tf_op jit(solution)/shard_map/pack/pallas_call | solution.py:512
  26.7 0.0 copy-start.14
  26.7 0.0 copy-start.15
  26.7 0.0 copy-start.16
  26.8 14.2 %all-to-all-start = ((f32[128,16,128]{2,1,0:T(8,128)}), f32[128,16,128]{2,1,0:T(8,128)S(1)}, u32[]{:S(2)}, u32[]{:S(2)}) async-start(f32[128,16,128]{2,1,0:T(8,128)} %get-tuple-element.23), calls=%async_computation | async-start | bytes 2097152 | tf_op jit(solution)/shard_map/all_to_all | solution.py:600
  41.6 0.0 copy-done.14
  41.6 0.0 copy-done.15
  41.6 0.0 copy-done.16
  41.6 0.0 copy-start.1
  41.6 0.0 copy-start.13
  41.6 4.7 %finish.1 = f32[32,16,1024]{2,1,0:T(8,128)} custom-call(f32[32,16,1024]{2,1,0:T(8,128)} %get-tuple-element.17.base_ref, bf16[512,1024]{1,0:T(8,128)(2,1)} %get-tuple-element.21.ghosts_ref, f32[32,1024]{1,0:T(8,128)} %get-tuple-element.22.fix_ref, bf16[512,1024]{1,0:T(8,128)(2,1)S(1)} %copy-done.14, bf16[256,128]{1,0:T(8,128)(2,1)S(1)} %copy-done.16, ...), custom_call_target="tpu_custom_call" | custom-call | flops 2000000000 | bytes 8000000 | tf_op jit(solution)/shard_map/finish/pallas_call | solution.py:538
  46.4 23.3 %all-to-all-done.recv_ref = f32[128,16,128]{2,1,0:T(8,128)S(1)} async-done(((f32[128,16,128]{2,1,0:T(8,128)}), f32[128,16,128]{2,1,0:T(8,128)S(1)}, u32[]{:S(2)}, u32[]{:S(2)}) %all-to-all-start) | async-done | bytes 1048608 | tf_op jit(solution)/shard_map/all_to_all | solution.py:600
  69.7 0.0 copy-done.1
  69.7 0.0 copy-done.13
  69.7 3.8 %refine.1 = bf16[192,16,1024]{2,1,0:T(8,128)(2,1)} custom-call(s32[1,192]{1,0:T(1,128)S(1)} %copy-done.13, s32[1]{0:T(128)S(6)} %copy.26.count_ref, f32[128,16,128]{2,1,0:T(8,128)S(1)} %all-to-all-done.recv_ref, bf16[256,1024]{1,0:T(8,128)(2,1)S(1)} %copy-done.1), custom_call_target="tpu_custom_call" | custom-call | tf_op jit(solution)/shard_map/refine/pallas_call | solution.py:563
Async XLA Ops:
  0.6 2.4 %copy-start = (f32[32,16,1024]{2,1,0:T(8,128)S(1)}, f32[32,16,1024]{2,1,0:T(8,128)}, u32[]{:S(2)}) copy-start(f32[32,16,1024]{2,1,0:T(8,128)} %state_ref.5) | copy-start | bytes 6291460
  0.6 2.4 %copy-start.7 = (f32[16]{0:T(128)S(1)}, f32[16]{0:T(128)}, u32[]{:S(2)}) copy-start(f32[16]{0:T(128)} %ccol_ref.5) | copy-start | bytes 196
  0.7 2.4 %copy-start.6 = (f32[16]{0:T(128)S(1)}, f32[16]{0:T(128)}, u32[]{:S(2)}) copy-start(f32[16]{0:T(128)} %crow_ref.5) | copy-start | bytes 196
  0.7 2.4 %copy-start.11 = (f32[16]{0:T(128)S(1)}, f32[16]{0:T(128)}, u32[]{:S(2)}) copy-start(f32[16]{0:T(128)} %mix_ref.3) | copy-start | bytes 196
  0.7 2.4 %copy-start.10 = (s32[32,4]{0,1:T(4,128)S(1)}, s32[32,4]{0,1:T(4,128)}, u32[]{:S(2)}) copy-start(s32[32,4]{0,1:T(4,128)} %param.28) | copy-start | bytes 1540
  0.7 2.4 %copy-start.9 = (s32[32,4]{0,1:T(4,128)S(1)}, s32[32,4]{0,1:T(4,128)}, u32[]{:S(2)}) copy-start(s32[32,4]{0,1:T(4,128)} %param.27) | copy-start | bytes 1540
  0.7 2.4 %copy-start.8 = (s32[32,4]{0,1:T(4,128)S(1)}, s32[32,4]{0,1:T(4,128)}, u32[]{:S(2)}) copy-start(s32[32,4]{0,1:T(4,128)} %param.26) | copy-start | bytes 1540
  8.9 13.5 %collective-permute-start.2 = (f32[32,2,16,128]{3,2,1,0:T(8,128)S(1)}, f32[32,2,16,128]{3,2,1,0:T(8,128)S(1)}, u32[]{:S(2)}, u32[]{:S(2)}) collective-permute-start(f32[32,2,16,128]{3,2,1,0:T(8,128)S(1)} %get-tuple-element.20.own_ref), channel_id=1, source_target_pairs={{0,254},{2,4},{4,2},{6,8},{8,6},{10,12},{12,10},{14,16},{16,14},{1... | collective-permute-start | bytes 1572872 | tf_op jit(solution)/shard_map/ppermute | solution.py:596
  13.8 9.2 %collective-permute-start.1 = (f32[32,2,16,128]{3,2,1,0:T(8,128)S(1)}, f32[32,2,16,128]{3,2,1,0:T(8,128)S(1)}, u32[]{:S(2)}, u32[]{:S(2)}) collective-permute-start(f32[32,2,16,128]{3,2,1,0:T(8,128)S(1)} %get-tuple-element.20.own_ref), channel_id=1, source_target_pairs={{0,2},{2,0},{4,6},{6,4},{8,10},{10,8},{12,14},{14,12},{16,18},{18,... | collective-permute-start | bytes 1572872 | tf_op jit(solution)/shard_map/ppermute | solution.py:596
  13.8 1.3 %collective-permute-start = (f32[32,1024]{1,0:T(8,128)S(1)}, f32[32,1024]{1,0:T(8,128)S(1)}, u32[]{:S(2)}, u32[]{:S(2)}) collective-permute-start(f32[32,1024]{1,0:T(8,128)S(1)} %get-tuple-element.13), channel_id=1, source_target_pairs={{0,1},{1,0},{2,3},{3,2},{4,5},{5,4},{6,7},{7,6},{8,9},{9,8},{10,11... | collective-permute-start | bytes 393224 | tf_op jit(solution)/shard_map/ppermute | solution.py:597
  15.1 7.8 %copy-start.2 = (bf16[256,512]{1,0:T(8,128)(2,1)S(1)}, bf16[256,512]{1,0:T(8,128)(2,1)}, u32[]{:S(2)}) copy-start(bf16[256,512]{1,0:T(8,128)(2,1)} %constant.23.clone.col1_ref) | copy-start | bytes 786436
  15.1 7.8 %copy-start.3 = (bf16[256,512]{1,0:T(8,128)(2,1)S(1)}, bf16[256,512]{1,0:T(8,128)(2,1)}, u32[]{:S(2)}) copy-start(bf16[256,512]{1,0:T(8,128)(2,1)} %constant.22.clone.col0_ref) | copy-start | bytes 786436
  15.1 7.8 %copy-start.4 = (bf16[256,256]{1,0:T(8,128)(2,1)S(1)}, bf16[256,256]{1,0:T(8,128)(2,1)}, u32[]{:S(2)}) copy-start(bf16[256,256]{1,0:T(8,128)(2,1)} %constant.25.clone.row1_ref) | copy-start | bytes 393220
  15.1 7.8 %copy-start.5 = (bf16[256,256]{1,0:T(8,128)(2,1)S(1)}, bf16[256,256]{1,0:T(8,128)(2,1)}, u32[]{:S(2)}) copy-start(bf16[256,256]{1,0:T(8,128)(2,1)} %constant.24.clone.row0_ref) | copy-start | bytes 393220
  15.1 7.8 %copy-start.12 = (s32[1,128,2]{1,2,0:T(2,128)S(1)}, s32[1,128,2]{1,2,0:T(2,128)}, u32[]{:S(2)}) copy-start(s32[1,128,2]{1,2,0:T(2,128)} %param.29) | copy-start | bytes 3076
  26.7 14.9 %copy-start.14 = (bf16[512,1024]{1,0:T(8,128)(2,1)S(1)}, bf16[512,1024]{1,0:T(8,128)(2,1)}, u32[]{:S(2)}) copy-start(bf16[512,1024]{1,0:T(8,128)(2,1)} %constant.26.clone.col_ref) | copy-start | bytes 3145732
  26.7 14.9 %copy-start.15 = (bf16[256,128]{1,0:T(8,128)(2,1)S(1)}, bf16[256,128]{1,0:T(8,128)(2,1)}, u32[]{:S(2)}) copy-start(bf16[256,128]{1,0:T(8,128)(2,1)} %constant.28.clone.row1_ref) | copy-start | bytes 196612
  26.7 14.9 %copy-start.16 = (bf16[256,128]{1,0:T(8,128)(2,1)S(1)}, bf16[256,128]{1,0:T(8,128)(2,1)}, u32[]{:S(2)}) copy-start(bf16[256,128]{1,0:T(8,128)(2,1)} %constant.27.clone.row0_ref) | copy-start | bytes 196612
  26.8 42.9 %all-to-all-start = ((f32[128,16,128]{2,1,0:T(8,128)}), f32[128,16,128]{2,1,0:T(8,128)S(1)}, u32[]{:S(2)}, u32[]{:S(2)}) async-start(f32[128,16,128]{2,1,0:T(8,128)} %get-tuple-element.23), calls=%async_computation | async-start | bytes 2097152 | tf_op jit(solution)/shard_map/all_to_all | solution.py:600
  41.6 28.1 %copy-start.1 = (bf16[256,1024]{1,0:T(8,128)(2,1)S(1)}, bf16[256,1024]{1,0:T(8,128)(2,1)}, u32[]{:S(2)}) copy-start(bf16[256,1024]{1,0:T(8,128)(2,1)} %constant.29.clone.table_ref) | copy-start | bytes 1572868
  41.6 28.0 %copy-start.13 = (s32[1,192]{1,0:T(1,128)S(1)}, s32[1,192]{1,0:T(1,128)}, u32[]{:S(2)}) copy-start(s32[1,192]{1,0:T(1,128)} %slot_ref.1) | copy-start | bytes 2308

commit v8 on v7

--- a/solution.py
+++ b/solution.py
@@ -175,7 +175,7 @@
     rel = (block >> 5) - here + 1
     rel = jnp.where(rel < 0, rel + peers, rel)
     rel = jnp.where(rel >= peers, rel - peers, rel)
-    rel = jnp.where((here & 1) == 0, 2 - rel, rel)
+    rel = jnp.where((here & 1) == 0, rel, 2 - rel)
     swap = (side & 1) ^ flip
     return (block & 31) * 32 + rel * 8 + (side >> 1) * 4 + swap * 2 + flip
 
@@ -260,38 +260,38 @@
     state_ref,
     sten_ref,
     win_ref,
-    done_ref,
     base_in_ref,
     wins_ref,
     base_ref,
-    fix_ref,
+    ready_ref,
     sten,
     win,
     kept,
-    fix,
     sems,
     base_sems,
-    fix_sem,
 ):
+    ready_ref[...] = edge_ref[...]
+
+    @pl.when(lax.axis_index("slab") == 1)
+    def _():
+        load_maps(sten_ref, win_ref, sten, win, sems)
+        local_blocks(crow_ref, ccol_ref, mix_ref, state_ref, wins_ref, base_ref, sten, win, kept, base_sems)
+
+
+def edge_kernel(mix_ref, edge_ref, win_ref, first_ref, second_ref, wins_ref, fix_ref, fix, sem):
     slab = lax.axis_index("slab")
-    count, lev = state_ref.shape[0], state_ref.shape[1]
+    lev = wins_ref.shape[2]
     fix[...] = edge_ref[...] * jnp.where(slab == 0, mix_ref[lev - 1], mix_ref[0])
-    fix_copy = pltpu.make_async_copy(fix, fix_ref, fix_sem.at[0])
+    fix_copy = pltpu.make_async_copy(fix, fix_ref, sem.at[0])
     fix_copy.start()
-    load_maps(sten_ref, win_ref, sten, win, sems)
-    edge = window_tiles([fix[:, 256 * j : 256 * j + 256] for j in range(4)], win)
-
-    @pl.when(slab == 1)
-    def _():
-        local_blocks(crow_ref, ccol_ref, mix_ref, state_ref, wins_ref, base_ref, sten, win, kept, base_sems)
-        for t in range(8):
-            wins_ref[:, t, 0, :] += edge[t]
-
-    @pl.when(slab == 0)
-    def _():
-        wins_ref[...] = done_ref[...]
-        for t in range(8):
-            wins_ref[:, t, lev - 1, :] += edge[t]
+    edge = window_tiles([fix[:, 256 * j : 256 * j + 256] for j in range(4)], win_ref)
+    for which, done_ref, level in ((0, first_ref, lev - 1), (1, second_ref, 0)):
+
+        @pl.when(slab == which)
+        def _():
+            wins_ref[...] = done_ref[...]
+            for t in range(8):
+                wins_ref[:, t, level, :] += edge[t]
 
     fix_copy.wait()
 
@@ -324,9 +324,9 @@
     crow_ref,
     ccol_ref,
     base_ref,
+    far_ref,
+    own_ref,
     near_ref,
-    own_ref,
-    far_ref,
     col0_ref,
     col1_ref,
     row0_ref,
@@ -342,7 +342,7 @@
 ):
     lev = own_ref.shape[2]
     half = lax.broadcasted_iota(jnp.int32, (lev, 128), 1) // 64
-    collect_strips((near_ref, own_ref, far_ref), near)
+    collect_strips((far_ref, own_ref, near_ref), near)
     a_row = levels_of(crow_ref, lev) * (1.0 / 12.0)
     a_col = levels_of(ccol_ref, lev) * (1.0 / 12.0)
     copies = []
@@ -479,29 +479,37 @@
     )(*coefs, *tables, strips, state, *local_maps())
 
 
-def make_second(coefs, edge, state, wins, base):
+def make_second(coefs, edge, state, base):
     count, lev = state.shape[:2]
     return pl.pallas_call(
         second_kernel,
         out_shape=(
-            jax.ShapeDtypeStruct(wins.shape, jnp.float32),
+            jax.ShapeDtypeStruct((count, 8, lev, 128), jnp.float32),
             pltpu.HBM(state.shape, jnp.float32),
-            pltpu.HBM(edge.shape, jnp.float32),
+            jax.ShapeDtypeStruct(edge.shape, jnp.float32),
         ),
-        in_specs=[SMEM] * 3 + [VMEM] * 2 + [HBM] * 2 + [VMEM, HBM],
-        out_specs=(VMEM, HBM, HBM),
+        in_specs=[SMEM] * 3 + [VMEM] * 2 + [HBM] * 3,
+        out_specs=(VMEM, HBM, VMEM),
         scratch_shapes=local_scratch(state)
-        + [
-            pltpu.VMEM(edge.shape, jnp.float32),
-            pltpu.SemaphoreType.DMA((4,)),
-            pltpu.SemaphoreType.DMA((count // CHUNK,)),
-            pltpu.SemaphoreType.DMA((1,)),
-        ],
-        input_output_aliases={8: 1},
+        + [pltpu.SemaphoreType.DMA((4,)), pltpu.SemaphoreType.DMA((count // CHUNK,))],
+        input_output_aliases={7: 1},
         compiler_params=PARAMS,
         cost_estimate=cost(10**3, 10**3),
         name="second",
-    )(*coefs, edge, state, *local_maps(), wins, base)
+    )(*coefs, edge, state, *local_maps(), base)
+
+
+def add_edge(mixing, edge, first, second):
+    return pl.pallas_call(
+        edge_kernel,
+        out_shape=(jax.ShapeDtypeStruct(first.shape, jnp.float32), pltpu.HBM(edge.shape, jnp.float32)),
+        in_specs=[SMEM] + [VMEM] * 4,
+        out_specs=(VMEM, HBM),
+        scratch_shapes=[pltpu.VMEM(edge.shape, jnp.float32), pltpu.SemaphoreType.DMA((1,))],
+        compiler_params=PARAMS,
+        cost_estimate=cost(10**3, 10**3),
+        name="edge",
+    )(mixing, edge, jnp.asarray(window_map()), first, second)
 
 
 def make_payload(code, send, coefs, base, nearby):
@@ -592,10 +600,11 @@
     near = [(i, i ^ 1) for i in range(peers)]
     coefs = (courant_row, courant_col, mixing)
     strips, edge = make_strips(state)
-    wins, base, code, strips = make_first(coefs, (nbr_block.T, nbr_side.T, nbr_flip.T), strips, state)
-    nearby = (lax.ppermute(strips, "blocks", near), strips, lax.ppermute(strips, "blocks", far))
+    first, base, code, strips = make_first(coefs, (nbr_block.T, nbr_side.T, nbr_flip.T), strips, state)
+    nearby = (lax.ppermute(strips, "blocks", far), strips, lax.ppermute(strips, "blocks", near))
+    second, base, edge = make_second(coefs, edge, state, base)
     edge = lax.ppermute(edge, "slab", [(0, 1), (1, 0)])
-    wins, base, fix = make_second(coefs, edge, state, wins, base)
+    wins, fix = add_edge(mixing, edge, first, second)
     payload, ghosts = make_payload(code, send_idx[0].T, coefs, wins, nearby)
     received = lax.all_to_all(payload, "blocks", split_axis=0, concat_axis=0, tiled=True)
     advanced = make_advanced(base, ghosts, fix)

time: 73.7 us -> 70 us (0.950)
  waiting for transfers between devices: 30.2 us -> 26.8 us
    all_to_all x1, waiting for transfers between devices: 23.3 us -> 19.7 us  [body(): lax.all_to_all(payload, 'blocks', split_axis=0, concat_axis=0, tiled=True)]
    pallas_call x1 -> x2, Pallas kernels: 2.31 us -> 1.92 us  [the longest x1 1.29 us: add_edge(): pl.pallas_call(edge_kernel, out_shape=(jax.ShapeDtypeStruct(first.shape,...]
  transfers between devices with their start and end apart: 4 -> 4, of which waited for: 4 -> 4; matrix products, arithmetic and copies ran while one was open for 0% -> 0% of each run, Pallas kernels for 10% -> 9%
where the time goes in v8:
time: 70 us; the launch traced here: 69.7 us
  waiting for transfers between devices  26.8 us (38%)
  Pallas kernels  22.2 us (32%)
  starting transfers between devices  19.1 us (27%)
  between operations  1.56 us (2%)
    all_to_all x1, waiting for transfers between devices, body(): lax.all_to_all(payload, 'blocks', split_axis=0, concat_axis=0, tiled=True)  19.7 us
    all_to_all x1, starting transfers between devices, body(): lax.all_to_all(payload, 'blocks', split_axis=0, concat_axis=0, tiled=True)  14.2 us
    pallas_call x1, Pallas kernels, make_first(): pl.pallas_call(first_kernel, out_shape=(jax.ShapeDtypeStruct((count, 8, l...  5.82 us
    ppermute x1, waiting for transfers between devices, body(): lax.ppermute(strips, 'blocks', far)  5.22 us
    ppermute x1, starting transfers between devices, body(): lax.ppermute(strips, 'blocks', far)  4.84 us
    pallas_call x1, Pallas kernels, make_advanced(): pl.pallas_call(finish_kernel, grid=(count // CHUNK,), out_shape=jax.Shape...  4.66 us
    pallas_call x1, Pallas kernels, make_refined(): pl.pallas_call(functools.partial(refine_kernel, tuple(sizes)), out_shape=...  3.76 us
    pallas_call x1, Pallas kernels, make_payload(): pl.pallas_call(pack_kernel, out_shape=(pltpu.HBM((peers, lev, 128), jnp.f...  3.71 us
  transfers between devices with their start and end apart: 4, of which 4 were waited for; matrix products, arithmetic and copies ran while one was open for 0% of the time, Pallas kernels for 9%

profile of v8, /device:TPU:32, one launch (start us, length us, event | category | flops | bytes accessed | tf_op | source)
XLA Modules:
  0.0 69.7 jit_solution(10016706314825887214)
XLA Ops:
  0.6 0.0 copy-start
  0.6 0.0 copy-start.10
  0.7 0.0 copy-start.11
  0.7 0.0 copy-start.12
  0.7 0.0 copy-start.8
  0.7 0.0 copy-start.9
  0.7 0.0 copy-start.7
  0.7 2.3 %strips.1 = (f32[32,2,16,128]{3,2,1,0:T(8,128)S(1)}, f32[32,1024]{1,0:T(8,128)S(1)}) custom-call(f32[32,16,1024]{2,1,0:T(8,128)} %state_ref.5), custom_call_target="tpu_custom_call" | custom-call | tf_op jit(solution)/shard_map/strips/pallas_call | solution.py:437
  3.0 0.0 copy-done
  3.0 0.0 copy-done.10
  3.0 0.0 copy-done.11
  3.1 0.0 copy-done.12
  3.1 0.0 copy-done.8
  3.1 0.0 copy-done.9
  3.1 0.0 copy-done.7
  3.1 5.8 %first.1 = (f32[32,8,16,128]{3,2,1,0:T(8,128)S(1)}, f32[32,16,1024]{2,1,0:T(8,128)}, s32[4,32]{1,0:T(4,128)S(1)}, f32[32,2,16,128]{3,2,1,0:T(8,128)S(1)}) custom-call(f32[16]{0:T(128)S(1)} %copy-done.8, f32[16]{0:T(128)S(1)} %copy-done.9, f32[16]{0:T(128)S(1)} %copy-done.7, s32[4,32]{1,0:T(4,128)S(1)} %bitcast.6, s32[4,32]{1,0:T(4,128)S(1)} %bitcast.7, ...), custom_call_target="tpu_custom_call" | custom-call | tf_op jit(solution)/shard_map/first/pallas_call | solution.py:465
  8.9 4.8 %collective-permute-start.1 = (f32[32,2,16,128]{3,2,1,0:T(8,128)S(1)}, f32[32,2,16,128]{3,2,1,0:T(8,128)S(1)}, u32[]{:S(2)}, u32[]{:S(2)}) collective-permute-start(f32[32,2,16,128]{3,2,1,0:T(8,128)S(1)} %get-tuple-element.24.own_ref), channel_id=1, source_target_pairs={{0,254},{2,4},{4,2},{6,8},{8,6},{10,12},{12,10},{14,16},{16,14},{1... | collective-permute-start | bytes 1572872 | tf_op jit(solution)/shard_map/ppermute | solution.py:604
  13.8 0.0 collective-permute-start.2
  13.8 0.0 copy-start.1
  13.8 0.6 second.1
  14.4 0.1 collective-permute-start
  14.5 1.3 %collective-permute-done.edge_ref = f32[32,1024]{1,0:T(8,128)S(1)} collective-permute-done((f32[32,1024]{1,0:T(8,128)S(1)}, f32[32,1024]{1,0:T(8,128)S(1)}, u32[]{:S(2)}, u32[]{:S(2)}) %collective-permute-start) | collective-permute-done | bytes 131104 | tf_op jit(solution)/shard_map/ppermute | solution.py:606
  15.9 0.0 copy-done.1
  15.9 0.0 copy-start.6
  15.9 0.0 copy-start.13
  15.9 1.3 %edge.1 = (f32[32,8,16,128]{3,2,1,0:T(8,128)S(1)}, f32[32,1024]{1,0:T(8,128)}) custom-call(f32[16]{0:T(128)S(1)} %copy-done.7, f32[32,1024]{1,0:T(8,128)S(1)} %collective-permute-done.edge_ref, bf16[512,256]{1,0:T(8,128)(2,1)S(1)} %copy-done.1, f32[32,8,16,128]{3,2,1,0:T(8,128)S(1)} %get-tuple-element.21.first_ref, ...), custom_call_target="tpu_custom_call" | custom-call | flops 1000 | bytes 1000 | tf_op jit(solution)/shard_map/edge/pallas_call | solution.py:503
  17.2 5.2 %collective-permute-done.1.far_ref = f32[32,2,16,128]{3,2,1,0:T(8,128)S(1)} collective-permute-done((f32[32,2,16,128]{3,2,1,0:T(8,128)S(1)}, f32[32,2,16,128]{3,2,1,0:T(8,128)S(1)}, u32[]{:S(2)}, u32[]{:S(2)}) %collective-permute-start.1) | collective-permute-done | bytes 524320 | tf_op jit(solution)/shard_map/ppermute | solution.py:604
  22.4 0.5 collective-permute-done.2.near_ref
  23.0 0.0 copy-done.3
  23.0 0.0 copy-done.4
  23.0 0.0 copy-done.5
  23.0 0.0 copy-done.6
  23.0 0.0 copy-done.13
  23.0 3.7 %pack.1 = (f32[128,16,128]{2,1,0:T(8,128)}, bf16[512,1024]{1,0:T(8,128)(2,1)}) custom-call(s32[4,32]{1,0:T(4,128)S(1)} %get-tuple-element.19.code_ref, s32[2,128]{1,0:T(2,128)S(1)} %bitcast.9, f32[16]{0:T(128)S(1)} %copy-done.8, f32[16]{0:T(128)S(1)} %copy-done.9, f32[32,8,16,128]{3,2,1,0:T(8,128)S(1)} %get-tuple-element.23.base_ref, ...), custom_call_target="tpu_custom_call" | custom-call | flops 1000000000 | bytes 8000000 | tf_op jit(solution)/shard_map/pack/pallas_call | solution.py:520
  26.7 0.0 copy-start.15
  26.7 0.0 copy-start.16
  26.7 0.0 copy-start.17
  26.7 14.2 %all-to-all-start = ((f32[128,16,128]{2,1,0:T(8,128)}), f32[128,16,128]{2,1,0:T(8,128)S(1)}, u32[]{:S(2)}, u32[]{:S(2)}) async-start(f32[128,16,128]{2,1,0:T(8,128)} %get-tuple-element.27), calls=%async_computation | async-start | bytes 2097152 | tf_op jit(solution)/shard_map/all_to_all | solution.py:609
  41.6 0.0 copy-done.15
  41.6 0.0 copy-done.16
  41.6 0.0 copy-done.17
  41.6 0.0 copy-start.2
  41.6 0.0 copy-start.14
  41.6 4.7 %finish.1 = f32[32,16,1024]{2,1,0:T(8,128)} custom-call(f32[32,16,1024]{2,1,0:T(8,128)} %get-tuple-element.18.base_ref, bf16[512,1024]{1,0:T(8,128)(2,1)} %get-tuple-element.25.ghosts_ref, f32[32,1024]{1,0:T(8,128)} %get-tuple-element.26.fix_ref, bf16[512,1024]{1,0:T(8,128)(2,1)S(1)} %copy-done.15, bf16[256,128]{1,0:T(8,128)(2,1)S(1)} %copy-done.16, ...), custom_call_target="tpu_custom_call" | custom-call | flops 2000000000 | bytes 8000000 | tf_op jit(solution)/shard_map/finish/pallas_call | solution.py:546
  46.3 19.7 %all-to-all-done.recv_ref = f32[128,16,128]{2,1,0:T(8,128)S(1)} async-done(((f32[128,16,128]{2,1,0:T(8,128)}), f32[128,16,128]{2,1,0:T(8,128)S(1)}, u32[]{:S(2)}, u32[]{:S(2)}) %all-to-all-start) | async-done | bytes 1048608 | tf_op jit(solution)/shard_map/all_to_all | solution.py:609
  66.0 0.0 copy-done.2
  66.0 0.0 copy-done.14
  66.0 3.8 %refine.1 = bf16[192,16,1024]{2,1,0:T(8,128)(2,1)} custom-call(s32[1,192]{1,0:T(1,128)S(1)} %copy-done.14, s32[1]{0:T(128)S(6)} %copy.27.count_ref, f32[128,16,128]{2,1,0:T(8,128)S(1)} %all-to-all-done.recv_ref, bf16[256,1024]{1,0:T(8,128)(2,1)S(1)} %copy-done.2), custom_call_target="tpu_custom_call" | custom-call | tf_op jit(solution)/shard_map/refine/pallas_call | solution.py:571
  (3 shorter events, 0.0 us)
Async XLA Ops:
  0.6 2.4 %copy-start = (f32[32,16,1024]{2,1,0:T(8,128)S(1)}, f32[32,16,1024]{2,1,0:T(8,128)}, u32[]{:S(2)}) copy-start(f32[32,16,1024]{2,1,0:T(8,128)} %state_ref.5) | copy-start | bytes 6291460
  0.6 2.4 %copy-start.10 = (s32[32,4]{0,1:T(4,128)S(1)}, s32[32,4]{0,1:T(4,128)}, u32[]{:S(2)}) copy-start(s32[32,4]{0,1:T(4,128)} %param.27) | copy-start | bytes 1540
  0.7 2.4 %copy-start.11 = (s32[32,4]{0,1:T(4,128)S(1)}, s32[32,4]{0,1:T(4,128)}, u32[]{:S(2)}) copy-start(s32[32,4]{0,1:T(4,128)} %param.28) | copy-start | bytes 1540
  0.7 2.4 %copy-start.12 = (s32[32,4]{0,1:T(4,128)S(1)}, s32[32,4]{0,1:T(4,128)}, u32[]{:S(2)}) copy-start(s32[32,4]{0,1:T(4,128)} %param.29) | copy-start | bytes 1540
  0.7 2.4 %copy-start.8 = (f32[16]{0:T(128)S(1)}, f32[16]{0:T(128)}, u32[]{:S(2)}) copy-start(f32[16]{0:T(128)} %crow_ref.5) | copy-start | bytes 196
  0.7 2.4 %copy-start.9 = (f32[16]{0:T(128)S(1)}, f32[16]{0:T(128)}, u32[]{:S(2)}) copy-start(f32[16]{0:T(128)} %ccol_ref.5) | copy-start | bytes 196
  0.7 2.4 %copy-start.7 = (f32[16]{0:T(128)S(1)}, f32[16]{0:T(128)}, u32[]{:S(2)}) copy-start(f32[16]{0:T(128)} %mix_ref.5) | copy-start | bytes 196
  8.9 13.5 %collective-permute-start.1 = (f32[32,2,16,128]{3,2,1,0:T(8,128)S(1)}, f32[32,2,16,128]{3,2,1,0:T(8,128)S(1)}, u32[]{:S(2)}, u32[]{:S(2)}) collective-permute-start(f32[32,2,16,128]{3,2,1,0:T(8,128)S(1)} %get-tuple-element.24.own_ref), channel_id=1, source_target_pairs={{0,254},{2,4},{4,2},{6,8},{8,6},{10,12},{12,10},{14,16},{16,14},{1... | collective-permute-start | bytes 1572872 | tf_op jit(solution)/shard_map/ppermute | solution.py:604
  13.8 9.2 %collective-permute-start.2 = (f32[32,2,16,128]{3,2,1,0:T(8,128)S(1)}, f32[32,2,16,128]{3,2,1,0:T(8,128)S(1)}, u32[]{:S(2)}, u32[]{:S(2)}) collective-permute-start(f32[32,2,16,128]{3,2,1,0:T(8,128)S(1)} %get-tuple-element.24.own_ref), channel_id=1, source_target_pairs={{0,2},{2,0},{4,6},{6,4},{8,10},{10,8},{12,14},{14,12},{16,18},{18,... | collective-permute-start | bytes 1572872 | tf_op jit(solution)/shard_map/ppermute | solution.py:604
  13.8 2.1 %copy-start.1 = (bf16[512,256]{1,0:T(8,128)(2,1)S(1)}, bf16[512,256]{1,0:T(8,128)(2,1)}, u32[]{:S(2)}) copy-start(bf16[512,256]{1,0:T(8,128)(2,1)} %constant.21.clone.win_ref) | copy-start | bytes 786436
  14.4 1.4 %collective-permute-start = (f32[32,1024]{1,0:T(8,128)S(1)}, f32[32,1024]{1,0:T(8,128)S(1)}, u32[]{:S(2)}, u32[]{:S(2)}) collective-permute-start(f32[32,1024]{1,0:T(8,128)S(1)} %get-tuple-element.20), channel_id=1, source_target_pairs={{0,1},{1,0},{2,3},{3,2},{4,5},{5,4},{6,7},{7,6},{8,9},{9,8},{10,11... | collective-permute-start | bytes 393224 | tf_op jit(solution)/shard_map/ppermute | solution.py:606
  15.9 7.1 %copy-start.3 = (bf16[256,512]{1,0:T(8,128)(2,1)S(1)}, bf16[256,512]{1,0:T(8,128)(2,1)}, u32[]{:S(2)}) copy-start(bf16[256,512]{1,0:T(8,128)(2,1)} %constant.22.clone.col0_ref) | copy-start | bytes 786436
  15.9 7.1 %copy-start.4 = (bf16[256,512]{1,0:T(8,128)(2,1)S(1)}, bf16[256,512]{1,0:T(8,128)(2,1)}, u32[]{:S(2)}) copy-start(bf16[256,512]{1,0:T(8,128)(2,1)} %constant.23.clone.col1_ref) | copy-start | bytes 786436
  15.9 7.1 %copy-start.5 = (bf16[256,256]{1,0:T(8,128)(2,1)S(1)}, bf16[256,256]{1,0:T(8,128)(2,1)}, u32[]{:S(2)}) copy-start(bf16[256,256]{1,0:T(8,128)(2,1)} %constant.24.clone.row0_ref) | copy-start | bytes 393220
  15.9 7.1 %copy-start.6 = (bf16[256,256]{1,0:T(8,128)(2,1)S(1)}, bf16[256,256]{1,0:T(8,128)(2,1)}, u32[]{:S(2)}) copy-start(bf16[256,256]{1,0:T(8,128)(2,1)} %constant.25.clone.row1_ref) | copy-start | bytes 393220
  15.9 7.1 %copy-start.13 = (s32[1,128,2]{1,2,0:T(2,128)S(1)}, s32[1,128,2]{1,2,0:T(2,128)}, u32[]{:S(2)}) copy-start(s32[1,128,2]{1,2,0:T(2,128)} %param.30) | copy-start | bytes 3076
  26.7 14.9 %copy-start.15 = (bf16[512,1024]{1,0:T(8,128)(2,1)S(1)}, bf16[512,1024]{1,0:T(8,128)(2,1)}, u32[]{:S(2)}) copy-start(bf16[512,1024]{1,0:T(8,128)(2,1)} %constant.26.clone.col_ref) | copy-start | bytes 3145732
  26.7 14.9 %copy-start.16 = (bf16[256,128]{1,0:T(8,128)(2,1)S(1)}, bf16[256,128]{1,0:T(8,128)(2,1)}, u32[]{:S(2)}) copy-start(bf16[256,128]{1,0:T(8,128)(2,1)} %constant.27.clone.row0_ref) | copy-start | bytes 196612
  26.7 14.9 %copy-start.17 = (bf16[256,128]{1,0:T(8,128)(2,1)S(1)}, bf16[256,128]{1,0:T(8,128)(2,1)}, u32[]{:S(2)}) copy-start(bf16[256,128]{1,0:T(8,128)(2,1)} %constant.28.clone.row1_ref) | copy-start | bytes 196612
  26.7 39.2 %all-to-all-start = ((f32[128,16,128]{2,1,0:T(8,128)}), f32[128,16,128]{2,1,0:T(8,128)S(1)}, u32[]{:S(2)}, u32[]{:S(2)}) async-start(f32[128,16,128]{2,1,0:T(8,128)} %get-tuple-element.27), calls=%async_computation | async-start | bytes 2097152 | tf_op jit(solution)/shard_map/all_to_all | solution.py:609
  41.6 24.4 %copy-start.2 = (bf16[256,1024]{1,0:T(8,128)(2,1)S(1)}, bf16[256,1024]{1,0:T(8,128)(2,1)}, u32[]{:S(2)}) copy-start(bf16[256,1024]{1,0:T(8,128)(2,1)} %constant.29.clone.table_ref) | copy-start | bytes 1572868
  41.6 24.4 %copy-start.14 = (s32[1,192]{1,0:T(1,128)S(1)}, s32[1,192]{1,0:T(1,128)}, u32[]{:S(2)}) copy-start(s32[1,192]{1,0:T(1,128)} %slot_ref.1) | copy-start | bytes 2308

commit v9 on v8

--- a/solution.py
+++ b/solution.py
@@ -95,6 +95,17 @@
         for col in range(32):
             pick[row * 32 + col, (col // 8) * 64 + row * 8 + col % 8] = 1.0
     return as_bf16(np.concatenate([pick, pick], 0))
+
+
+def plane_size(peers):
+    return max(peers // 8, 1)
+
+
+def send_order(peers):
+    size = plane_size(peers)
+    planes = peers // size
+    fold = [p // 2 if p % 2 == 0 else planes - 1 - p // 2 for p in range(planes)]
+    return [plane * size + i for plane in fold for i in range(size)]
 
 
 def split(x):
@@ -364,12 +375,13 @@
                     v = v + row1[:, :, 128 * h : 128 * h + 128]
                 wins[blocks, 2 * j + h] = v
 
+    order = send_order(pay_ref.shape[0])
     size = pay_ref.shape[0] // pay_sems.shape[0]
     for i in range(pay_sems.shape[0]):
         for d in range(i * size, i * size + size):
             parts = []
             for k in range(2):
-                w = send_ref[k, d]
+                w = send_ref[k, order[d]]
                 x = wins[w >> 4, (w >> 1) & 7]
                 parts.append(jnp.where((w & 1) == k, x, pltpu.roll(x, 64, 1)))
             held_pay[d] = jnp.where(half == 0, parts[0], parts[1])
@@ -402,11 +414,17 @@
     lev = recv_ref.shape[1]
     half = lax.broadcasted_iota(jnp.int32, (lev, 128), 1) // 64
     live = count_ref[0]
+    size_in = plane_size(recv_ref.shape[0])
+    planes = recv_ref.shape[0] // size_in
+    shift = size_in.bit_length() - 1
     copies, start = [], 0
     for i, size in enumerate(sizes):
         for n in range(size):
             slot = slot_ref[0, start + n]
-            x = recv_ref[slot >> 1]
+            src = slot >> 1
+            plane = src >> shift
+            place = jnp.where(plane < (planes + 1) // 2, 2 * plane, 2 * planes - 1 - 2 * plane)
+            x = recv_ref[(place << shift) + (src & (size_in - 1))]
             x = jnp.where(half == (slot & 1), x, pltpu.roll(x, 64, 1))
             x = jnp.where(start + n < live, x, 0.0)
             high, low = split(x)
@@ -606,7 +624,9 @@
     edge = lax.ppermute(edge, "slab", [(0, 1), (1, 0)])
     wins, fix = add_edge(mixing, edge, first, second)
     payload, ghosts = make_payload(code, send_idx[0].T, coefs, wins, nearby)
-    received = lax.all_to_all(payload, "blocks", split_axis=0, concat_axis=0, tiled=True)
+    received = lax.all_to_all(
+        payload, "blocks", split_axis=0, concat_axis=0, axis_index_groups=[send_order(peers)], tiled=True
+    )
     advanced = make_advanced(base, ghosts, fix)
     return advanced, make_refined(fine_slot, fine_count, received)
 

time: 70 us -> 69.3 us (0.990)
  waiting for transfers between devices: 26.8 us -> 25.5 us
    all_to_all x1, waiting for transfers between devices: 19.7 us -> 18.4 us  [body(): lax.all_to_all(payload, 'blocks', split_axis=0, concat_axis=0, axis_index...]
  transfers between devices with their start and end apart: 4 -> 4, of which waited for: 4 -> 4; matrix products, arithmetic and copies ran while one was open for 0% -> 0% of each run, Pallas kernels for 9% -> 10%
where the time goes in v9:
time: 69.3 us; the launch traced here: 68.5 us
  waiting for transfers between devices  25.5 us (37%)
  Pallas kernels  22.2 us (32%)
  starting transfers between devices  19.2 us (28%)
  between operations  1.56 us (2%)
    all_to_all x1, waiting for transfers between devices, body(): lax.all_to_all(payload, 'blocks', split_axis=0, concat_axis=0, axis_index...  18.4 us
    all_to_all x1, starting transfers between devices, body(): lax.all_to_all(payload, 'blocks', split_axis=0, concat_axis=0, axis_index...  14.3 us
    pallas_call x1, Pallas kernels, make_first(): pl.pallas_call(first_kernel, out_shape=(jax.ShapeDtypeStruct((count, 8, l...  5.82 us
    ppermute x1, waiting for transfers between devices, body(): lax.ppermute(strips, 'blocks', far)  5.22 us
    ppermute x1, starting transfers between devices, body(): lax.ppermute(strips, 'blocks', far)  4.84 us
    pallas_call x1, Pallas kernels, make_advanced(): pl.pallas_call(finish_kernel, grid=(count // CHUNK,), out_shape=jax.Shape...  4.66 us
    pallas_call x1, Pallas kernels, make_refined(): pl.pallas_call(functools.partial(refine_kernel, tuple(sizes)), out_shape=...  3.76 us
    pallas_call x1, Pallas kernels, make_payload(): pl.pallas_call(pack_kernel, out_shape=(pltpu.HBM((peers, lev, 128), jnp.f...  3.71 us
  transfers between devices with their start and end apart: 4, of which 4 were waited for; matrix products, arithmetic and copies ran while one was open for 0% of the time, Pallas kernels for 10%

profile of v9, /device:TPU:32, one launch (start us, length us, event | category | flops | bytes accessed | tf_op | source)
XLA Modules:
  0.0 68.5 jit_solution(3708544377136188290)
XLA Ops:
  0.6 0.0 copy-start
  0.6 0.0 copy-start.10
  0.7 0.0 copy-start.11
  0.7 0.0 copy-start.12
  0.7 0.0 copy-start.8
  0.7 0.0 copy-start.9
  0.7 0.0 copy-start.7
  0.7 2.3 %strips.1 = (f32[32,2,16,128]{3,2,1,0:T(8,128)S(1)}, f32[32,1024]{1,0:T(8,128)S(1)}) custom-call(f32[32,16,1024]{2,1,0:T(8,128)} %state_ref.5), custom_call_target="tpu_custom_call" | custom-call | tf_op jit(solution)/shard_map/strips/pallas_call | solution.py:455
  3.0 0.0 copy-done
  3.0 0.0 copy-done.10
  3.0 0.0 copy-done.11
  3.1 0.0 copy-done.12
  3.1 0.0 copy-done.8
  3.1 0.0 copy-done.9
  3.1 0.0 copy-done.7
  3.1 5.8 %first.1 = (f32[32,8,16,128]{3,2,1,0:T(8,128)S(1)}, f32[32,16,1024]{2,1,0:T(8,128)}, s32[4,32]{1,0:T(4,128)S(1)}, f32[32,2,16,128]{3,2,1,0:T(8,128)S(1)}) custom-call(f32[16]{0:T(128)S(1)} %copy-done.8, f32[16]{0:T(128)S(1)} %copy-done.9, f32[16]{0:T(128)S(1)} %copy-done.7, s32[4,32]{1,0:T(4,128)S(1)} %bitcast.6, s32[4,32]{1,0:T(4,128)S(1)} %bitcast.7, ...), custom_call_target="tpu_custom_call" | custom-call | tf_op jit(solution)/shard_map/first/pallas_call | solution.py:483
  8.9 4.8 %collective-permute-start.1 = (f32[32,2,16,128]{3,2,1,0:T(8,128)S(1)}, f32[32,2,16,128]{3,2,1,0:T(8,128)S(1)}, u32[]{:S(2)}, u32[]{:S(2)}) collective-permute-start(f32[32,2,16,128]{3,2,1,0:T(8,128)S(1)} %get-tuple-element.24.own_ref), channel_id=1, source_target_pairs={{0,254},{2,4},{4,2},{6,8},{8,6},{10,12},{12,10},{14,16},{16,14},{1... | collective-permute-start | bytes 1572872 | tf_op jit(solution)/shard_map/ppermute | solution.py:622
  13.8 0.0 collective-permute-start.2
  13.8 0.6 second.1
  14.4 0.1 collective-permute-start
  14.5 1.3 %collective-permute-done.edge_ref = f32[32,1024]{1,0:T(8,128)S(1)} collective-permute-done((f32[32,1024]{1,0:T(8,128)S(1)}, f32[32,1024]{1,0:T(8,128)S(1)}, u32[]{:S(2)}, u32[]{:S(2)}) %collective-permute-start) | collective-permute-done | bytes 131104 | tf_op jit(solution)/shard_map/ppermute | solution.py:624
  15.9 0.0 copy-done.1
  15.9 0.0 copy-start.3
  15.9 0.0 copy-start.6
  15.9 0.0 copy-start.13
  15.9 1.3 %edge.1 = (f32[32,8,16,128]{3,2,1,0:T(8,128)S(1)}, f32[32,1024]{1,0:T(8,128)}) custom-call(f32[16]{0:T(128)S(1)} %copy-done.7, f32[32,1024]{1,0:T(8,128)S(1)} %collective-permute-done.edge_ref, bf16[512,256]{1,0:T(8,128)(2,1)S(1)} %copy-done.1, f32[32,8,16,128]{3,2,1,0:T(8,128)S(1)} %get-tuple-element.21.first_ref, ...), custom_call_target="tpu_custom_call" | custom-call | flops 1000 | bytes 1000 | tf_op jit(solution)/shard_map/edge/pallas_call | solution.py:521
  17.2 5.2 %collective-permute-done.1.far_ref = f32[32,2,16,128]{3,2,1,0:T(8,128)S(1)} collective-permute-done((f32[32,2,16,128]{3,2,1,0:T(8,128)S(1)}, f32[32,2,16,128]{3,2,1,0:T(8,128)S(1)}, u32[]{:S(2)}, u32[]{:S(2)}) %collective-permute-start.1) | collective-permute-done | bytes 524320 | tf_op jit(solution)/shard_map/ppermute | solution.py:622
  22.4 0.5 collective-permute-done.2.near_ref
  23.0 0.0 copy-done.3
  23.0 0.0 copy-done.4
  23.0 0.0 copy-done.5
  23.0 0.0 copy-done.6
  23.0 0.0 copy-done.13
  23.0 3.7 %pack.1 = (f32[128,16,128]{2,1,0:T(8,128)}, bf16[512,1024]{1,0:T(8,128)(2,1)}) custom-call(s32[4,32]{1,0:T(4,128)S(1)} %get-tuple-element.19.code_ref, s32[2,128]{1,0:T(2,128)S(1)} %bitcast.9, f32[16]{0:T(128)S(1)} %copy-done.8, f32[16]{0:T(128)S(1)} %copy-done.9, f32[32,8,16,128]{3,2,1,0:T(8,128)S(1)} %get-tuple-element.23.base_ref, ...), custom_call_target="tpu_custom_call" | custom-call | flops 1000000000 | bytes 8000000 | tf_op jit(solution)/shard_map/pack/pallas_call | solution.py:538
  26.7 0.0 copy-start.15
  26.7 0.0 copy-start.16
  26.7 0.0 copy-start.17
  26.7 14.3 %all-to-all-start = ((f32[128,16,128]{2,1,0:T(8,128)}), f32[128,16,128]{2,1,0:T(8,128)S(1)}, u32[]{:S(2)}, u32[]{:S(2)}) async-start(f32[128,16,128]{2,1,0:T(8,128)} %get-tuple-element.27), calls=%async_computation | async-start | bytes 2097152 | tf_op jit(solution)/shard_map/all_to_all | solution.py:627
  41.7 0.0 copy-done.15
  41.7 0.0 copy-done.16
  41.7 0.0 copy-done.17
  41.7 0.0 copy-start.2
  41.7 0.0 copy-start.14
  41.7 4.7 %finish.1 = f32[32,16,1024]{2,1,0:T(8,128)} custom-call(f32[32,16,1024]{2,1,0:T(8,128)} %get-tuple-element.18.base_ref, bf16[512,1024]{1,0:T(8,128)(2,1)} %get-tuple-element.25.ghosts_ref, f32[32,1024]{1,0:T(8,128)} %get-tuple-element.26.fix_ref, bf16[512,1024]{1,0:T(8,128)(2,1)S(1)} %copy-done.15, bf16[256,128]{1,0:T(8,128)(2,1)S(1)} %copy-done.16, ...), custom_call_target="tpu_custom_call" | custom-call | flops 2000000000 | bytes 8000000 | tf_op jit(solution)/shard_map/finish/pallas_call | solution.py:564
  46.4 18.4 %all-to-all-done.recv_ref = f32[128,16,128]{2,1,0:T(8,128)S(1)} async-done(((f32[128,16,128]{2,1,0:T(8,128)}), f32[128,16,128]{2,1,0:T(8,128)S(1)}, u32[]{:S(2)}, u32[]{:S(2)}) %all-to-all-start) | async-done | bytes 1048608 | tf_op jit(solution)/shard_map/all_to_all | solution.py:627
  64.7 0.0 copy-done.2
  64.7 0.0 copy-done.14
  64.7 3.8 %refine.1 = bf16[192,16,1024]{2,1,0:T(8,128)(2,1)} custom-call(s32[1,192]{1,0:T(1,128)S(1)} %copy-done.14, s32[1]{0:T(128)S(6)} %copy.27.count_ref, f32[128,16,128]{2,1,0:T(8,128)S(1)} %all-to-all-done.recv_ref, bf16[256,1024]{1,0:T(8,128)(2,1)S(1)} %copy-done.2), custom_call_target="tpu_custom_call" | custom-call | tf_op jit(solution)/shard_map/refine/pallas_call | solution.py:589
  (3 shorter events, 0.0 us)
Async XLA Ops:
  0.6 2.4 %copy-start = (f32[32,16,1024]{2,1,0:T(8,128)S(1)}, f32[32,16,1024]{2,1,0:T(8,128)}, u32[]{:S(2)}) copy-start(f32[32,16,1024]{2,1,0:T(8,128)} %state_ref.5) | copy-start | bytes 6291460
  0.6 2.4 %copy-start.10 = (s32[32,4]{0,1:T(4,128)S(1)}, s32[32,4]{0,1:T(4,128)}, u32[]{:S(2)}) copy-start(s32[32,4]{0,1:T(4,128)} %param.27) | copy-start | bytes 1540
  0.7 2.4 %copy-start.11 = (s32[32,4]{0,1:T(4,128)S(1)}, s32[32,4]{0,1:T(4,128)}, u32[]{:S(2)}) copy-start(s32[32,4]{0,1:T(4,128)} %param.28) | copy-start | bytes 1540
  0.7 2.4 %copy-start.12 = (s32[32,4]{0,1:T(4,128)S(1)}, s32[32,4]{0,1:T(4,128)}, u32[]{:S(2)}) copy-start(s32[32,4]{0,1:T(4,128)} %param.29) | copy-start | bytes 1540
  0.7 2.4 %copy-start.8 = (f32[16]{0:T(128)S(1)}, f32[16]{0:T(128)}, u32[]{:S(2)}) copy-start(f32[16]{0:T(128)} %crow_ref.5) | copy-start | bytes 196
  0.7 2.4 %copy-start.9 = (f32[16]{0:T(128)S(1)}, f32[16]{0:T(128)}, u32[]{:S(2)}) copy-start(f32[16]{0:T(128)} %ccol_ref.5) | copy-start | bytes 196
  0.7 2.4 %copy-start.7 = (f32[16]{0:T(128)S(1)}, f32[16]{0:T(128)}, u32[]{:S(2)}) copy-start(f32[16]{0:T(128)} %mix_ref.5) | copy-start | bytes 196
  8.9 13.5 %collective-permute-start.1 = (f32[32,2,16,128]{3,2,1,0:T(8,128)S(1)}, f32[32,2,16,128]{3,2,1,0:T(8,128)S(1)}, u32[]{:S(2)}, u32[]{:S(2)}) collective-permute-start(f32[32,2,16,128]{3,2,1,0:T(8,128)S(1)} %get-tuple-element.24.own_ref), channel_id=1, source_target_pairs={{0,254},{2,4},{4,2},{6,8},{8,6},{10,12},{12,10},{14,16},{16,14},{1... | collective-permute-start | bytes 1572872 | tf_op jit(solution)/shard_map/ppermute | solution.py:622
  13.8 9.2 %collective-permute-start.2 = (f32[32,2,16,128]{3,2,1,0:T(8,128)S(1)}, f32[32,2,16,128]{3,2,1,0:T(8,128)S(1)}, u32[]{:S(2)}, u32[]{:S(2)}) collective-permute-start(f32[32,2,16,128]{3,2,1,0:T(8,128)S(1)} %get-tuple-element.24.own_ref), channel_id=1, source_target_pairs={{0,2},{2,0},{4,6},{6,4},{8,10},{10,8},{12,14},{14,12},{16,18},{18,... | collective-permute-start | bytes 1572872 | tf_op jit(solution)/shard_map/ppermute | solution.py:622
  13.8 2.1 %copy-start.1 = (bf16[512,256]{1,0:T(8,128)(2,1)S(1)}, bf16[512,256]{1,0:T(8,128)(2,1)}, u32[]{:S(2)}) copy-start(bf16[512,256]{1,0:T(8,128)(2,1)} %constant.21.clone.win_ref) | copy-start | bytes 786436
  14.4 1.4 %collective-permute-start = (f32[32,1024]{1,0:T(8,128)S(1)}, f32[32,1024]{1,0:T(8,128)S(1)}, u32[]{:S(2)}, u32[]{:S(2)}) collective-permute-start(f32[32,1024]{1,0:T(8,128)S(1)} %get-tuple-element.20), channel_id=1, source_target_pairs={{0,1},{1,0},{2,3},{3,2},{4,5},{5,4},{6,7},{7,6},{8,9},{9,8},{10,11... | collective-permute-start | bytes 393224 | tf_op jit(solution)/shard_map/ppermute | solution.py:624
  15.9 7.1 %copy-start.3 = (bf16[256,512]{1,0:T(8,128)(2,1)S(1)}, bf16[256,512]{1,0:T(8,128)(2,1)}, u32[]{:S(2)}) copy-start(bf16[256,512]{1,0:T(8,128)(2,1)} %constant.22.clone.col0_ref) | copy-start | bytes 786436
  15.9 7.1 %copy-start.4 = (bf16[256,512]{1,0:T(8,128)(2,1)S(1)}, bf16[256,512]{1,0:T(8,128)(2,1)}, u32[]{:S(2)}) copy-start(bf16[256,512]{1,0:T(8,128)(2,1)} %constant.23.clone.col1_ref) | copy-start | bytes 786436
  15.9 7.1 %copy-start.5 = (bf16[256,256]{1,0:T(8,128)(2,1)S(1)}, bf16[256,256]{1,0:T(8,128)(2,1)}, u32[]{:S(2)}) copy-start(bf16[256,256]{1,0:T(8,128)(2,1)} %constant.24.clone.row0_ref) | copy-start | bytes 393220
  15.9 7.1 %copy-start.6 = (bf16[256,256]{1,0:T(8,128)(2,1)S(1)}, bf16[256,256]{1,0:T(8,128)(2,1)}, u32[]{:S(2)}) copy-start(bf16[256,256]{1,0:T(8,128)(2,1)} %constant.25.clone.row1_ref) | copy-start | bytes 393220
  15.9 7.1 %copy-start.13 = (s32[1,128,2]{1,2,0:T(2,128)S(1)}, s32[1,128,2]{1,2,0:T(2,128)}, u32[]{:S(2)}) copy-start(s32[1,128,2]{1,2,0:T(2,128)} %param.30) | copy-start | bytes 3076
  26.7 15.0 %copy-start.15 = (bf16[512,1024]{1,0:T(8,128)(2,1)S(1)}, bf16[512,1024]{1,0:T(8,128)(2,1)}, u32[]{:S(2)}) copy-start(bf16[512,1024]{1,0:T(8,128)(2,1)} %constant.26.clone.col_ref) | copy-start | bytes 3145732
  26.7 15.0 %copy-start.16 = (bf16[256,128]{1,0:T(8,128)(2,1)S(1)}, bf16[256,128]{1,0:T(8,128)(2,1)}, u32[]{:S(2)}) copy-start(bf16[256,128]{1,0:T(8,128)(2,1)} %constant.27.clone.row0_ref) | copy-start | bytes 196612
  26.7 15.0 %copy-start.17 = (bf16[256,128]{1,0:T(8,128)(2,1)S(1)}, bf16[256,128]{1,0:T(8,128)(2,1)}, u32[]{:S(2)}) copy-start(bf16[256,128]{1,0:T(8,128)(2,1)} %constant.28.clone.row1_ref) | copy-start | bytes 196612
  26.7 38.0 %all-to-all-start = ((f32[128,16,128]{2,1,0:T(8,128)}), f32[128,16,128]{2,1,0:T(8,128)S(1)}, u32[]{:S(2)}, u32[]{:S(2)}) async-start(f32[128,16,128]{2,1,0:T(8,128)} %get-tuple-element.27), calls=%async_computation | async-start | bytes 2097152 | tf_op jit(solution)/shard_map/all_to_all | solution.py:627
  41.7 23.0 %copy-start.2 = (bf16[256,1024]{1,0:T(8,128)(2,1)S(1)}, bf16[256,1024]{1,0:T(8,128)(2,1)}, u32[]{:S(2)}) copy-start(bf16[256,1024]{1,0:T(8,128)(2,1)} %constant.29.clone.table_ref) | copy-start | bytes 1572868
  41.7 23.0 %copy-start.14 = (s32[1,192]{1,0:T(1,128)S(1)}, s32[1,192]{1,0:T(1,128)}, u32[]{:S(2)}) copy-start(s32[1,192]{1,0:T(1,128)} %slot_ref.1) | copy-start | bytes 2308

commit v10 on v9

--- a/solution.py
+++ b/solution.py
@@ -307,20 +307,17 @@
     fix_copy.wait()
 
 
-def collect_strips(near_refs, near):
-    for i, ref in enumerate(near_refs):
-        near[i] = ref[...]
-
-
 def gather_ghosts(i, code_ref, a_row, a_col, near, ghosts_ref):
-    lev = near.shape[3]
+    lev = near[0].shape[2]
     half = lax.broadcasted_iota(jnp.int32, (lev, 128), 1) // 64
     rows = CHUNK * lev
     for s in range(4):
         parts = []
         for n in range(CHUNK):
             code = code_ref[s, i * CHUNK + n]
-            x = near[(code >> 3) & 3, code >> 5, (code >> 2) & 1]
+            owner = (code >> 3) & 3
+            x, middle, last = (ref[code >> 5, (code >> 2) & 1] for ref in near)
+            x = jnp.where(owner == 0, x, jnp.where(owner == 1, middle, last))
             x = jnp.where((code & 2) == 0, x, pltpu.roll(x, 64, 1))
             parts.append(jnp.where(half == (code & 1), x, 0.0))
         x = jnp.stack(parts) * (a_row if s < 2 else a_col)
@@ -344,7 +341,6 @@
     row1_ref,
     pay_ref,
     ghosts_ref,
-    near,
     wins,
     held_pay,
     pay_sems,
@@ -353,7 +349,7 @@
 ):
     lev = own_ref.shape[2]
     half = lax.broadcasted_iota(jnp.int32, (lev, 128), 1) // 64
-    collect_strips((far_ref, own_ref, near_ref), near)
+    near = (far_ref, own_ref, near_ref)
     a_row = levels_of(crow_ref, lev) * (1.0 / 12.0)
     a_col = levels_of(ccol_ref, lev) * (1.0 / 12.0)
     copies = []
@@ -544,7 +540,6 @@
         in_specs=[SMEM] * 4 + [VMEM] * 8,
         out_specs=(HBM, HBM),
         scratch_shapes=[
-            pltpu.VMEM((3, count, 2, lev, 128), jnp.float32),
             pltpu.VMEM((count, 8, lev, 128), jnp.float32),
             pltpu.VMEM((peers, lev, 128), jnp.float32),
             pltpu.SemaphoreType.DMA((4,)),

time: 69.3 us -> 69.5 us (level)
  no operation moved by 1% of the time
where the time goes in v10:
time: 69.5 us; the launch traced here: 68.7 us
  waiting for transfers between devices  25.4 us (37%)
  Pallas kernels  22.4 us (32%)
  starting transfers between devices  19.2 us (28%)
  between operations  1.56 us (2%)
    all_to_all x1, waiting for transfers between devices, body(): lax.all_to_all(payload, 'blocks', split_axis=0, concat_axis=0, axis_index...  18.3 us
    all_to_all x1, starting transfers between devices, body(): lax.all_to_all(payload, 'blocks', split_axis=0, concat_axis=0, axis_index...  14.3 us
    pallas_call x1, Pallas kernels, make_first(): pl.pallas_call(first_kernel, out_shape=(jax.ShapeDtypeStruct((count, 8, l...  5.82 us
    ppermute x1, waiting for transfers between devices, body(): lax.ppermute(strips, 'blocks', far)  5.22 us
    ppermute x1, starting transfers between devices, body(): lax.ppermute(strips, 'blocks', far)  4.84 us
    pallas_call x1, Pallas kernels, make_advanced(): pl.pallas_call(finish_kernel, grid=(count // CHUNK,), out_shape=jax.Shape...  4.67 us
    pallas_call x1, Pallas kernels, make_payload(): pl.pallas_call(pack_kernel, out_shape=(pltpu.HBM((peers, lev, 128), jnp.f...  3.89 us
    pallas_call x1, Pallas kernels, make_refined(): pl.pallas_call(functools.partial(refine_kernel, tuple(sizes)), out_shape=...  3.76 us
  transfers between devices with their start and end apart: 4, of which 4 were waited for; matrix products, arithmetic and copies ran while one was open for 0% of the time, Pallas kernels for 10%

profile of v10, /device:TPU:32, one launch (start us, length us, event | category | flops | bytes accessed | tf_op | source)
XLA Modules:
  0.0 68.7 jit_solution(5144326568572734103)
XLA Ops:
  0.6 0.0 copy-start
  0.6 0.0 copy-start.10
  0.7 0.0 copy-start.11
  0.7 0.0 copy-start.12
  0.7 0.0 copy-start.8
  0.7 0.0 copy-start.9
  0.7 0.0 copy-start.7
  0.7 2.3 %strips.1 = (f32[32,2,16,128]{3,2,1,0:T(8,128)S(1)}, f32[32,1024]{1,0:T(8,128)S(1)}) custom-call(f32[32,16,1024]{2,1,0:T(8,128)} %state_ref.5), custom_call_target="tpu_custom_call" | custom-call | tf_op jit(solution)/shard_map/strips/pallas_call | solution.py:451
  3.0 0.0 copy-done
  3.0 0.0 copy-done.10
  3.0 0.0 copy-done.11
  3.1 0.0 copy-done.12
  3.1 0.0 copy-done.8
  3.1 0.0 copy-done.9
  3.1 0.0 copy-done.7
  3.1 5.8 %first.1 = (f32[32,8,16,128]{3,2,1,0:T(8,128)S(1)}, f32[32,16,1024]{2,1,0:T(8,128)}, s32[4,32]{1,0:T(4,128)S(1)}, f32[32,2,16,128]{3,2,1,0:T(8,128)S(1)}) custom-call(f32[16]{0:T(128)S(1)} %copy-done.8, f32[16]{0:T(128)S(1)} %copy-done.9, f32[16]{0:T(128)S(1)} %copy-done.7, s32[4,32]{1,0:T(4,128)S(1)} %bitcast.6, s32[4,32]{1,0:T(4,128)S(1)} %bitcast.7, ...), custom_call_target="tpu_custom_call" | custom-call | tf_op jit(solution)/shard_map/first/pallas_call | solution.py:479
  8.9 4.8 %collective-permute-start.1 = (f32[32,2,16,128]{3,2,1,0:T(8,128)S(1)}, f32[32,2,16,128]{3,2,1,0:T(8,128)S(1)}, u32[]{:S(2)}, u32[]{:S(2)}) collective-permute-start(f32[32,2,16,128]{3,2,1,0:T(8,128)S(1)} %get-tuple-element.24.own_ref), channel_id=1, source_target_pairs={{0,254},{2,4},{4,2},{6,8},{8,6},{10,12},{12,10},{14,16},{16,14},{1... | collective-permute-start | bytes 1572872 | tf_op jit(solution)/shard_map/ppermute | solution.py:617
  13.8 0.0 collective-permute-start.2
  13.8 0.0 copy-start.1
  13.8 0.6 second.1
  14.4 0.1 collective-permute-start
  14.5 1.3 %collective-permute-done.edge_ref = f32[32,1024]{1,0:T(8,128)S(1)} collective-permute-done((f32[32,1024]{1,0:T(8,128)S(1)}, f32[32,1024]{1,0:T(8,128)S(1)}, u32[]{:S(2)}, u32[]{:S(2)}) %collective-permute-start) | collective-permute-done | bytes 131104 | tf_op jit(solution)/shard_map/ppermute | solution.py:619
  15.9 0.0 copy-done.1
  15.9 0.0 copy-start.6
  15.9 0.0 copy-start.13
  15.9 1.3 %edge.1 = (f32[32,8,16,128]{3,2,1,0:T(8,128)S(1)}, f32[32,1024]{1,0:T(8,128)}) custom-call(f32[16]{0:T(128)S(1)} %copy-done.7, f32[32,1024]{1,0:T(8,128)S(1)} %collective-permute-done.edge_ref, bf16[512,256]{1,0:T(8,128)(2,1)S(1)} %copy-done.1, f32[32,8,16,128]{3,2,1,0:T(8,128)S(1)} %get-tuple-element.21.first_ref, ...), custom_call_target="tpu_custom_call" | custom-call | flops 1000 | bytes 1000 | tf_op jit(solution)/shard_map/edge/pallas_call | solution.py:517
  17.2 5.2 %collective-permute-done.1.far_ref = f32[32,2,16,128]{3,2,1,0:T(8,128)S(1)} collective-permute-done((f32[32,2,16,128]{3,2,1,0:T(8,128)S(1)}, f32[32,2,16,128]{3,2,1,0:T(8,128)S(1)}, u32[]{:S(2)}, u32[]{:S(2)}) %collective-permute-start.1) | collective-permute-done | bytes 524320 | tf_op jit(solution)/shard_map/ppermute | solution.py:617
  22.4 0.5 collective-permute-done.2.near_ref
  23.0 0.0 copy-done.3
  23.0 0.0 copy-done.4
  23.0 0.0 copy-done.5
  23.0 0.0 copy-done.6
  23.0 0.0 copy-done.13
  23.0 3.9 %pack.1 = (f32[128,16,128]{2,1,0:T(8,128)}, bf16[512,1024]{1,0:T(8,128)(2,1)}) custom-call(s32[4,32]{1,0:T(4,128)S(1)} %get-tuple-element.19.code_ref, s32[2,128]{1,0:T(2,128)S(1)} %bitcast.9, f32[16]{0:T(128)S(1)} %copy-done.8, f32[16]{0:T(128)S(1)} %copy-done.9, f32[32,8,16,128]{3,2,1,0:T(8,128)S(1)} %get-tuple-element.23.base_ref, ...), custom_call_target="tpu_custom_call" | custom-call | flops 1000000000 | bytes 8000000 | tf_op jit(solution)/shard_map/pack/pallas_call | solution.py:534
  26.9 0.0 copy-start.15
  26.9 0.0 copy-start.16
  26.9 0.0 copy-start.17
  26.9 14.3 %all-to-all-start = ((f32[128,16,128]{2,1,0:T(8,128)}), f32[128,16,128]{2,1,0:T(8,128)S(1)}, u32[]{:S(2)}, u32[]{:S(2)}) async-start(f32[128,16,128]{2,1,0:T(8,128)} %get-tuple-element.27), calls=%async_computation | async-start | bytes 2097152 | tf_op jit(solution)/shard_map/all_to_all | solution.py:622
  41.8 0.0 copy-done.15
  41.9 0.0 copy-done.16
  41.9 0.0 copy-done.17
  41.9 0.0 copy-start.2
  41.9 0.0 copy-start.14
  41.9 4.7 %finish.1 = f32[32,16,1024]{2,1,0:T(8,128)} custom-call(f32[32,16,1024]{2,1,0:T(8,128)} %get-tuple-element.18.base_ref, bf16[512,1024]{1,0:T(8,128)(2,1)} %get-tuple-element.25.ghosts_ref, f32[32,1024]{1,0:T(8,128)} %get-tuple-element.26.fix_ref, bf16[512,1024]{1,0:T(8,128)(2,1)S(1)} %copy-done.15, bf16[256,128]{1,0:T(8,128)(2,1)S(1)} %copy-done.16, ...), custom_call_target="tpu_custom_call" | custom-call | flops 2000000000 | bytes 8000000 | tf_op jit(solution)/shard_map/finish/pallas_call | solution.py:559
  46.6 18.3 %all-to-all-done.recv_ref = f32[128,16,128]{2,1,0:T(8,128)S(1)} async-done(((f32[128,16,128]{2,1,0:T(8,128)}), f32[128,16,128]{2,1,0:T(8,128)S(1)}, u32[]{:S(2)}, u32[]{:S(2)}) %all-to-all-start) | async-done | bytes 1048608 | tf_op jit(solution)/shard_map/all_to_all | solution.py:622
  64.9 0.0 copy-done.2
  64.9 0.0 copy-done.14
  64.9 3.8 %refine.1 = bf16[192,16,1024]{2,1,0:T(8,128)(2,1)} custom-call(s32[1,192]{1,0:T(1,128)S(1)} %copy-done.14, s32[1]{0:T(128)S(6)} %copy.27.count_ref, f32[128,16,128]{2,1,0:T(8,128)S(1)} %all-to-all-done.recv_ref, bf16[256,1024]{1,0:T(8,128)(2,1)S(1)} %copy-done.2), custom_call_target="tpu_custom_call" | custom-call | tf_op jit(solution)/shard_map/refine/pallas_call | solution.py:584
  (3 shorter events, 0.0 us)
Async XLA Ops:
  0.6 2.4 %copy-start = (f32[32,16,1024]{2,1,0:T(8,128)S(1)}, f32[32,16,1024]{2,1,0:T(8,128)}, u32[]{:S(2)}) copy-start(f32[32,16,1024]{2,1,0:T(8,128)} %state_ref.5) | copy-start | bytes 6291460
  0.6 2.4 %copy-start.10 = (s32[32,4]{0,1:T(4,128)S(1)}, s32[32,4]{0,1:T(4,128)}, u32[]{:S(2)}) copy-start(s32[32,4]{0,1:T(4,128)} %param.27) | copy-start | bytes 1540
  0.7 2.4 %copy-start.11 = (s32[32,4]{0,1:T(4,128)S(1)}, s32[32,4]{0,1:T(4,128)}, u32[]{:S(2)}) copy-start(s32[32,4]{0,1:T(4,128)} %param.28) | copy-start | bytes 1540
  0.7 2.4 %copy-start.12 = (s32[32,4]{0,1:T(4,128)S(1)}, s32[32,4]{0,1:T(4,128)}, u32[]{:S(2)}) copy-start(s32[32,4]{0,1:T(4,128)} %param.29) | copy-start | bytes 1540
  0.7 2.4 %copy-start.8 = (f32[16]{0:T(128)S(1)}, f32[16]{0:T(128)}, u32[]{:S(2)}) copy-start(f32[16]{0:T(128)} %crow_ref.5) | copy-start | bytes 196
  0.7 2.4 %copy-start.9 = (f32[16]{0:T(128)S(1)}, f32[16]{0:T(128)}, u32[]{:S(2)}) copy-start(f32[16]{0:T(128)} %ccol_ref.5) | copy-start | bytes 196
  0.7 2.4 %copy-start.7 = (f32[16]{0:T(128)S(1)}, f32[16]{0:T(128)}, u32[]{:S(2)}) copy-start(f32[16]{0:T(128)} %mix_ref.5) | copy-start | bytes 196
  8.9 13.5 %collective-permute-start.1 = (f32[32,2,16,128]{3,2,1,0:T(8,128)S(1)}, f32[32,2,16,128]{3,2,1,0:T(8,128)S(1)}, u32[]{:S(2)}, u32[]{:S(2)}) collective-permute-start(f32[32,2,16,128]{3,2,1,0:T(8,128)S(1)} %get-tuple-element.24.own_ref), channel_id=1, source_target_pairs={{0,254},{2,4},{4,2},{6,8},{8,6},{10,12},{12,10},{14,16},{16,14},{1... | collective-permute-start | bytes 1572872 | tf_op jit(solution)/shard_map/ppermute | solution.py:617
  13.8 9.2 %collective-permute-start.2 = (f32[32,2,16,128]{3,2,1,0:T(8,128)S(1)}, f32[32,2,16,128]{3,2,1,0:T(8,128)S(1)}, u32[]{:S(2)}, u32[]{:S(2)}) collective-permute-start(f32[32,2,16,128]{3,2,1,0:T(8,128)S(1)} %get-tuple-element.24.own_ref), channel_id=1, source_target_pairs={{0,2},{2,0},{4,6},{6,4},{8,10},{10,8},{12,14},{14,12},{16,18},{18,... | collective-permute-start | bytes 1572872 | tf_op jit(solution)/shard_map/ppermute | solution.py:617
  13.8 2.1 %copy-start.1 = (bf16[512,256]{1,0:T(8,128)(2,1)S(1)}, bf16[512,256]{1,0:T(8,128)(2,1)}, u32[]{:S(2)}) copy-start(bf16[512,256]{1,0:T(8,128)(2,1)} %constant.21.clone.win_ref) | copy-start | bytes 786436
  14.4 1.4 %collective-permute-start = (f32[32,1024]{1,0:T(8,128)S(1)}, f32[32,1024]{1,0:T(8,128)S(1)}, u32[]{:S(2)}, u32[]{:S(2)}) collective-permute-start(f32[32,1024]{1,0:T(8,128)S(1)} %get-tuple-element.20), channel_id=1, source_target_pairs={{0,1},{1,0},{2,3},{3,2},{4,5},{5,4},{6,7},{7,6},{8,9},{9,8},{10,11... | collective-permute-start | bytes 393224 | tf_op jit(solution)/shard_map/ppermute | solution.py:619
  15.9 7.1 %copy-start.3 = (bf16[256,512]{1,0:T(8,128)(2,1)S(1)}, bf16[256,512]{1,0:T(8,128)(2,1)}, u32[]{:S(2)}) copy-start(bf16[256,512]{1,0:T(8,128)(2,1)} %constant.22.clone.col0_ref) | copy-start | bytes 786436
  15.9 7.1 %copy-start.4 = (bf16[256,512]{1,0:T(8,128)(2,1)S(1)}, bf16[256,512]{1,0:T(8,128)(2,1)}, u32[]{:S(2)}) copy-start(bf16[256,512]{1,0:T(8,128)(2,1)} %constant.23.clone.col1_ref) | copy-start | bytes 786436
  15.9 7.1 %copy-start.5 = (bf16[256,256]{1,0:T(8,128)(2,1)S(1)}, bf16[256,256]{1,0:T(8,128)(2,1)}, u32[]{:S(2)}) copy-start(bf16[256,256]{1,0:T(8,128)(2,1)} %constant.24.clone.row0_ref) | copy-start | bytes 393220
  15.9 7.1 %copy-start.6 = (bf16[256,256]{1,0:T(8,128)(2,1)S(1)}, bf16[256,256]{1,0:T(8,128)(2,1)}, u32[]{:S(2)}) copy-start(bf16[256,256]{1,0:T(8,128)(2,1)} %constant.25.clone.row1_ref) | copy-start | bytes 393220
  15.9 7.1 %copy-start.13 = (s32[1,128,2]{1,2,0:T(2,128)S(1)}, s32[1,128,2]{1,2,0:T(2,128)}, u32[]{:S(2)}) copy-start(s32[1,128,2]{1,2,0:T(2,128)} %param.30) | copy-start | bytes 3076
  26.9 15.0 %copy-start.15 = (bf16[512,1024]{1,0:T(8,128)(2,1)S(1)}, bf16[512,1024]{1,0:T(8,128)(2,1)}, u32[]{:S(2)}) copy-start(bf16[512,1024]{1,0:T(8,128)(2,1)} %constant.26.clone.col_ref) | copy-start | bytes 3145732
  26.9 15.0 %copy-start.16 = (bf16[256,128]{1,0:T(8,128)(2,1)S(1)}, bf16[256,128]{1,0:T(8,128)(2,1)}, u32[]{:S(2)}) copy-start(bf16[256,128]{1,0:T(8,128)(2,1)} %constant.27.clone.row0_ref) | copy-start | bytes 196612
  26.9 15.0 %copy-start.17 = (bf16[256,128]{1,0:T(8,128)(2,1)S(1)}, bf16[256,128]{1,0:T(8,128)(2,1)}, u32[]{:S(2)}) copy-start(bf16[256,128]{1,0:T(8,128)(2,1)} %constant.28.clone.row1_ref) | copy-start | bytes 196612
  26.9 38.0 %all-to-all-start = ((f32[128,16,128]{2,1,0:T(8,128)}), f32[128,16,128]{2,1,0:T(8,128)S(1)}, u32[]{:S(2)}, u32[]{:S(2)}) async-start(f32[128,16,128]{2,1,0:T(8,128)} %get-tuple-element.27), calls=%async_computation | async-start | bytes 2097152 | tf_op jit(solution)/shard_map/all_to_all | solution.py:622
  41.9 23.0 %copy-start.2 = (bf16[256,1024]{1,0:T(8,128)(2,1)S(1)}, bf16[256,1024]{1,0:T(8,128)(2,1)}, u32[]{:S(2)}) copy-start(bf16[256,1024]{1,0:T(8,128)(2,1)} %constant.29.clone.table_ref) | copy-start | bytes 1572868
  41.9 23.0 %copy-start.14 = (s32[1,192]{1,0:T(1,128)S(1)}, s32[1,192]{1,0:T(1,128)}, u32[]{:S(2)}) copy-start(s32[1,192]{1,0:T(1,128)} %slot_ref.1) | copy-start | bytes 2308
